TPU v7x, 32 devices: a whole 2x2x4 slice. The times are simulated.
32 devices in a mesh: seq: 8 (over z, x), head: 4 (over y, core).
Axes of the slice: x: 2, y: 2, z: 4, core: 2. Of those that a mesh axis runs over, the one named last changes fastest.
Arguments:
- tokens: bfloat16 [4096, 4096], P('seq'), may hold values from -6 to 6
- w_xz: bfloat16 [4096, 2, 4096], P('seq', None, 'head'), may hold values from -0.09375 to 0.09375
- w_bc: bfloat16 [4096, 256], P('seq'), may hold values from -0.09375 to 0.09375
- conv_x: float32 [4, 4096], P(None, 'head'), may hold values from -3 to 3
- conv_bc: float32 [4, 256], replicated, may hold values from -3 to 3
- tail_x: bfloat16 [3, 4096], P(None, 'head'), may hold values from -6 to 6
- tail_bc: bfloat16 [3, 256], replicated, may hold values from -6 to 6
- decay_code: int32 [4096, 64], P('seq', 'head'), may hold values from 0 to 49152, as said below
- skip_gain: float32 [64], P('head'), may hold values from 0.5 to 2
- state_in: float32 [64, 64, 128], P('head'), may hold values from -180 to 180
- norm_gain: float32 [4096], P('head'), may hold values from 0.1 to 1.9
- w_out: bfloat16 [4096, 4096], P('head', 'seq'), may hold values from -0.125 to 0.125
Outputs:
- mixed: bfloat16 [4096, 4096], P('seq', 'head')
Inputs may be any that keep to these rules, and one draw needn't show every extreme that they name: `decay_code`: the decay factor of a token and head is exp(-code / 65536).
All inputs are finite; a program needn't handle non-finite values.
Results may differ from a plain program's by a relative error of at most 0.0085.
Values may be sent and summed in bfloat16 or wider, within the bound.
No kernel may reach another device: no remote copies, remote signals or barrier semaphores. Data moves between devices by JAX's collectives and lax.ppermute only.
A program may use at most 128 MiB of HBM per device.

v0:
```python
import jax
import jax.numpy as jnp
from jax import lax
from jax.sharding import PartitionSpec as P

Q = 256


def passed_along(value, axis, by):
    size = lax.axis_size(axis)
    pairs = [(i, i + by) for i in range(size) if 0 <= i + by < size]
    return lax.ppermute(value, axis, pairs)


def depthwise(pre, tail, kernel):
    whole = jnp.concatenate([tail, pre], axis=0).astype(jnp.float32)
    length = pre.shape[0]
    total = jnp.zeros((length, pre.shape[1]), jnp.float32)
    for offset in range(kernel.shape[0]):
        total = total + kernel[offset] * whole[offset : offset + length]
    return jax.nn.silu(total).astype(jnp.bfloat16)


def block_step(state, inputs):
    xval, bval, cval, logdec = inputs
    cum = jnp.cumsum(logdec, axis=0)
    span = cum.shape[0]
    places = jnp.arange(span)
    lower = places[:, None] >= places[None, :]
    cumt = cum.T
    diff = cumt[:, :, None] - cumt[:, None, :]
    decay = jnp.where(lower[None], jnp.exp(jnp.where(lower[None], diff, 0.0)), 0.0)
    scores = jnp.dot(cval, bval.T, preferred_element_type=jnp.float32)
    weights = (decay * scores[None]).astype(jnp.bfloat16)
    inner = jnp.einsum("hts,shp->thp", weights, xval, preferred_element_type=jnp.float32)
    carried = jnp.einsum(
        "tn,hpn->thp", cval.astype(jnp.float32), state, precision=lax.Precision.HIGHEST
    )
    carried = carried * jnp.exp(cum)[:, :, None]
    tail_decay = jnp.exp(cum[-1][None, :] - cum)
    decayed_b = (tail_decay.T[:, :, None] * bval.astype(jnp.float32)[None]).astype(jnp.bfloat16)
    added = jnp.einsum("hsn,shp->hpn", decayed_b, xval, preferred_element_type=jnp.float32)
    new_state = jnp.exp(cum[-1])[:, None, None] * state + added
    return (new_state, inner + carried)


def local(
    tokens,
    w_xz,
    w_bc,
    conv_x,
    conv_bc,
    tail_x,
    tail_bc,
    decay_code,
    skip_gain,
    state_in,
    norm_gain,
    w_out,
):
    rows = tokens.shape[0]
    heads, head_dim, nstate = state_in.shape
    inner = heads * head_dim
    seq_count = lax.axis_size("seq")
    first = lax.axis_index("seq") == 0
    pieces = (
        lax.all_gather(w_xz, "seq", axis=0, tiled=True),
        lax.all_gather(w_bc, "seq", axis=0, tiled=True),
    )
    count = pieces[0].shape[0]
    xz = jnp.dot(tokens, pieces[0].reshape(count, 2 * inner), preferred_element_type=jnp.float32)
    bc_sum = jnp.dot(tokens, pieces[1], preferred_element_type=jnp.float32)
    x_pre = xz[:, :inner].astype(jnp.bfloat16)
    z_val = xz[:, inner:].astype(jnp.bfloat16)
    bc_pre = bc_sum.astype(jnp.bfloat16)
    lag = conv_x.shape[0] - 1
    before_x, before_bc = passed_along((x_pre[rows - lag :], bc_pre[rows - lag :]), "seq", 1)
    before_x = jnp.where(first, tail_x, before_x)
    before_bc = jnp.where(first, tail_bc, before_bc)
    x_conv = depthwise(x_pre, before_x, conv_x)
    bc_conv = depthwise(bc_pre, before_bc, conv_bc)
    b_val = bc_conv[:, :nstate]
    c_val = bc_conv[:, nstate:]
    logdec = -decay_code.astype(jnp.float32) / (16.0 * rows * seq_count)
    blocks = rows // Q
    inputs = (
        x_conv.reshape(blocks, Q, heads, head_dim),
        b_val.reshape(blocks, Q, nstate),
        c_val.reshape(blocks, Q, nstate),
        logdec.reshape(blocks, Q, heads),
    )
    local_state, parts = lax.scan(block_step, jnp.zeros_like(state_in), inputs)
    parts = parts.reshape(rows, heads, head_dim)
    cum_range = jnp.cumsum(logdec, axis=0)
    range_decay = jnp.exp(cum_range[-1])

    def link(step, incoming):
        outgoing = range_decay[:, None, None] * incoming + local_state
        received = passed_along(outgoing, "seq", 1)
        return jnp.where(first, state_in, received)

    opening = jnp.where(first, state_in, jnp.zeros_like(state_in))
    incoming = lax.fori_loop(0, seq_count - 1, link, opening)
    correction = jnp.einsum(
        "tn,hpn->thp", c_val.astype(jnp.float32), incoming, precision=lax.Precision.HIGHEST
    )
    parts = (parts + correction * jnp.exp(cum_range)[:, :, None]).reshape(rows, inner)
    y_val = parts / nstate + jnp.repeat(skip_gain, head_dim)[None, :] * x_conv.astype(jnp.float32)
    gated = y_val * jax.nn.silu(z_val.astype(jnp.float32))
    total_sq = lax.psum(jnp.sum(gated * gated, axis=1), "head")
    meansq = total_sq / (inner * lax.axis_size("head"))
    normed = (gated * lax.rsqrt(meansq[:, None] + 1e-05) * norm_gain[None, :]).astype(jnp.bfloat16)
    partial_out = jnp.dot(
        normed, lax.all_gather(w_out, "seq", axis=1, tiled=True), preferred_element_type=jnp.float32
    )
    result = lax.psum_scatter(partial_out, "head", scatter_dimension=1, tiled=True)
    return result.astype(jnp.bfloat16)


def solution(mesh):
    return jax.shard_map(
        local,
        mesh=mesh,
        in_specs=(
            P("seq", None),
            P("seq", None, "head"),
            P("seq", None),
            P(None, "head"),
            P(),
            P(None, "head"),
            P(),
            P("seq", "head"),
            P("head"),
            P("head", None, None),
            P("head"),
            P("head", "seq"),
        ),
        out_specs=P("seq", "head"),
        check_vma=False,
    )
```

profile of v0, /device:TPU:0, one launch (start us, length us, event | category | flops | bytes accessed | tf_op | source)
XLA Modules:
  0.0 648.3 jit_solution(13489106142598580153)
XLA Ops:
  11.9 49.6 %all-gather.6.cloned.1.call-done = bf16[4096,256]{1,0:T(8,128)(2,1)} async-done(((bf16[512,256]{1,0:T(8,128)(2,1)}), bf16[4096,256]{1,0:T(8,128)(2,1)}) %all-gather.6.cloned.1.call-update) | async-done | bytes 2097168 | tf_op jit(solution)/shard_map/all_gather | solution.py:68
  69.8 220.0 %all-gather.4.cloned.1.call-done = bf16[4096,2,1024]{2,1,0:T(2,128)(2,1)} async-done(((bf16[512,2,1024]{2,1,0:T(2,128)(2,1)}), bf16[4096,2,1024]{2,1,0:T(2,128)(2,1)}) %all-gather.4.cloned.1.call-update) | async-done | bytes 16777232 | tf_op jit(solution)/shard_map/all_gather | solution.py:67
  289.8 12.2 %copy.61 = bf16[512,8,2,1024]{3,1,2,0:T(8,128)(2,1)S(1)} copy(bf16[512,8,2,1024]{3,2,1,0:T(2,128)(2,1)} %bitcast.121) | data formatting | bytes 33554432
  302.0 9.1 %convolution_convert_fusion = bf16[512,2048]{1,0:T(8,128)(2,1)S(1)} fusion(bf16[512,4096]{1,0:T(8,128)(2,1)S(1)} %copy-done.14, bf16[4096,2048]{1,0:T(8,128)(2,1)S(1)} %bitcast.122), kind=kOutput, calls=%fused_computation.49 | convolution fusion | flops 8590983168 | bytes 23068672 | tf_op jit(solution)/shard_map/dot_general | solution.py:71
  322.5 61.7 %while.24 = (s32[]{:T(128)}, f32[16,64,128]{2,1,0:T(8,128)}, f32[2,256,16,64]{1,0,3,2:T(2,128)}, f32[2,256,16]{1,0,2:T(2,128)S(1)}, bf16[2,256,16,64]{1,3,2,0:T(...) while((s32[]{:T(128)}, f32[16,64,128]{2,1,0:T(8,128)}, ...), condition=%wide.region_3.4_spmd.clone, body=%wide.region_0.3_spmd.clone.sunk | while | flops 628731968 | bytes 11423432 | solution.py:92
  327.9 21.9 %dynamic_update_slice.6 = f32[2,256,16,64]{1,0,3,2:T(2,128)} dynamic-update-slice(f32[2,256,16,64]{1,0,3,2:T(2,128)} %get-tuple-element.268, f32[1,256,16,64]{1,0,3,2:T(1,128)S(1)} %copy.88, s32[]{:T(128)} %get-tuple-element.266, s32[]{:T(128)} %constant.46.clone.1..sunk, s32[]{:T(128)} %constant.46.clone.1..sunk, s32[]{:T(128)} %constant.46.clone.1..sunk) | dynamic-update-slice | bytes 2097156 | tf_op jit(solution)/shard_map/while/body/jit(dynamic_update_index_in_dim)/dynamic_update_slice | solution.py:92
  359.2 21.9 %dynamic_update_slice.6 = f32[2,256,16,64]{1,0,3,2:T(2,128)} dynamic-update-slice(f32[2,256,16,64]{1,0,3,2:T(2,128)} %get-tuple-element.268, f32[1,256,16,64]{1,0,3,2:T(1,128)S(1)} %copy.88, s32[]{:T(128)} %get-tuple-element.266, s32[]{:T(128)} %constant.46.clone.1..sunk, s32[]{:T(128)} %constant.46.clone.1..sunk, s32[]{:T(128)} %constant.46.clone.1..sunk) | dynamic-update-slice | bytes 2097156 | tf_op jit(solution)/shard_map/while/body/jit(dynamic_update_index_in_dim)/dynamic_update_slice | solution.py:92
  388.3 141.9 %while.23 = (s32[]{:T(128)}, f32[16,64,128]{2,1,0:T(8,128)S(1)}, pred[]{:T(512)}, f32[16]{0:T(128)S(1)}, f32[16,64,128]{2,1,0:T(8,128)}, /*index=5*/f32[16,64,128]{2,1,0:T(8,128)S(1)}, s32[]{:T(128)}) while((s32[]{:T(128)}, f32[16,64,128]{2,1,0:T(8,128)S(1)}, pred[]{:T(512)}, f32[16]{0:T(128)S(1)}, f32[16,64,128]{2,1,0:T(8,128)}, ...), condition=%wide.region_7.8_spmd, body=%wide.region_6.7_spmd.sunk | while | flops 393218 | bytes 7340242 | solution.py:103
  394.5 10.2 %collective-permute-done = f32[16,64,128]{2,1,0:T(8,128)S(1)} collective-permute-done((f32[16,64,128]{2,1,0:T(8,128)}, f32[16,64,128]{2,1,0:T(8,128)S(1)}, u32[]{:S(2)}, u32[]{:S(2)}) %collective-permute-start) | collective-permute-done | bytes 524320 | tf_op jit(solution)/shard_map/while/body/eval_jaxpr/ppermute | solution.py:12
  407.5 17.0 %collective-permute-start = (f32[16,64,128]{2,1,0:T(8,128)}, f32[16,64,128]{2,1,0:T(8,128)S(1)}, u32[]{:S(2)}, u32[]{:S(2)}) collective-permute-start(f32[16,64,128]{2,1,0:T(8,128)} %multiply_add_fusion.2), channel_id=1, source_target_pairs={{0,4},{4,8},{8,12},{12,16},{16,20},{20,24},{24,28},{1,5},{5,9},{9,... | collective-permute-start | bytes 1572872 | tf_op jit(solution)/shard_map/while/body/eval_jaxpr/ppermute | solution.py:12
  424.6 9.0 %collective-permute-done = f32[16,64,128]{2,1,0:T(8,128)S(1)} collective-permute-done((f32[16,64,128]{2,1,0:T(8,128)}, f32[16,64,128]{2,1,0:T(8,128)S(1)}, u32[]{:S(2)}, u32[]{:S(2)}) %collective-permute-start) | collective-permute-done | bytes 524320 | tf_op jit(solution)/shard_map/while/body/eval_jaxpr/ppermute | solution.py:12
  436.4 6.4 collective-permute-start
  442.7 8.2 %collective-permute-done = f32[16,64,128]{2,1,0:T(8,128)S(1)} collective-permute-done((f32[16,64,128]{2,1,0:T(8,128)}, f32[16,64,128]{2,1,0:T(8,128)S(1)}, u32[]{:S(2)}, u32[]{:S(2)}) %collective-permute-start) | collective-permute-done | bytes 524320 | tf_op jit(solution)/shard_map/while/body/eval_jaxpr/ppermute | solution.py:12
  453.8 14.6 %collective-permute-start = (f32[16,64,128]{2,1,0:T(8,128)}, f32[16,64,128]{2,1,0:T(8,128)S(1)}, u32[]{:S(2)}, u32[]{:S(2)}) collective-permute-start(f32[16,64,128]{2,1,0:T(8,128)} %multiply_add_fusion.2), channel_id=1, source_target_pairs={{0,4},{4,8},{8,12},{12,16},{16,20},{20,24},{24,28},{1,5},{5,9},{9,... | collective-permute-start | bytes 1572872 | tf_op jit(solution)/shard_map/while/body/eval_jaxpr/ppermute | solution.py:12
  468.3 9.8 %collective-permute-done = f32[16,64,128]{2,1,0:T(8,128)S(1)} collective-permute-done((f32[16,64,128]{2,1,0:T(8,128)}, f32[16,64,128]{2,1,0:T(8,128)S(1)}, u32[]{:S(2)}, u32[]{:S(2)}) %collective-permute-start) | collective-permute-done | bytes 524320 | tf_op jit(solution)/shard_map/while/body/eval_jaxpr/ppermute | solution.py:12
  481.0 6.2 collective-permute-start
  487.2 8.9 %collective-permute-done = f32[16,64,128]{2,1,0:T(8,128)S(1)} collective-permute-done((f32[16,64,128]{2,1,0:T(8,128)}, f32[16,64,128]{2,1,0:T(8,128)S(1)}, u32[]{:S(2)}, u32[]{:S(2)}) %collective-permute-start) | collective-permute-done | bytes 524320 | tf_op jit(solution)/shard_map/while/body/eval_jaxpr/ppermute | solution.py:12
  498.9 6.2 collective-permute-start
  505.2 8.0 %collective-permute-done = f32[16,64,128]{2,1,0:T(8,128)S(1)} collective-permute-done((f32[16,64,128]{2,1,0:T(8,128)}, f32[16,64,128]{2,1,0:T(8,128)S(1)}, u32[]{:S(2)}, u32[]{:S(2)}) %collective-permute-start) | collective-permute-done | bytes 524320 | tf_op jit(solution)/shard_map/while/body/eval_jaxpr/ppermute | solution.py:12
  516.0 6.2 collective-permute-start
  522.2 7.1 %collective-permute-done = f32[16,64,128]{2,1,0:T(8,128)S(1)} collective-permute-done((f32[16,64,128]{2,1,0:T(8,128)}, f32[16,64,128]{2,1,0:T(8,128)S(1)}, u32[]{:S(2)}, u32[]{:S(2)}) %collective-permute-start) | collective-permute-done | bytes 524320 | tf_op jit(solution)/shard_map/while/body/eval_jaxpr/ppermute | solution.py:12
  541.9 5.9 psum.7
  547.7 11.8 %fusion.39 = f32[512,4096]{1,0:T(8,128)} fusion(bf16[1024,4096]{1,0:T(8,128)(2,1)} %all-gather.8.cloned.1.call-done, f32[512,1024]{1,0:T(8,128)} %get-tuple-element.157, f32[1024]{0:T(1024)S(1)} %copy-done.15, f32[512]{0:T(512)S(1)} %add_rsqrt_fusion), kind=kOutput, calls=%fused_computation.69 | convolution fusion | flops 4296540160 | bytes 18880512 | tf_op jit(solution)/shard_map/dot_general | solution.py:113
  559.6 79.4 %reduce-scatter.2.cloned.1.call-done = f32[512,1024]{1,0:T(8,128)} async-done(((f32[512,4096]{1,0:T(8,128)}), f32[512,1024]{1,0:T(8,128)}) %reduce-scatter.2.cloned.1.call-update) | async-done | bytes 2097168 | tf_op jit(solution)/shard_map/reduce_scatter | solution.py:116
  (144 shorter events, 84.9 us)
Async XLA Ops:
  6.5 4.5 copy-start.9
  6.5 4.5 copy-start.11
  6.5 4.5 copy-start.1
  6.5 55.0 %all-gather.6.cloned.1.call-start = ((), (), s32[]{:S(2)}) async-start(), calls=%async_computation.2 | async-start | bytes 2359296 | tf_op jit(solution)/shard_map/all_gather | solution.py:68
  7.3 282.5 %all-gather.4.cloned.1.call-start = ((), (), s32[]{:S(2)}) async-start(), calls=%async_computation.1 | async-start | bytes 18874368 | tf_op jit(solution)/shard_map/all_gather | solution.py:67
  8.0 539.7 %all-gather.8.cloned.1.call-start = ((), (), s32[]{:S(2)}) async-start(), calls=%async_computation.3 | async-start | bytes 9437184 | tf_op jit(solution)/shard_map/all_gather | solution.py:114
  8.8 630.3 %reduce-scatter.2.cloned.1.call-start = ((), (), s32[]{:S(2)}) async-start(), calls=%async_computation.4 | async-start | bytes 10485760 | tf_op jit(solution)/shard_map/reduce_scatter | solution.py:116
  11.9 56.4 %copy-start.13 = (f32[16]{0:T(128)S(1)}, f32[16]{0:T(128)}, u32[]{:S(2)}) copy-start(f32[16]{0:T(128)} %param.24) | copy-start | bytes 196
  11.9 57.5 %copy-start.12 = (bf16[3,256]{1,0:T(4,128)(2,1)S(1)}, bf16[3,256]{1,0:T(4,128)(2,1)}, u32[]{:S(2)}) copy-start(bf16[3,256]{1,0:T(4,128)(2,1)} %param.22) | copy-start | bytes 4612
  65.6 3.8 collective-permute-start.2
  69.8 244.1 %copy-start.5 = (bf16[512,256]{1,0:T(8,128)(2,1)}, bf16[512,256]{1,0:T(8,128)(2,1)S(1)}, u32[]{:S(2)}) copy-start(bf16[512,256]{1,0:T(8,128)(2,1)S(1)} %multiply_convert_fusion.9) | copy-start | bytes 786436
  289.8 12.2 %copy-start.14 = (bf16[512,4096]{1,0:T(8,128)(2,1)S(1)}, bf16[512,4096]{1,0:T(8,128)(2,1)}, u32[]{:S(2)}) copy-start(bf16[512,4096]{1,0:T(8,128)(2,1)} %param.16) | copy-start | bytes 12582916
  311.1 3.9 collective-permute-start.1
  384.2 4.0 copy-start.2
  388.2 141.9 %copy-start.6 = (bf16[512,256]{1,0:T(8,128)(2,1)S(1)}, bf16[512,256]{1,0:T(8,128)(2,1)}, u32[]{:S(2)}) copy-start(bf16[512,256]{1,0:T(8,128)(2,1)} %copy-done.5) | copy-start | bytes 786436
  388.2 141.9 %copy-start.7 = (f32[512,16]{0,1:T(8,128)S(1)}, f32[512,16]{0,1:T(8,128)}, u32[]{:S(2)}) copy-start(f32[512,16]{0,1:T(8,128)} %fusion.47) | copy-start | bytes 98308
  390.3 14.5 %collective-permute-start = (f32[16,64,128]{2,1,0:T(8,128)}, f32[16,64,128]{2,1,0:T(8,128)S(1)}, u32[]{:S(2)}, u32[]{:S(2)}) collective-permute-start(f32[16,64,128]{2,1,0:T(8,128)} %multiply_add_fusion.2), channel_id=1, source_target_pairs={{0,4},{4,8},{8,12},{12,16},{16,20},{20,24},{24,28},{1,5},{5,9},{9,... | collective-permute-start | bytes 1572872 | tf_op jit(solution)/shard_map/while/body/eval_jaxpr/ppermute | solution.py:12
  407.5 26.0 %collective-permute-start = (f32[16,64,128]{2,1,0:T(8,128)}, f32[16,64,128]{2,1,0:T(8,128)S(1)}, u32[]{:S(2)}, u32[]{:S(2)}) collective-permute-start(f32[16,64,128]{2,1,0:T(8,128)} %multiply_add_fusion.2), channel_id=1, source_target_pairs={{0,4},{4,8},{8,12},{12,16},{16,20},{20,24},{24,28},{1,5},{5,9},{9,... | collective-permute-start | bytes 1572872 | tf_op jit(solution)/shard_map/while/body/eval_jaxpr/ppermute | solution.py:12
  436.4 14.6 %collective-permute-start = (f32[16,64,128]{2,1,0:T(8,128)}, f32[16,64,128]{2,1,0:T(8,128)S(1)}, u32[]{:S(2)}, u32[]{:S(2)}) collective-permute-start(f32[16,64,128]{2,1,0:T(8,128)} %multiply_add_fusion.2), channel_id=1, source_target_pairs={{0,4},{4,8},{8,12},{12,16},{16,20},{20,24},{24,28},{1,5},{5,9},{9,... | collective-permute-start | bytes 1572872 | tf_op jit(solution)/shard_map/while/body/eval_jaxpr/ppermute | solution.py:12
  453.8 24.4 %collective-permute-start = (f32[16,64,128]{2,1,0:T(8,128)}, f32[16,64,128]{2,1,0:T(8,128)S(1)}, u32[]{:S(2)}, u32[]{:S(2)}) collective-permute-start(f32[16,64,128]{2,1,0:T(8,128)} %multiply_add_fusion.2), channel_id=1, source_target_pairs={{0,4},{4,8},{8,12},{12,16},{16,20},{20,24},{24,28},{1,5},{5,9},{9,... | collective-permute-start | bytes 1572872 | tf_op jit(solution)/shard_map/while/body/eval_jaxpr/ppermute | solution.py:12
  481.0 15.1 %collective-permute-start = (f32[16,64,128]{2,1,0:T(8,128)}, f32[16,64,128]{2,1,0:T(8,128)S(1)}, u32[]{:S(2)}, u32[]{:S(2)}) collective-permute-start(f32[16,64,128]{2,1,0:T(8,128)} %multiply_add_fusion.2), channel_id=1, source_target_pairs={{0,4},{4,8},{8,12},{12,16},{16,20},{20,24},{24,28},{1,5},{5,9},{9,... | collective-permute-start | bytes 1572872 | tf_op jit(solution)/shard_map/while/body/eval_jaxpr/ppermute | solution.py:12
  498.9 14.2 %collective-permute-start = (f32[16,64,128]{2,1,0:T(8,128)}, f32[16,64,128]{2,1,0:T(8,128)S(1)}, u32[]{:S(2)}, u32[]{:S(2)}) collective-permute-start(f32[16,64,128]{2,1,0:T(8,128)} %multiply_add_fusion.2), channel_id=1, source_target_pairs={{0,4},{4,8},{8,12},{12,16},{16,20},{20,24},{24,28},{1,5},{5,9},{9,... | collective-permute-start | bytes 1572872 | tf_op jit(solution)/shard_map/while/body/eval_jaxpr/ppermute | solution.py:12
  516.0 13.3 %collective-permute-start = (f32[16,64,128]{2,1,0:T(8,128)}, f32[16,64,128]{2,1,0:T(8,128)S(1)}, u32[]{:S(2)}, u32[]{:S(2)}) collective-permute-start(f32[16,64,128]{2,1,0:T(8,128)} %multiply_add_fusion.2), channel_id=1, source_target_pairs={{0,4},{4,8},{8,12},{12,16},{16,20},{20,24},{24,28},{1,5},{5,9},{9,... | collective-permute-start | bytes 1572872 | tf_op jit(solution)/shard_map/while/body/eval_jaxpr/ppermute | solution.py:12
  537.1 10.7 %copy-start.15 = (f32[1024]{0:T(1024)S(1)}, f32[1024]{0:T(1024)}, u32[]{:S(2)}) copy-start(f32[1024]{0:T(1024)} %param.26) | copy-start | bytes 12292
  (11 other events, 19.7 us)
Sparse Core Ops, SparseCore 0:
  9.5 51.9 all-gather.5
  63.6 226.1 all-gather.3
  291.9 125.1 all-gather.7
  559.7 79.2 reduce-scatter.1
where the time goes:
time: 653 us; the launch traced here: 648 us
  waiting for transfers between devices  414 us (63%)
  local copies, waits for them, and re-layouts  78 us (12%)
  starting transfers between devices  66.2 us (10%)
  matrix products  42 us (6%)
  other arithmetic  28.3 us (4%)
  between operations  13.4 us (2%)
    all_gather x1, waiting for transfers between devices, local(): lax.all_gather(w_xz, 'seq', axis=0, tiled=True)  220 us
    reduce_scatter x1, waiting for transfers between devices, local(): lax.psum_scatter(partial_out, 'head', scatter_dimension=1, tiled=True)  79.4 us
    ppermute x9, starting transfers between devices, passed_along(): return lax.ppermute(value, axis, pairs)  66.1 us
    ppermute x9, waiting for transfers between devices, passed_along(): return lax.ppermute(value, axis, pairs)  63.1 us
    all_gather x1, waiting for transfers between devices, local(): lax.all_gather(w_bc, 'seq', axis=0, tiled=True)  49.6 us
    dynamic_update_slice x4, local copies, waits for them, and re-layouts, local(): local_state, parts = lax.scan(block_step, jnp.zeros_like(state_in), inputs)  46 us
    unnamed x32, local copies, waits for them, and re-layouts  15.8 us
    add x7, other arithmetic, link(): outgoing = range_decay[:, None, None] * incoming + local_state  13.7 us
  transfers between devices with their start and end apart: 13, of which 12 were waited for; matrix products, arithmetic and copies ran while one was open for 20% of the time, Pallas kernels for 0%

commit v1 on v0

v1 whole, which is shorter than its diff:
```python
import functools

import jax
import jax.numpy as jnp
from jax import lax
from jax.experimental import pallas as pl
from jax.experimental.pallas import tpu as pltpu
from jax.sharding import PartitionSpec as P

Q = 256
HALO = 16
PAIR = 2
F32 = jnp.float32
BF16 = jnp.bfloat16
VMEM_LIMIT = 48 * 1024 * 1024


def swapped(value, axis, bit):
    size = lax.axis_size(axis)
    return lax.ppermute(value, axis, [(i, i ^ bit) for i in range(size)])


def shifted(value, axis, by):
    size = lax.axis_size(axis)
    return lax.ppermute(value, axis, [(i, i + by) for i in range(size - by)])


def cut(value, index, size, axis):
    return lax.dynamic_slice_in_dim(value, index * size, size, axis)


def spread(own, other, seq_count):
    pieces = {0: own, PAIR: swapped(other, "seq", PAIR)}
    bits = [1 << b for b in range(seq_count.bit_length() - 1)]
    for bit in [b for b in bits if b > PAIR] + [b for b in bits if b < PAIR]:
        for mask in list(pieces):
            pieces[mask | bit] = swapped(pieces[mask], "seq", bit)
    return pieces


def dot(a, b):
    return jnp.dot(a, b, preferred_element_type=F32)


def front_kernel(first_ref, x_ref, bc_ref, tx_ref, tbc_ref, kx_ref, kbc_ref, dec_ref, xc_ref, bcc_ref, f_ref):
    is_first = first_ref[pl.program_id(0)] == 1
    rows = xc_ref.shape[1]

    def conv(pre_ref, tail_ref, k_ref):
        pre = pre_ref[0].astype(F32)
        halo = jnp.where(is_first, tail_ref[...].astype(F32), pre[:HALO])
        whole = jnp.concatenate([halo, pre[HALO:]], axis=0)
        taps = k_ref.shape[0]
        total = jnp.zeros((rows, pre.shape[1]), F32)
        for k in range(taps):
            start = HALO - (taps - 1) + k
            total = total + k_ref[k : k + 1, :] * whole[start : start + rows]
        return (total * jax.nn.sigmoid(total)).astype(BF16)

    x_val = conv(x_ref, tx_ref, kx_ref)
    bc_val = conv(bc_ref, tbc_ref, kbc_ref)
    xc_ref[0] = x_val
    bcc_ref[0] = bc_val
    decayed = (x_val.astype(F32) * dec_ref[0]).astype(BF16)
    nstate = bc_val.shape[1] // 2
    for start in range(0, rows, Q):
        f_ref[0, start // Q] = lax.dot_general(
            bc_val[start : start + Q, :nstate],
            decayed[start : start + Q],
            (((0,), (0,)), ((), ())),
            preferred_element_type=F32,
        )


def intra_kernel(heads, x_ref, bc_ref, cum_ref, cumt_ref, y_ref):
    nstate = bc_ref.shape[2] // 2
    span = x_ref.shape[1]
    head_dim = x_ref.shape[2] // heads
    b_val = bc_ref[0, :, :nstate]
    c_val = bc_ref[0, :, nstate:]
    scores = lax.dot_general(c_val, b_val, (((1,), (1,)), ((), ())), preferred_element_type=F32)
    lower = lax.broadcasted_iota(jnp.int32, (span, span), 0) >= lax.broadcasted_iota(jnp.int32, (span, span), 1)
    scores = jnp.where(lower, scores, 0.0)
    pair = 128 // head_dim
    for start in range(0, heads, pair):
        outs = []
        for h in range(start, start + pair):
            diff = cum_ref[0, :, h : h + 1] - cumt_ref[0, 0, h : h + 1, :]
            weights = (jnp.exp(jnp.where(lower, diff, 0.0)) * scores).astype(BF16)
            outs.append(dot(weights, x_ref[0, :, h * head_dim : (h + 1) * head_dim]))
        y_ref[0, :, start * head_dim : (start + pair) * head_dim] = jnp.concatenate(outs, axis=1)


def gate_kernel(y_ref, x_ref, bc_ref, st_ref, e_ref, skip_ref, z_ref, gain_ref, g_ref, ss_ref):
    nstate = st_ref.shape[2]
    c_val = bc_ref[0, :, nstate:]
    state = st_ref[0, 0]
    high = state.astype(BF16)
    low = (state - high.astype(F32)).astype(BF16)
    carried = dot(c_val, high) + dot(c_val, low)
    y_val = (y_ref[0] + e_ref[0] * carried) / nstate + skip_ref[...] * x_ref[0].astype(F32)
    z_val = z_ref[0].astype(F32)
    gated = y_val * (z_val * jax.nn.sigmoid(z_val))
    g_ref[0] = (gated * gain_ref[...]).astype(BF16)
    total = jnp.sum(gated * gated, axis=1, keepdims=True)
    ss_ref[0] = jnp.broadcast_to(total, ss_ref.shape[1:])


def params(grid):
    return pltpu.CompilerParams(dimension_semantics=("arbitrary",) * grid, vmem_limit_bytes=VMEM_LIMIT)


def whole_block(shape):
    return pl.BlockSpec(shape, lambda *_: (0,) * len(shape))


def front(first, x_pre, bc_pre, tail_x, tail_bc, conv_x, conv_bc, decay):
    _, ext, chans = x_pre.shape
    rows = ext - HALO
    bcw = bc_pre.shape[2]

    def ranged(n, w):
        return pl.BlockSpec((1, n, w), lambda r: (r, 0, 0))

    return pl.pallas_call(
        front_kernel,
        grid=(2,),
        in_specs=[
            pl.BlockSpec(memory_space=pltpu.SMEM),
            ranged(ext, chans),
            ranged(ext, bcw),
            whole_block(tail_x.shape),
            whole_block(tail_bc.shape),
            whole_block(conv_x.shape),
            whole_block(conv_bc.shape),
            ranged(rows, chans),
        ],
        out_specs=[
            ranged(rows, chans),
            ranged(rows, bcw),
            pl.BlockSpec((1, rows // Q, bcw // 2, chans), lambda r: (r, 0, 0, 0)),
        ],
        out_shape=[
            jax.ShapeDtypeStruct((2, rows, chans), BF16),
            jax.ShapeDtypeStruct((2, rows, bcw), BF16),
            jax.ShapeDtypeStruct((2, rows // Q, bcw // 2, chans), F32),
        ],
        compiler_params=params(1),
        name="front",
    )(first, x_pre, bc_pre, tail_x, tail_bc, conv_x, conv_bc, decay)


def intra(x_conv, bc_conv, cum, cumt, heads):
    _, rows, chans = x_conv.shape
    bcw = bc_conv.shape[2]
    blocks = rows // Q

    def tile(w):
        return pl.BlockSpec((1, Q, w), lambda r, i: (r, i, 0))

    work = 2 * rows * Q
    return pl.pallas_call(
        functools.partial(intra_kernel, heads),
        grid=(2, blocks),
        in_specs=[tile(chans), tile(bcw), tile(heads), pl.BlockSpec((1, 1, heads, Q), lambda r, i: (r, i, 0, 0))],
        out_specs=tile(chans),
        out_shape=jax.ShapeDtypeStruct((2, rows, chans), F32),
        compiler_params=params(2),
        cost_estimate=pl.CostEstimate(
            flops=2 * work * (chans + bcw // 2), bytes_accessed=12 * rows * chans, transcendentals=work * heads
        ),
        name="intra",
    )(x_conv, bc_conv, cum, cumt)


def gate(y_in, x_conv, bc_conv, state, grown, skip, z_val, gain):
    _, rows, chans = x_conv.shape
    bcw = bc_conv.shape[2]

    def tile(w):
        return pl.BlockSpec((1, Q, w), lambda r, i: (r, i, 0))

    return pl.pallas_call(
        gate_kernel,
        grid=(2, rows // Q),
        in_specs=[
            tile(chans),
            tile(chans),
            tile(bcw),
            pl.BlockSpec((1, 1, bcw // 2, chans), lambda r, i: (r, i, 0, 0)),
            tile(chans),
            whole_block((1, chans)),
            tile(chans),
            whole_block((1, chans)),
        ],
        out_specs=[tile(chans), tile(128)],
        out_shape=[
            jax.ShapeDtypeStruct((2, rows, chans), BF16),
            jax.ShapeDtypeStruct((2, rows, 128), F32),
        ],
        compiler_params=params(2),
        name="gate",
    )(y_in, x_conv, bc_conv, state, grown, skip, z_val, gain)


def local(
    tokens,
    w_xz,
    w_bc,
    conv_x,
    conv_bc,
    tail_x,
    tail_bc,
    decay_code,
    skip_gain,
    state_in,
    norm_gain,
    w_out,
):
    rows = tokens.shape[0]
    all_heads, head_dim, nstate = state_in.shape
    seq_count = lax.axis_size("seq")
    head_count = lax.axis_size("head")
    inner = all_heads * head_dim * head_count
    me = lax.axis_index("seq")
    mine = lax.axis_index("head")
    half = (me // PAIR) % 2
    heads = all_heads // 2
    chans = heads * head_dim
    depth = w_xz.shape[0]

    before = shifted(tokens[rows - HALO :], "seq", 1)
    ext_own = jnp.concatenate([before, tokens], axis=0)
    share = tokens.shape[1] // head_count
    ext_other = lax.all_gather(
        swapped(cut(ext_own, mine, share, 1), "seq", PAIR), "head", axis=1, tiled=True
    )

    def halves(which):
        part = w_xz[:, which, :]
        return cut(part, half, chans, 1), cut(part, 1 - half, chans, 1)

    x_pieces = spread(*halves(0), seq_count)
    z_pieces = spread(*halves(1), seq_count)
    out_pieces = spread(cut(w_out, half, chans, 0), cut(w_out, 1 - half, chans, 0), seq_count)
    part = depth // head_count
    w_bc_all = lax.all_gather(cut(w_bc, mine, part, 0), ("seq", "head"), axis=0, tiled=True)

    logdec = -decay_code.astype(F32) / (16.0 * rows * seq_count)
    ld_own = cut(logdec, half, heads, 1)
    ld = jnp.stack([ld_own, swapped(cut(logdec, 1 - half, heads, 1), "seq", PAIR)])
    blocks = rows // Q
    cum = jnp.cumsum(ld.reshape(2, blocks, Q, heads), axis=2)
    cumt = cum.transpose(0, 1, 3, 2)
    ends = cum[:, :, -1:, :]
    remaining = jnp.repeat(jnp.exp(ends - cum).reshape(2, rows, heads), head_dim, axis=2)
    block_decay = jnp.repeat(jnp.exp(ends), head_dim, axis=3)
    cum = cum.reshape(2, rows, heads)
    grown = jnp.repeat(jnp.exp(cum), head_dim, axis=2)
    totals = lax.all_gather(jnp.sum(logdec, axis=0), "seq", axis=0)
    totals = cut(totals, half, heads, 1)
    places = jnp.arange(seq_count)

    def decay_between(low, high):
        chosen = jnp.where((places >= low) & (places < high), 1.0, 0.0)[:, None]
        return jnp.repeat(jnp.exp(jnp.sum(chosen * totals, axis=0)), head_dim)[None, :]

    def project(ext, pieces):
        total = None
        for mask, piece in pieces.items():
            term = dot(cut(ext, me ^ mask, depth, 1), piece)
            total = term if total is None else total + term
        return total.astype(BF16)

    x_pre = jnp.stack([project(ext_own, x_pieces), project(ext_other, x_pieces)])
    bc_pre = jnp.stack([dot(ext_own, w_bc_all).astype(BF16), dot(ext_other, w_bc_all).astype(BF16)])
    z_val = jnp.stack([project(tokens, z_pieces), project(ext_other[HALO:], z_pieces)])

    ranges = [me, me ^ PAIR]
    first = jnp.stack([(r == 0).astype(jnp.int32) for r in ranges])

    def padded(tail):
        return jnp.pad(tail, ((HALO - tail.shape[0], 0), (0, 0)))

    x_conv, bc_conv, added = front(
        first,
        x_pre,
        bc_pre,
        padded(cut(tail_x, half, chans, 1)),
        padded(tail_bc),
        cut(conv_x, half, chans, 1),
        conv_bc,
        remaining,
    )

    inside = [jnp.zeros_like(added[:, 0])]
    for b in range(blocks):
        inside.append(block_decay[:, b] * inside[-1] + added[:, b])
    ending = inside.pop()

    group = 4
    across = swapped(ending.astype(BF16), "seq", 1).astype(F32)
    ended = {0: ending[0], PAIR: ending[1], 1: across[0], PAIR | 1: across[1]}
    base = (me // group) * group
    groups = seq_count // group
    total = 0.0
    for mask, value in ended.items():
        total = total + decay_between((me ^ mask) + 1, base + group) * value
    carry = shifted(total.astype(BF16), "seq", group).astype(F32)
    covered = 1
    while covered < groups - 1:
        more = shifted(carry.astype(BF16), "seq", group * covered).astype(F32)
        carry = carry + decay_between(base - group * covered, base) * more
        covered *= 2
    begin = cut(state_in, half, heads, 0).transpose(2, 0, 1).reshape(nstate, chans)
    incoming = []
    for place in ranges:
        value = decay_between(0, place) * begin + decay_between(base, place) * carry
        for mask, ended_value in ended.items():
            scale = jnp.where((me ^ mask) < place, decay_between((me ^ mask) + 1, place), 0.0)
            value = value + scale * ended_value
        incoming.append(value)
    opening = jnp.stack(incoming)
    states = []
    for b in range(blocks):
        states.append(opening + inside[b])
        opening = block_decay[:, b] * opening

    y_in = intra(x_conv, bc_conv, cum, cumt, heads)
    gated, squares = gate(
        y_in,
        x_conv,
        bc_conv,
        jnp.stack(states, axis=1),
        grown,
        jnp.repeat(cut(skip_gain, half, heads, 0), head_dim)[None, :],
        z_val,
        cut(norm_gain, half, chans, 0)[None, :],
    )

    squares = squares[0, :, 0] + swapped(squares[1, :, 0], "seq", PAIR)
    bit = 1
    while bit < head_count:
        squares = squares + swapped(squares, "head", bit)
        bit *= 2
    scale = lax.rsqrt(squares / inner + 1e-05)[:, None]

    per = seq_count // head_count
    stacked = jnp.stack([out_pieces[mask] for mask in range(seq_count)])

    def columns(relative):
        base_piece = (mine ^ relative) * per
        return [lax.dynamic_index_in_dim(stacked, me ^ (base_piece + j), 0, keepdims=False) for j in range(per)]

    near = jnp.concatenate([c for r in range(0, head_count, 2) for c in columns(r)], axis=1)
    far = jnp.concatenate([c for r in range(1, head_count, 2) for c in columns(r)], axis=1)
    flat = gated.reshape(2 * rows, chans)
    received = swapped(dot(flat, far).astype(BF16), "head", 1)
    sums = dot(flat, near) + received.astype(F32)
    sums = sums.reshape(2, rows, head_count // 2, -1)

    def fold_head(value):
        count = value.shape[2]
        while count > 1:
            count //= 2
            got = swapped(value[:, :, count:].astype(BF16), "head", 2 * count)
            value = value[:, :, :count] + got.astype(F32)
        return value

    def fold_pair(value):
        return value[:1] + swapped(value[1:].astype(BF16), "seq", PAIR).astype(F32)

    width = sums.shape[3] // 2
    left = fold_pair(fold_head(sums[..., :width]))
    right = fold_head(fold_pair(sums[..., width:]))
    result = jnp.concatenate([left, right], axis=3).reshape(rows, 2 * width)
    return (result * scale).astype(BF16)


def solution(mesh):
    return jax.shard_map(
        local,
        mesh=mesh,
        in_specs=(
            P("seq", None),
            P("seq", None, "head"),
            P("seq", None),
            P(None, "head"),
            P(),
            P(None, "head"),
            P(),
            P("seq", "head"),
            P("head"),
            P("head", None, None),
            P("head"),
            P("head", "seq"),
        ),
        out_specs=P("seq", "head"),
        check_vma=False,
    )
```

time: 653 us -> 408 us (0.62)
  waiting for transfers between devices: 414 us -> 154 us
  blocking collectives: 5.85 us -> 29.9 us
  other arithmetic: 28.3 us -> 6.38 us
  local copies, waits for them, and re-layouts: 78 us -> 64.4 us
  Pallas kernels: 0 us -> 12 us
  starting transfers between devices: 66.2 us -> 74.9 us
    all_gather x3 -> x2, waiting for transfers between devices: 270 us -> 0.02 us  [the longest x1 0.02 us: local(): lax.all_gather(swapped(cut(ext_own, mine, share, 1), 'seq', PAIR), 'head'...]
    ppermute x9 -> x34, waiting for transfers between devices: 63.1 us -> 154 us  [the longest x32 151 us: swapped(): return lax.ppermute(value, axis, [(i, i ^ bit) for i in range(size)])]
    reduce_scatter x1 -> x0, waiting for transfers between devices: 79.4 us -> none  [local(): lax.psum_scatter(partial_out, 'head', scatter_dimension=1, tiled=True)]
    dynamic_update_slice x4 -> x0, local copies, waits for them, and re-layouts: 46 us -> none  [local(): local_state, parts = lax.scan(block_step, jnp.zeros_like(state_in), inputs)]
    unnamed x0 -> x1, blocking collectives: none -> 29.9 us
    slice x10 -> x9, local copies, waits for them, and re-layouts: 0.82 us -> 15.1 us  [the longest x1 6.54 us: halves(): part = w_xz[:, which, :]]
    reshape x5 -> x6, local copies, waits for them, and re-layouts: 6.35 us -> 18.6 us  [the longest x2 14.4 us: local(): sums = sums.reshape(2, rows, head_count // 2, -1)]
    add x7 -> x9, other arithmetic: 13.7 us -> 1.56 us  [the longest x2 0.57 us: fold_head(): value = value[:, :, :count] + got.astype(F32)]
  transfers between devices with their start and end apart: 13 -> 36, of which waited for: 12 -> 16; matrix products, arithmetic and copies ran while one was open for 20% -> 16% of each run, Pallas kernels for 0% -> 1%
where the time goes in v1:
time: 408 us; the launch traced here: 401 us
  waiting for transfers between devices  154 us (38%)
  starting transfers between devices  74.9 us (18%)
  local copies, waits for them, and re-layouts  64.4 us (16%)
  matrix products  44.1 us (11%)
  blocking collectives  29.9 us (7%)
  between operations  15.9 us (4%)
  Pallas kernels  12 us (3%)
  other arithmetic  6.38 us (2%)
    ppermute x32, waiting for transfers between devices, swapped(): return lax.ppermute(value, axis, [(i, i ^ bit) for i in range(size)])  151 us
    ppermute x32, starting transfers between devices, swapped(): return lax.ppermute(value, axis, [(i, i ^ bit) for i in range(size)])  71 us
    dot_general x36, matrix products, dot(): return jnp.dot(a, b, preferred_element_type=F32)  44.1 us
    unnamed x1, blocking collectives  29.9 us
    reshape x2, local copies, waits for them, and re-layouts, local(): sums = sums.reshape(2, rows, head_count // 2, -1)  14.4 us
    dynamic_slice x10, local copies, waits for them, and re-layouts, cut(): return lax.dynamic_slice_in_dim(value, index * size, size, axis)  11.5 us
    unnamed x109, local copies, waits for them, and re-layouts  11.4 us
  transfers between devices with their start and end apart: 36, of which 16 were waited for; matrix products, arithmetic and copies ran while one was open for 16% of the time, Pallas kernels for 1%

profile of v1, /device:TPU:0, one launch (start us, length us, event | category | flops | bytes accessed | tf_op | source)
XLA Modules:
  0.0 401.2 jit_solution(16862378267473010360)
XLA Ops:
  6.5 6.5 %fusion.139 = (bf16[512,1,1024]{2,1,0:T(2,128)(2,1)S(1)}, bf16[512,1,1024]{2,1,0:T(2,128)(2,1)}) fusion(bf16[512,2,1024]{2,1,0:T(2,128)(2,1)} %param.13), kind=kLoop, calls=%fused_computation.267 | loop fusion | bytes 4194304 | tf_op jit(solution)/shard_map/slice | solution.py:240
  13.1 6.8 %constant_dynamic-slice_fusion.2 = (bf16[512,1,512]{2,1,0:T(2,128)(2,1)}, bf16[512,1,512]{2,1,0:T(2,128)(2,1)}, bf16[512,1,512]{2,1,0:T(2,128)(2,1)S(1)}, bf16[512,1,512]{2,1,0:T(2,128)(2,1)}) fusion(bf16[512,1,1024]{2,1,0:T(2,128)(2,1)S(1)} %get-tuple-element.45, s32[]{:T(128)S(6)} %select_n.317, s32[]{:T(128)S(6)} %select_n.315, ...), kind=kLoop, calls=%fused_computation.188 | loop fusion | bytes 4194312 | tf_op jit(solution)/shard_map/dynamic_slice | solution.py:29
  41.1 29.9 %all-reduce.3 = f32[8,16]{1,0:T(8,128)S(1)} all-reduce(f32[8,16]{1,0:T(8,128)S(1)} %reshape.241), channel_id=2, replica_groups=mesh['seq'=8,'head'=4] {'seq'}, use_global_device_ids=true, to_apply=%add.2 | all-reduce | flops 128 | bytes 1024
  78.6 16.8 %collective-permute-start.1 = (bf16[512,512]{1,0:T(8,128)(2,1)}, bf16[512,512]{1,0:T(8,128)(2,1)}, u32[]{:S(2)}, u32[]{:S(2)}) collective-permute-start(bf16[512,512]{1,0:T(8,128)(2,1)} %bitcast.186), channel_id=1, source_target_pairs={{0,8},{4,12},{8,0},{12,4},{16,24},{20,28},{24,16},{28,20},{1,9},{5... | collective-permute-start | bytes 1572872 | tf_op jit(solution)/shard_map/ppermute | solution.py:20
  107.8 21.0 %collective-permute-done.8 = bf16[528,1024]{1,0:T(8,128)(2,1)} collective-permute-done((bf16[528,1024]{1,0:T(8,128)(2,1)}, bf16[528,1024]{1,0:T(8,128)(2,1)}, u32[]{:S(2)}, u32[]{:S(2)}) %collective-permute-start.8) | collective-permute-done | bytes 1081376 | tf_op jit(solution)/shard_map/ppermute | solution.py:20
  138.3 5.4 %collective-permute-done.12 = bf16[512,512]{1,0:T(8,128)(2,1)S(1)} collective-permute-done((bf16[512,512]{1,0:T(8,128)(2,1)}, bf16[512,512]{1,0:T(8,128)(2,1)S(1)}, u32[]{:S(2)}, u32[]{:S(2)}) %collective-permute-start.12) | collective-permute-done | bytes 524320 | tf_op jit(solution)/shard_map/ppermute | solution.py:20
  149.6 5.7 %collective-permute-done.19 = bf16[512,512]{1,0:T(8,128)(2,1)S(1)} collective-permute-done((bf16[512,512]{1,0:T(8,128)(2,1)}, bf16[512,512]{1,0:T(8,128)(2,1)S(1)}, u32[]{:S(2)}, u32[]{:S(2)}) %collective-permute-start.19) | collective-permute-done | bytes 524320 | tf_op jit(solution)/shard_map/ppermute | solution.py:20
  161.8 7.3 %collective-permute-done.20 = bf16[512,512]{1,0:T(8,128)(2,1)S(1)} collective-permute-done((bf16[512,512]{1,0:T(8,128)(2,1)S(1)}, bf16[512,512]{1,0:T(8,128)(2,1)S(1)}, u32[]{:S(2)}, u32[]{:S(2)}) %collective-permute-start.20) | collective-permute-done | bytes 524320 | tf_op jit(solution)/shard_map/ppermute | solution.py:20
  169.6 16.7 %collective-permute-done.3 = bf16[512,512]{1,0:T(8,128)(2,1)S(1)} collective-permute-done((bf16[512,512]{1,0:T(8,128)(2,1)}, bf16[512,512]{1,0:T(8,128)(2,1)S(1)}, u32[]{:S(2)}, u32[]{:S(2)}) %collective-permute-start.3) | collective-permute-done | bytes 524320 | tf_op jit(solution)/shard_map/ppermute | solution.py:20
  192.9 17.7 %collective-permute-done.14 = bf16[512,512]{1,0:T(8,128)(2,1)S(1)} collective-permute-done((bf16[512,512]{1,0:T(8,128)(2,1)S(1)}, bf16[512,512]{1,0:T(8,128)(2,1)S(1)}, u32[]{:S(2)}, u32[]{:S(2)}) %collective-permute-start.14) | collective-permute-done | bytes 524320 | tf_op jit(solution)/shard_map/ppermute | solution.py:20
  210.6 6.3 %collective-permute-start.23 = (bf16[512,512]{1,0:T(8,128)(2,1)S(1)}, bf16[512,512]{1,0:T(8,128)(2,1)S(1)}, u32[]{:S(2)}, u32[]{:S(2)}) collective-permute-start(bf16[512,512]{1,0:T(8,128)(2,1)S(1)} %collective-permute-done.22), channel_id=1, source_target_pairs={{0,4},{4,0},{8,12},{12,8},{16,20},{20,16},{24,28},{28,24},{1,5},{5... | collective-permute-start | bytes 1572872 | tf_op jit(solution)/shard_map/ppermute | solution.py:20
  220.0 12.3 %collective-permute-done.24 = bf16[512,512]{1,0:T(8,128)(2,1)S(1)} collective-permute-done((bf16[512,512]{1,0:T(8,128)(2,1)S(1)}, bf16[512,512]{1,0:T(8,128)(2,1)S(1)}, u32[]{:S(2)}, u32[]{:S(2)}) %collective-permute-start.24) | collective-permute-done | bytes 524320 | tf_op jit(solution)/shard_map/ppermute | solution.py:20
  233.5 18.7 %collective-permute-done.18 = bf16[512,512]{1,0:T(8,128)(2,1)S(1)} collective-permute-done((bf16[512,512]{1,0:T(8,128)(2,1)S(1)}, bf16[512,512]{1,0:T(8,128)(2,1)S(1)}, u32[]{:S(2)}, u32[]{:S(2)}) %collective-permute-start.18) | collective-permute-done | bytes 524320 | tf_op jit(solution)/shard_map/ppermute | solution.py:20
  253.9 7.1 %collective-permute-done.25 = bf16[512,512]{1,0:T(8,128)(2,1)S(1)} collective-permute-done((bf16[512,512]{1,0:T(8,128)(2,1)S(1)}, bf16[512,512]{1,0:T(8,128)(2,1)S(1)}, u32[]{:S(2)}, u32[]{:S(2)}) %collective-permute-start.25) | collective-permute-done | bytes 524320 | tf_op jit(solution)/shard_map/ppermute | solution.py:20
  263.1 4.2 %fusion.38 = bf16[1,528,256]{2,1,0:T(8,128)(2,1)S(1)} fusion(bf16[528,4096]{1,0:T(8,128)(2,1)} %copy-done.7, bf16[4096,256]{1,0:T(8,128)(2,1)} %all-gather.6.cloned.1.call-done), kind=kOutput, calls=%fused_computation.60 | convolution fusion | flops 1107431424 | bytes 6692864 | tf_op jit(solution)/shard_map/dot_general | solution.py:42
  279.1 4.9 %front.1 = (bf16[2,512,512]{2,1,0:T(8,128)(2,1)S(1)}, bf16[2,512,256]{2,1,0:T(8,128)(2,1)S(1)}, f32[2,2,128,512]{3,2,1,0:T(8,128)S(1)}) custom-call(s32[2]{0:T(128)S(1)} %add_convert_fusion.1.first_ref, bf16[2,528,512]{2,1,0:T(8,128)(2,1)S(1)} %pad_maximum_fusion.x_ref, bf16[2,528,256]{2,1,0:T(8,128)(2,1)S(1)} %pad_maximum_fusion.3.bc_ref, ...), custom_call_target="tpu_custom_call" | custom-call | tf_op jit(solution)/shard_map/front/pallas_call | solution.py:125
  306.5 7.1 %collective-permute-done.26 = bf16[1024,2048]{1,0:T(8,128)(2,1)S(1)} collective-permute-done((bf16[1024,2048]{1,0:T(8,128)(2,1)S(1)}, bf16[1024,2048]{1,0:T(8,128)(2,1)S(1)}, u32[]{:S(2)}, u32[]{:S(2)}) %collective-permute-start.26) | collective-permute-done | bytes 4194336 | tf_op jit(solution)/shard_map/ppermute | solution.py:20
  313.7 5.1 %convert_add_fusion = f32[1024,2048]{1,0:T(8,128)} fusion(bf16[1024,2048]{1,0:T(8,128)(2,1)S(1)} %collective-permute-done.26, bf16[1024,512]{1,0:T(8,128)(2,1)S(1)} %bitcast.190, bf16[512,512]{1,0:T(8,128)(2,1)S(1)} %copy-done.29, bf16[512,512]{1,0:T(8,128)(2,1)S(1)} %copy-done.30, bf16[512,512]{1,0:T(8,128)(2,1)S(1)} %copy-done.31, ...), kind=kOutput, calls=%fused_computation | convolution fusion | flops 2160066560 | bytes 15728640 | tf_op jit(solution)/shard_map/dot_general | solution.py:42
  318.8 12.0 %reshape.239 = f32[2,512,2,1024]{3,2,1,0:T(2,128)} reshape(f32[1024,2048]{1,0:T(8,128)} %convert_add_fusion) | data formatting | bytes 16777216 | tf_op jit(solution)/shard_map/reshape | solution.py:360
  334.2 9.7 %collective-permute-start.29 = (bf16[1,512,2,512]{3,1,2,0:T(8,128)(2,1)}, bf16[1,512,2,512]{3,1,2,0:T(8,128)(2,1)S(1)}, u32[]{:S(2)}, u32[]{:S(2)}) collective-permute-start(bf16[1,512,2,512]{3,1,2,0:T(8,128)(2,1)} %copy.52), channel_id=1, source_target_pairs={{0,8},{4,12},{8,0},{12,4},{16,24},{20,28},{24,16},{28,20},{1,9},{5... | collective-permute-start | bytes 3145736 | tf_op jit(solution)/shard_map/ppermute | solution.py:20
  343.8 4.3 %slice.123 = bf16[2,512,1,512]{3,2,1,0:T(2,128)(2,1)S(1)} slice(f32[2,512,2,1024]{3,2,1,0:T(2,128)} %reshape.239), slice={[0:2], [0:512], [1:2], [0:512]} | slice | bytes 2097152 | tf_op jit(solution)/shard_map/slice | solution.py:366
  353.3 14.2 %collective-permute-done.29 = bf16[1,512,2,512]{3,1,2,0:T(8,128)(2,1)S(1)} collective-permute-done((bf16[1,512,2,512]{3,1,2,0:T(8,128)(2,1)}, bf16[1,512,2,512]{3,1,2,0:T(8,128)(2,1)S(1)}, u32[]{:S(2)}, u32[]{:S(2)}) %collective-permute-start.29) | collective-permute-done | bytes 1048608 | tf_op jit(solution)/shard_map/ppermute | solution.py:20
  370.3 4.5 %collective-permute-done.27 = bf16[2,512,1,512]{3,1,2,0:T(8,128)(2,1)S(1)} collective-permute-done((bf16[2,512,1,512]{3,1,2,0:T(8,128)(2,1)S(1)}, bf16[2,512,1,512]{3,1,2,0:T(8,128)(2,1)S(1)}, u32[]{:S(2)}, u32[]{:S(2)}) %collective-permute-start.27) | collective-permute-done | bytes 1048608 | tf_op jit(solution)/shard_map/ppermute | solution.py:20
  377.6 10.1 %collective-permute-done.31 = f32[512]{0:T(512)S(1)} collective-permute-done((f32[512]{0:T(512)S(1)}, f32[512]{0:T(512)S(1)}, u32[]{:S(2)}, u32[]{:S(2)}) %collective-permute-start.31) | collective-permute-done | bytes 2080 | tf_op jit(solution)/shard_map/ppermute | solution.py:20
  (321 shorter events, 131.1 us)
Async XLA Ops:
  6.5 256.6 %all-gather.6.cloned.1.call-start = ((), (), s32[]{:S(2)}) async-start(), calls=%async_computation.1 | async-start | bytes 2162688 | tf_op jit(solution)/shard_map/all_gather | solution.py:247
  20.8 110.2 %collective-permute-start.2 = (bf16[512,512]{1,0:T(8,128)(2,1)}, bf16[512,512]{1,0:T(8,128)(2,1)}, u32[]{:S(2)}, u32[]{:S(2)}) collective-permute-start(bf16[512,512]{1,0:T(8,128)(2,1)} %bitcast.187), channel_id=1, source_target_pairs={{0,16},{4,20},{8,24},{12,28},{16,0},{20,4},{24,8},{28,12},{1,17},{... | collective-permute-start | bytes 1572872 | tf_op jit(solution)/shard_map/ppermute | solution.py:20
  24.9 133.3 %collective-permute-start.4 = (bf16[512,512]{1,0:T(8,128)(2,1)}, bf16[512,512]{1,0:T(8,128)(2,1)}, u32[]{:S(2)}, u32[]{:S(2)}) collective-permute-start(bf16[512,512]{1,0:T(8,128)(2,1)} %bitcast.187), channel_id=1, source_target_pairs={{0,4},{4,0},{8,12},{12,8},{16,20},{20,16},{24,28},{28,24},{1,5},{5... | collective-permute-start | bytes 1572872 | tf_op jit(solution)/shard_map/ppermute | solution.py:20
  27.3 71.1 %collective-permute-start = (bf16[16,4096]{1,0:T(8,128)(2,1)S(1)}, bf16[16,4096]{1,0:T(8,128)(2,1)S(1)}, u32[]{:S(2)}, u32[]{:S(2)}) collective-permute-start(bf16[16,4096]{1,0:T(8,128)(2,1)S(1)} %slice.86), channel_id=1, source_target_pairs={{0,4},{4,8},{8,12},{12,16},{16,20},{20,24},{24,28},{1,5},{5,9},{9,... | collective-permute-start | bytes 393224 | tf_op jit(solution)/shard_map/ppermute | solution.py:25
  31.2 236.1 %all-gather.4.cloned.1.call-start = ((), (), s32[]{:S(2)}) async-start(), calls=%async_computation | async-start | bytes 5406720 | tf_op jit(solution)/shard_map/all_gather | solution.py:235
  31.4 47.1 %collective-permute-start.9 = (f32[512,8]{0,1:T(8,128)S(1)}, f32[512,8]{0,1:T(8,128)S(1)}, u32[]{:S(2)}, u32[]{:S(2)}) collective-permute-start(f32[512,8]{0,1:T(8,128)S(1)} %get-tuple-element.54), channel_id=1, source_target_pairs={{0,8},{4,12},{8,0},{12,4},{16,24},{20,28},{24,16},{28,20},{1,9},{5... | collective-permute-start | bytes 49160 | tf_op jit(solution)/shard_map/ppermute | solution.py:20
  35.0 111.6 %collective-permute-start.13 = (bf16[512,512]{1,0:T(8,128)(2,1)}, bf16[512,512]{1,0:T(8,128)(2,1)}, u32[]{:S(2)}, u32[]{:S(2)}) collective-permute-start(bf16[512,512]{1,0:T(8,128)(2,1)} %bitcast.185), channel_id=1, source_target_pairs={{0,16},{4,20},{8,24},{12,28},{16,0},{20,4},{24,8},{28,12},{1,17},{... | collective-permute-start | bytes 1572872 | tf_op jit(solution)/shard_map/ppermute | solution.py:20
  78.6 56.0 %collective-permute-start.1 = (bf16[512,512]{1,0:T(8,128)(2,1)}, bf16[512,512]{1,0:T(8,128)(2,1)}, u32[]{:S(2)}, u32[]{:S(2)}) collective-permute-start(bf16[512,512]{1,0:T(8,128)(2,1)} %bitcast.186), channel_id=1, source_target_pairs={{0,8},{4,12},{8,0},{12,4},{16,24},{20,28},{24,16},{28,20},{1,9},{5... | collective-permute-start | bytes 1572872 | tf_op jit(solution)/shard_map/ppermute | solution.py:20
  102.1 26.7 %collective-permute-start.8 = (bf16[528,1024]{1,0:T(8,128)(2,1)}, bf16[528,1024]{1,0:T(8,128)(2,1)}, u32[]{:S(2)}, u32[]{:S(2)}) collective-permute-start(bf16[528,1024]{1,0:T(8,128)(2,1)} %constant_dynamic-slice_fusion.11), channel_id=1, source_target_pairs={{0,8},{4,12},{8,0},{12,4},{16,24},{20,28},{24,16},{28,20},{1,9},{5... | collective-permute-start | bytes 3244040 | tf_op jit(solution)/shard_map/ppermute | solution.py:20
  143.7 46.2 %collective-permute-start.22 = (bf16[512,512]{1,0:T(8,128)(2,1)S(1)}, bf16[512,512]{1,0:T(8,128)(2,1)S(1)}, u32[]{:S(2)}, u32[]{:S(2)}) collective-permute-start(bf16[512,512]{1,0:T(8,128)(2,1)S(1)} %copy-done.26), channel_id=1, source_target_pairs={{0,16},{4,20},{8,24},{12,28},{16,0},{20,4},{24,8},{28,12},{1,17},{... | collective-permute-start | bytes 1572872 | tf_op jit(solution)/shard_map/ppermute | solution.py:20
  149.1 37.7 %collective-permute-start.6 = (bf16[512,512]{1,0:T(8,128)(2,1)}, bf16[512,512]{1,0:T(8,128)(2,1)S(1)}, u32[]{:S(2)}, u32[]{:S(2)}) collective-permute-start(bf16[512,512]{1,0:T(8,128)(2,1)} %collective-permute-done.2), channel_id=1, source_target_pairs={{0,4},{4,0},{8,12},{12,8},{16,20},{20,16},{24,28},{28,24},{1,5},{5... | collective-permute-start | bytes 1572872 | tf_op jit(solution)/shard_map/ppermute | solution.py:20
  155.3 31.0 %collective-permute-start.3 = (bf16[512,512]{1,0:T(8,128)(2,1)}, bf16[512,512]{1,0:T(8,128)(2,1)S(1)}, u32[]{:S(2)}, u32[]{:S(2)}) collective-permute-start(bf16[512,512]{1,0:T(8,128)(2,1)} %collective-permute-done.1), channel_id=1, source_target_pairs={{0,16},{4,20},{8,24},{12,28},{16,0},{20,4},{24,8},{28,12},{1,17},{... | collective-permute-start | bytes 1572872 | tf_op jit(solution)/shard_map/ppermute | solution.py:20
  158.2 29.7 %collective-permute-start.5 = (bf16[512,512]{1,0:T(8,128)(2,1)}, bf16[512,512]{1,0:T(8,128)(2,1)S(1)}, u32[]{:S(2)}, u32[]{:S(2)}) collective-permute-start(bf16[512,512]{1,0:T(8,128)(2,1)} %collective-permute-done.1), channel_id=1, source_target_pairs={{0,4},{4,0},{8,12},{12,8},{16,20},{20,16},{24,28},{28,24},{1,5},{5... | collective-permute-start | bytes 1572872 | tf_op jit(solution)/shard_map/ppermute | solution.py:20
  169.1 48.2 %collective-permute-start.17 = (bf16[512,512]{1,0:T(8,128)(2,1)}, bf16[512,512]{1,0:T(8,128)(2,1)S(1)}, u32[]{:S(2)}, u32[]{:S(2)}) collective-permute-start(bf16[512,512]{1,0:T(8,128)(2,1)} %collective-permute-done.13), channel_id=1, source_target_pairs={{0,4},{4,0},{8,12},{12,8},{16,20},{20,16},{24,28},{28,24},{1,5},{5... | collective-permute-start | bytes 1572872 | tf_op jit(solution)/shard_map/ppermute | solution.py:20
  186.3 24.3 %collective-permute-start.14 = (bf16[512,512]{1,0:T(8,128)(2,1)S(1)}, bf16[512,512]{1,0:T(8,128)(2,1)S(1)}, u32[]{:S(2)}, u32[]{:S(2)}) collective-permute-start(bf16[512,512]{1,0:T(8,128)(2,1)S(1)} %collective-permute-done.12), channel_id=1, source_target_pairs={{0,16},{4,20},{8,24},{12,28},{16,0},{20,4},{24,8},{28,12},{1,17},{... | collective-permute-start | bytes 1572872 | tf_op jit(solution)/shard_map/ppermute | solution.py:20
  186.8 31.1 %collective-permute-start.16 = (bf16[512,512]{1,0:T(8,128)(2,1)S(1)}, bf16[512,512]{1,0:T(8,128)(2,1)S(1)}, u32[]{:S(2)}, u32[]{:S(2)}) collective-permute-start(bf16[512,512]{1,0:T(8,128)(2,1)S(1)} %collective-permute-done.12), channel_id=1, source_target_pairs={{0,4},{4,0},{8,12},{12,8},{16,20},{20,16},{24,28},{28,24},{1,5},{5... | collective-permute-start | bytes 1572872 | tf_op jit(solution)/shard_map/ppermute | solution.py:20
  187.9 45.4 %collective-permute-start.21 = (bf16[512,512]{1,0:T(8,128)(2,1)S(1)}, bf16[512,512]{1,0:T(8,128)(2,1)S(1)}, u32[]{:S(2)}, u32[]{:S(2)}) collective-permute-start(bf16[512,512]{1,0:T(8,128)(2,1)S(1)} %collective-permute-done.20), channel_id=1, source_target_pairs={{0,4},{4,0},{8,12},{12,8},{16,20},{20,16},{24,28},{28,24},{1,5},{5... | collective-permute-start | bytes 1572872 | tf_op jit(solution)/shard_map/ppermute | solution.py:20
  189.9 42.4 %collective-permute-start.24 = (bf16[512,512]{1,0:T(8,128)(2,1)S(1)}, bf16[512,512]{1,0:T(8,128)(2,1)S(1)}, u32[]{:S(2)}, u32[]{:S(2)}) collective-permute-start(bf16[512,512]{1,0:T(8,128)(2,1)S(1)} %collective-permute-done.20), channel_id=1, source_target_pairs={{0,16},{4,20},{8,24},{12,28},{16,0},{20,4},{24,8},{28,12},{1,17},{... | collective-permute-start | bytes 1572872 | tf_op jit(solution)/shard_map/ppermute | solution.py:20
  217.4 36.1 %collective-permute-start.7 = (bf16[512,512]{1,0:T(8,128)(2,1)S(1)}, bf16[512,512]{1,0:T(8,128)(2,1)S(1)}, u32[]{:S(2)}, u32[]{:S(2)}) collective-permute-start(bf16[512,512]{1,0:T(8,128)(2,1)S(1)} %collective-permute-done.3), channel_id=1, source_target_pairs={{0,4},{4,0},{8,12},{12,8},{16,20},{20,16},{24,28},{28,24},{1,5},{5... | collective-permute-start | bytes 1572872 | tf_op jit(solution)/shard_map/ppermute | solution.py:20
  217.9 34.3 %collective-permute-start.18 = (bf16[512,512]{1,0:T(8,128)(2,1)S(1)}, bf16[512,512]{1,0:T(8,128)(2,1)S(1)}, u32[]{:S(2)}, u32[]{:S(2)}) collective-permute-start(bf16[512,512]{1,0:T(8,128)(2,1)S(1)} %collective-permute-done.14), channel_id=1, source_target_pairs={{0,4},{4,0},{8,12},{12,8},{16,20},{20,16},{24,28},{28,24},{1,5},{5... | collective-permute-start | bytes 1572872 | tf_op jit(solution)/shard_map/ppermute | solution.py:20
  232.3 28.8 %collective-permute-start.25 = (bf16[512,512]{1,0:T(8,128)(2,1)S(1)}, bf16[512,512]{1,0:T(8,128)(2,1)S(1)}, u32[]{:S(2)}, u32[]{:S(2)}) collective-permute-start(bf16[512,512]{1,0:T(8,128)(2,1)S(1)} %collective-permute-done.24), channel_id=1, source_target_pairs={{0,4},{4,0},{8,12},{12,8},{16,20},{20,16},{24,28},{28,24},{1,5},{5... | collective-permute-start | bytes 1572872 | tf_op jit(solution)/shard_map/ppermute | solution.py:20
  334.2 33.3 %collective-permute-start.29 = (bf16[1,512,2,512]{3,1,2,0:T(8,128)(2,1)}, bf16[1,512,2,512]{3,1,2,0:T(8,128)(2,1)S(1)}, u32[]{:S(2)}, u32[]{:S(2)}) collective-permute-start(bf16[1,512,2,512]{3,1,2,0:T(8,128)(2,1)} %copy.52), channel_id=1, source_target_pairs={{0,8},{4,12},{8,0},{12,4},{16,24},{20,28},{24,16},{28,20},{1,9},{5... | collective-permute-start | bytes 3145736 | tf_op jit(solution)/shard_map/ppermute | solution.py:20
  348.5 26.3 %collective-permute-start.27 = (bf16[2,512,1,512]{3,1,2,0:T(8,128)(2,1)S(1)}, bf16[2,512,1,512]{3,1,2,0:T(8,128)(2,1)S(1)}, u32[]{:S(2)}, u32[]{:S(2)}) collective-permute-start(bf16[2,512,1,512]{3,1,2,0:T(8,128)(2,1)S(1)} %copy.53), channel_id=1, source_target_pairs={{0,2},{1,3},{2,0},{3,1},{4,6},{5,7},{6,4},{7,5},{8,10},{9,11},{10,... | collective-permute-start | bytes 3145736 | tf_op jit(solution)/shard_map/ppermute | solution.py:20
  368.0 24.5 %collective-permute-start.30 = (bf16[1,512,1,512]{3,1,2,0:T(8,128)(2,1)S(1)}, bf16[1,512,1,512]{3,1,2,0:T(8,128)(2,1)S(1)}, u32[]{:S(2)}, u32[]{:S(2)}) collective-permute-start(bf16[1,512,1,512]{3,1,2,0:T(8,128)(2,1)S(1)} %slice.178), channel_id=1, source_target_pairs={{0,2},{1,3},{2,0},{3,1},{4,6},{5,7},{6,4},{7,5},{8,10},{9,11},{10,... | collective-permute-start | bytes 1572872 | tf_op jit(solution)/shard_map/ppermute | solution.py:20
  (58 other events, 908.9 us)
Sparse Core Ops, SparseCore 0:
  31.3 65.2 all-gather.5
  131.1 34.7 all-gather.3

commit v2 on v1

--- a/solution.py
+++ b/solution.py
@@ -29,47 +29,78 @@
     return lax.dynamic_slice_in_dim(value, index * size, size, axis)
 
 
-def spread(own, other, seq_count):
+def after(value, *others):
+    return lax.optimization_barrier((value, *others))[0]
+
+
+def spread(own, other, seq_count, earlier=None):
+    bits = [1 << b for b in range(seq_count.bit_length() - 1)]
+    bits = [b for b in bits if b > PAIR] + [b for b in bits if b < PAIR]
+    if earlier is not None:
+        other = after(other, earlier[PAIR])
     pieces = {0: own, PAIR: swapped(other, "seq", PAIR)}
-    bits = [1 << b for b in range(seq_count.bit_length() - 1)]
-    for bit in [b for b in bits if b > PAIR] + [b for b in bits if b < PAIR]:
+    for bit in bits:
         for mask in list(pieces):
-            pieces[mask | bit] = swapped(pieces[mask], "seq", bit)
+            value = pieces[mask]
+            if mask == 0 and earlier is not None:
+                value = after(value, earlier[bit] if bit > PAIR else earlier[PAIR | bit])
+            pieces[mask | bit] = swapped(value, "seq", bit)
     return pieces
+
+
+def natural(value, axis_name, bit, axis):
+    other = swapped(value, axis_name, bit)
+    low = (lax.axis_index(axis_name) & bit) == 0
+    return jnp.where(
+        low, jnp.concatenate([value, other], axis=axis), jnp.concatenate([other, value], axis=axis)
+    )
+
+
+def by_xor(values, index):
+    bit = 1
+    while bit < len(values):
+        flip = (index & bit) != 0
+        values = [jnp.where(flip, values[j ^ bit], values[j]) for j in range(len(values))]
+        bit *= 2
+    return values
 
 
 def dot(a, b):
     return jnp.dot(a, b, preferred_element_type=F32)
 
 
-def front_kernel(first_ref, x_ref, bc_ref, tx_ref, tbc_ref, kx_ref, kbc_ref, dec_ref, xc_ref, bcc_ref, f_ref):
-    is_first = first_ref[pl.program_id(0)] == 1
+def front_kernel(
+    first_ref, xo_ref, xp_ref, bo_ref, bp_ref, tx_ref, tbc_ref, kx_ref, kbc_ref, dec_ref, xc_ref, bcc_ref, f_ref
+):
     rows = xc_ref.shape[1]
-
-    def conv(pre_ref, tail_ref, k_ref):
-        pre = pre_ref[0].astype(F32)
-        halo = jnp.where(is_first, tail_ref[...].astype(F32), pre[:HALO])
-        whole = jnp.concatenate([halo, pre[HALO:]], axis=0)
-        taps = k_ref.shape[0]
-        total = jnp.zeros((rows, pre.shape[1]), F32)
-        for k in range(taps):
-            start = HALO - (taps - 1) + k
-            total = total + k_ref[k : k + 1, :] * whole[start : start + rows]
-        return (total * jax.nn.sigmoid(total)).astype(BF16)
-
-    x_val = conv(x_ref, tx_ref, kx_ref)
-    bc_val = conv(bc_ref, tbc_ref, kbc_ref)
-    xc_ref[0] = x_val
-    bcc_ref[0] = bc_val
-    decayed = (x_val.astype(F32) * dec_ref[0]).astype(BF16)
-    nstate = bc_val.shape[1] // 2
-    for start in range(0, rows, Q):
-        f_ref[0, start // Q] = lax.dot_general(
-            bc_val[start : start + Q, :nstate],
-            decayed[start : start + Q],
-            (((0,), (0,)), ((), ())),
-            preferred_element_type=F32,
-        )
+    for r in range(2):
+        is_first = first_ref[r] == 1
+
+        def conv(own_ref, other_ref, tail_ref, k_ref):
+            halo = own_ref[r * HALO : (r + 1) * HALO].astype(F32)
+            halo = jnp.where(is_first, tail_ref[...].astype(F32), halo)
+            body = (own_ref[2 * HALO :] if r == 0 else other_ref[...]).astype(F32)
+            whole = jnp.concatenate([halo, body], axis=0)
+            taps = k_ref.shape[0]
+            total = jnp.zeros(body.shape, F32)
+            for k in range(taps):
+                start = HALO - (taps - 1) + k
+                total = total + k_ref[k : k + 1, :] * whole[start : start + rows]
+            return (total * jax.nn.sigmoid(total)).astype(BF16)
+
+        x_val = conv(xo_ref, xp_ref, tx_ref, kx_ref)
+        bc_val = conv(bo_ref, bp_ref, tbc_ref, kbc_ref)
+        xc_ref[r] = x_val
+        bcc_ref[r] = bc_val
+        decayed = (x_val.astype(F32) * dec_ref[r]).astype(BF16)
+        nstate = bc_val.shape[1] // 2
+        for start in range(0, rows, Q):
+            f_ref[r, start // Q] = lax.dot_general(
+                bc_val[start : start + Q, :nstate],
+                decayed[start : start + Q],
+                (((0,), (0,)), ((), ())),
+                preferred_element_type=F32,
+            )
 
 
 def intra_kernel(heads, x_ref, bc_ref, cum_ref, cumt_ref, y_ref):
@@ -114,40 +145,21 @@
     return pl.BlockSpec(shape, lambda *_: (0,) * len(shape))
 
 
-def front(first, x_pre, bc_pre, tail_x, tail_bc, conv_x, conv_bc, decay):
-    _, ext, chans = x_pre.shape
-    rows = ext - HALO
-    bcw = bc_pre.shape[2]
-
-    def ranged(n, w):
-        return pl.BlockSpec((1, n, w), lambda r: (r, 0, 0))
-
+def front(first, x_own, x_other, bc_own, bc_other, tail_x, tail_bc, conv_x, conv_bc, decay):
+    rows, chans = x_other.shape
+    bcw = bc_other.shape[1]
     return pl.pallas_call(
         front_kernel,
-        grid=(2,),
-        in_specs=[
-            pl.BlockSpec(memory_space=pltpu.SMEM),
-            ranged(ext, chans),
-            ranged(ext, bcw),
-            whole_block(tail_x.shape),
-            whole_block(tail_bc.shape),
-            whole_block(conv_x.shape),
-            whole_block(conv_bc.shape),
-            ranged(rows, chans),
-        ],
-        out_specs=[
-            ranged(rows, chans),
-            ranged(rows, bcw),
-            pl.BlockSpec((1, rows // Q, bcw // 2, chans), lambda r: (r, 0, 0, 0)),
-        ],
+        in_specs=[pl.BlockSpec(memory_space=pltpu.SMEM)] + [pl.BlockSpec(memory_space=pltpu.VMEM)] * 9,
+        out_specs=[pl.BlockSpec(memory_space=pltpu.VMEM)] * 3,
         out_shape=[
             jax.ShapeDtypeStruct((2, rows, chans), BF16),
             jax.ShapeDtypeStruct((2, rows, bcw), BF16),
             jax.ShapeDtypeStruct((2, rows // Q, bcw // 2, chans), F32),
         ],
-        compiler_params=params(1),
+        compiler_params=pltpu.CompilerParams(vmem_limit_bytes=VMEM_LIMIT),
         name="front",
-    )(first, x_pre, bc_pre, tail_x, tail_bc, conv_x, conv_bc, decay)
+    )(first, x_own, x_other, bc_own, bc_other, tail_x, tail_bc, conv_x, conv_bc, decay)
 
 
 def intra(x_conv, bc_conv, cum, cumt, heads):
@@ -229,22 +241,40 @@
     chans = heads * head_dim
     depth = w_xz.shape[0]
 
+    share = tokens.shape[1] // head_count
+    quarters = {0: swapped(cut(tokens, mine, share, 1), "seq", PAIR)}
     before = shifted(tokens[rows - HALO :], "seq", 1)
-    ext_own = jnp.concatenate([before, tokens], axis=0)
-    share = tokens.shape[1] // head_count
-    ext_other = lax.all_gather(
-        swapped(cut(ext_own, mine, share, 1), "seq", PAIR), "head", axis=1, tiled=True
-    )
-
-    def halves(which):
-        part = w_xz[:, which, :]
-        return cut(part, half, chans, 1), cut(part, 1 - half, chans, 1)
-
-    x_pieces = spread(*halves(0), seq_count)
-    z_pieces = spread(*halves(1), seq_count)
-    out_pieces = spread(cut(w_out, half, chans, 0), cut(w_out, 1 - half, chans, 0), seq_count)
-    part = depth // head_count
-    w_bc_all = lax.all_gather(cut(w_bc, mine, part, 0), ("seq", "head"), axis=0, tiled=True)
+    before_other = swapped(before, "seq", PAIR)
+    bit = head_count // 2
+    while bit >= 1:
+        for mask in list(quarters):
+            quarters[mask | bit] = swapped(quarters[mask], "head", bit)
+        bit //= 2
+    own = jnp.concatenate([before, before_other, tokens], axis=0)
+    others = jnp.stack([quarters[mask] for mask in range(head_count)])
+
+    flat_w = lax.optimization_barrier(w_xz.reshape(depth, -1))
+    full = flat_w.shape[1] // 2
+    x_w, z_w = flat_w[:, :full], flat_w[:, full:]
+    x_pieces = spread(cut(x_w, half, chans, 1), cut(x_w, 1 - half, chans, 1), seq_count)
+    z_pieces = spread(cut(z_w, half, chans, 1), cut(z_w, 1 - half, chans, 1), seq_count, x_pieces)
+    out_pieces = spread(cut(w_out, half, chans, 0), cut(w_out, 1 - half, chans, 0), seq_count, z_pieces)
+
+    narrow = w_bc.shape[1] // head_count
+    pack = max(1, 128 // narrow)
+    some = cut(w_bc, mine, narrow, 1).reshape(pack, depth // pack, narrow)
+    some = some.transpose(1, 0, 2).reshape(1, depth // pack, pack * narrow)
+    bit = 1
+    while bit < seq_count:
+        some = natural(some, "seq", bit, 0)
+        bit *= 2
+    some = some.reshape(seq_count, depth // pack, pack, narrow).transpose(0, 2, 1, 3)
+    bc_own = dot(own, some.reshape(-1, narrow)).astype(BF16)
+    bit = 1
+    while bit < head_count:
+        bc_own = natural(bc_own, "head", bit, 1)
+        bit *= 2
+    bc_other = swapped(bc_own[2 * HALO :], "seq", PAIR)
 
     logdec = -decay_code.astype(F32) / (16.0 * rows * seq_count)
     ld_own = cut(logdec, half, heads, 1)
@@ -257,24 +287,38 @@
     block_decay = jnp.repeat(jnp.exp(ends), head_dim, axis=3)
     cum = cum.reshape(2, rows, heads)
     grown = jnp.repeat(jnp.exp(cum), head_dim, axis=2)
-    totals = lax.all_gather(jnp.sum(logdec, axis=0), "seq", axis=0)
-    totals = cut(totals, half, heads, 1)
-    places = jnp.arange(seq_count)
+    totals = jnp.sum(ld, axis=1)
+    masks = [0, PAIR]
+    bit = 1
+    while bit < seq_count:
+        if bit != PAIR:
+            totals = jnp.concatenate([totals, swapped(totals, "seq", bit)])
+            masks = masks + [m | bit for m in masks]
+        bit *= 2
+    places = me ^ jnp.array(masks, jnp.int32)
 
     def decay_between(low, high):
         chosen = jnp.where((places >= low) & (places < high), 1.0, 0.0)[:, None]
         return jnp.repeat(jnp.exp(jnp.sum(chosen * totals, axis=0)), head_dim)[None, :]
 
-    def project(ext, pieces):
+    def own_part(mask):
+        return cut(own, me ^ mask, depth, 1)
+
+    def other_part(mask):
+        start = (me ^ mask) * depth
+        return lax.dynamic_slice(others, (start // share ^ mine, 0, start % share), (1, rows, depth))[0]
+
+    def project(pieces, part):
         total = None
         for mask, piece in pieces.items():
-            term = dot(cut(ext, me ^ mask, depth, 1), piece)
+            term = dot(part(mask), piece)
             total = term if total is None else total + term
         return total.astype(BF16)
 
-    x_pre = jnp.stack([project(ext_own, x_pieces), project(ext_other, x_pieces)])
-    bc_pre = jnp.stack([dot(ext_own, w_bc_all).astype(BF16), dot(ext_other, w_bc_all).astype(BF16)])
-    z_val = jnp.stack([project(tokens, z_pieces), project(ext_other[HALO:], z_pieces)])
+    x_own = project(x_pieces, own_part)
+    x_other = project(x_pieces, other_part)
+    z_own = project(z_pieces, lambda mask: own_part(mask)[2 * HALO :])
+    z_other = project(z_pieces, other_part)
 
     ranges = [me, me ^ PAIR]
     first = jnp.stack([(r == 0).astype(jnp.int32) for r in ranges])
@@ -284,8 +328,10 @@
 
     x_conv, bc_conv, added = front(
         first,
-        x_pre,
-        bc_pre,
+        x_own,
+        x_other,
+        bc_own,
+        bc_other,
         padded(cut(tail_x, half, chans, 1)),
         padded(tail_bc),
         cut(conv_x, half, chans, 1),
@@ -334,7 +380,7 @@
         jnp.stack(states, axis=1),
         grown,
         jnp.repeat(cut(skip_gain, half, heads, 0), head_dim)[None, :],
-        z_val,
+        jnp.stack([z_own, z_other]),
         cut(norm_gain, half, chans, 0)[None, :],
     )
 
@@ -346,35 +392,40 @@
     scale = lax.rsqrt(squares / inner + 1e-05)[:, None]
 
     per = seq_count // head_count
-    stacked = jnp.stack([out_pieces[mask] for mask in range(seq_count)])
-
-    def columns(relative):
-        base_piece = (mine ^ relative) * per
-        return [lax.dynamic_index_in_dim(stacked, me ^ (base_piece + j), 0, keepdims=False) for j in range(per)]
-
-    near = jnp.concatenate([c for r in range(0, head_count, 2) for c in columns(r)], axis=1)
-    far = jnp.concatenate([c for r in range(1, head_count, 2) for c in columns(r)], axis=1)
+    relation = (me // per) ^ mine
+
+    def by_destination(low):
+        return by_xor([out_pieces[q * per + low] for q in range(head_count)], relation)
+
+    def fold_head(parts):
+        bit = 1
+        while bit < head_count:
+            for r in list(parts):
+                if r & bit:
+                    got = swapped(parts.pop(r).astype(BF16), "head", bit)
+                    parts[r ^ bit] = parts[r ^ bit] + got.astype(F32)
+            bit *= 2
+        return parts[0]
+
+    def fold_core(weights, value):
+        sent = {r: swapped(dot(value, w).astype(BF16), "head", 1) for r, w in enumerate(weights) if r & 1}
+        return {r: dot(value, w) + sent[r | 1].astype(F32) for r, w in enumerate(weights) if not r & 1}
+
+    def fold_pair(mine_part, other_part):
+        return mine_part + swapped(other_part.astype(BF16), "seq", PAIR).astype(F32)
+
     flat = gated.reshape(2 * rows, chans)
-    received = swapped(dot(flat, far).astype(BF16), "head", 1)
-    sums = dot(flat, near) + received.astype(F32)
-    sums = sums.reshape(2, rows, head_count // 2, -1)
-
-    def fold_head(value):
-        count = value.shape[2]
-        while count > 1:
-            count //= 2
-            got = swapped(value[:, :, count:].astype(BF16), "head", 2 * count)
-            value = value[:, :, :count] + got.astype(F32)
-        return value
-
-    def fold_pair(value):
-        return value[:1] + swapped(value[1:].astype(BF16), "seq", PAIR).astype(F32)
-
-    width = sums.shape[3] // 2
-    left = fold_pair(fold_head(sums[..., :width]))
-    right = fold_head(fold_pair(sums[..., width:]))
-    result = jnp.concatenate([left, right], axis=3).reshape(rows, 2 * width)
-    return (result * scale).astype(BF16)
+    done = {}
+    for low in range(0, per, 2):
+        whole = fold_head(fold_core(by_destination(low), flat))
+        done[low] = fold_pair(whole[:rows], whole[rows:])
+    for low in range(1, per, 2):
+        weights = by_destination(low)
+        away = fold_core(weights, gated[1])
+        here = fold_core(weights, gated[0])
+        done[low] = fold_head({r: fold_pair(here[r], away[r]) for r in here})
+    result = by_xor([done[low] for low in range(per)], me % per)
+    return jnp.concatenate([(piece * scale).astype(BF16) for piece in result], axis=1)
 
 
 def solution(mesh):

time: 408 us -> 334 us (0.82); the launches traced: 401 us -> 333 us
  local copies, waits for them, and re-layouts: 64.4 us -> 27.4 us
  blocking collectives: 29.9 us -> 0 us
  waiting for transfers between devices: 154 us -> 179 us
  starting transfers between devices: 74.9 us -> 54.7 us
  between operations: 15.9 us -> 1.57 us
  other arithmetic: 6.38 us -> 10.5 us
    unnamed x1 -> x0, blocking collectives: 29.9 us -> none
    ppermute x32 -> x50, waiting for transfers between devices: 151 us -> 176 us  [swapped(): return lax.ppermute(value, axis, [(i, i ^ bit) for i in range(size)])]
    ppermute x32 -> x50, starting transfers between devices: 71 us -> 50.8 us  [swapped(): return lax.ppermute(value, axis, [(i, i ^ bit) for i in range(size)])]
    slice x7 -> x4, local copies, waits for them, and re-layouts: 14 us -> 0.42 us  [the longest x1 0.17 us: local(): x_w, z_w = (flat_w[:, :full], flat_w[:, full:])]
    reshape x2, local copies, waits for them, and re-layouts: 14.4 us -> 1.3 us  [the longest x1 1.18 us: local(): bc_own = dot(own, some.reshape(-1, narrow)).astype(BF16)]
    unnamed x109 -> x75, local copies, waits for them, and re-layouts: 11.4 us -> 3.85 us
    dynamic_slice x10 -> x11, local copies, waits for them, and re-layouts: 11.5 us -> 5.87 us  [cut(): return lax.dynamic_slice_in_dim(value, index * size, size, axis)]
    dot_general x36 -> x45, matrix products: 44.1 us -> 47.8 us  [dot(): return jnp.dot(a, b, preferred_element_type=F32)]
  transfers between devices with their start and end apart: 36 -> 52, of which waited for: 16 -> 25; matrix products, arithmetic and copies ran while one was open for 16% -> 24% of each run, Pallas kernels for 1% -> 1%
where the time goes in v2:
time: 334 us; the launch traced here: 333 us
  waiting for transfers between devices  179 us (54%)
  starting transfers between devices  54.7 us (16%)
  matrix products  47.8 us (14%)
  local copies, waits for them, and re-layouts  27.4 us (8%)
  Pallas kernels  12.2 us (4%)
  other arithmetic  10.5 us (3%)
    ppermute x50, waiting for transfers between devices, swapped(): return lax.ppermute(value, axis, [(i, i ^ bit) for i in range(size)])  176 us
    ppermute x50, starting transfers between devices, swapped(): return lax.ppermute(value, axis, [(i, i ^ bit) for i in range(size)])  50.8 us
    dot_general x45, matrix products, dot(): return jnp.dot(a, b, preferred_element_type=F32)  47.8 us
  transfers between devices with their start and end apart: 52, of which 25 were waited for; matrix products, arithmetic and copies ran while one was open for 24% of the time, Pallas kernels for 1%

profile of v2, /device:TPU:0, one launch (start us, length us, event | category | flops | bytes accessed | tf_op | source)
XLA Modules:
  0.0 332.7 jit_solution(1959376093104446815)
XLA Ops:
  3.6 4.0 %collective-permute-start.3 = (bf16[512,512]{1,0:T(8,128)(2,1)}, bf16[512,512]{1,0:T(8,128)(2,1)}, u32[]{:S(2)}, u32[]{:S(2)}) collective-permute-start(bf16[512,512]{1,0:T(8,128)(2,1)} %get-tuple-element.58), channel_id=1, source_target_pairs={{0,16},{4,20},{8,24},{12,28},{16,0},{20,4},{24,8},{28,12},{1,17},{... | collective-permute-start | bytes 1572872 | tf_op jit(solution)/shard_map/ppermute | solution.py:20
  22.4 13.6 %collective-permute-done.19 = f32[512,8]{0,1:T(8,128)S(1)} collective-permute-done((f32[512,8]{0,1:T(8,128)S(1)}, f32[512,8]{0,1:T(8,128)S(1)}, u32[]{:S(2)}, u32[]{:S(2)}) %collective-permute-start.19) | collective-permute-done | bytes 16416 | tf_op jit(solution)/shard_map/ppermute | solution.py:20
  56.2 23.3 %collective-permute-done.14 = bf16[2,256,128]{1,2,0:T(8,128)(2,1)S(1)} collective-permute-done((bf16[2,256,128]{1,2,0:T(8,128)(2,1)S(1)}, bf16[2,256,128]{1,2,0:T(8,128)(2,1)S(1)}, u32[]{:S(2)}, u32[]{:S(2)}) %collective-permute-start.14) | collective-permute-done | bytes 131104 | tf_op jit(solution)/shard_map/ppermute | solution.py:20
  82.0 4.8 %collective-permute-done.1 = bf16[16,4096]{1,0:T(8,128)(2,1)S(1)} collective-permute-done((bf16[16,4096]{1,0:T(8,128)(2,1)S(1)}, bf16[16,4096]{1,0:T(8,128)(2,1)S(1)}, u32[]{:S(2)}, u32[]{:S(2)}) %collective-permute-start.1) | collective-permute-done | bytes 131104 | tf_op jit(solution)/shard_map/ppermute | solution.py:20
  87.8 4.7 %constant_dynamic-update-slice_fusion = bf16[544,4096]{1,0:T(8,128)(2,1)} fusion(bf16[544,4096]{1,0:T(8,128)(2,1)} %constant_dynamic-update-slice_fusion.1, bf16[512,4096]{1,0:T(8,128)(2,1)} %param.13), kind=kLoop, calls=%fused_computation.201 | loop fusion | bytes 8388608 | tf_op jit(solution)/shard_map/concatenate | solution.py:253
  92.5 4.3 %collective-permute-done.15 = bf16[4,256,128]{1,2,0:T(8,128)(2,1)S(1)} collective-permute-done((bf16[4,256,128]{1,2,0:T(8,128)(2,1)S(1)}, bf16[4,256,128]{1,2,0:T(8,128)(2,1)S(1)}, u32[]{:S(2)}, u32[]{:S(2)}) %collective-permute-start.15) | collective-permute-done | bytes 262176 | tf_op jit(solution)/shard_map/ppermute | solution.py:20
  99.8 3.7 %convolution_convert_fusion.6 = bf16[544,64]{1,0:T(8,128)(2,1)S(1)} fusion(bf16[544,4096]{1,0:T(8,128)(2,1)} %constant_dynamic-update-slice_fusion, bf16[4096,64]{0,1:T(8,128)(2,1)} %reshape.184), kind=kOutput, calls=%fused_computation.51 | convolution fusion | flops 285247488 | bytes 5050368 | tf_op jit(solution)/shard_map/dot_general | solution.py:69
  117.7 5.8 %collective-permute-done.6 = bf16[512,512]{1,0:T(8,128)(2,1)S(1)} collective-permute-done((bf16[512,512]{1,0:T(8,128)(2,1)}, bf16[512,512]{1,0:T(8,128)(2,1)S(1)}, u32[]{:S(2)}, u32[]{:S(2)}) %collective-permute-start.6) | collective-permute-done | bytes 524320 | tf_op jit(solution)/shard_map/ppermute | solution.py:20
  125.0 4.4 %collective-permute-done.24 = bf16[512,512]{1,0:T(8,128)(2,1)S(1)} collective-permute-done((bf16[512,512]{1,0:T(8,128)(2,1)S(1)}, bf16[512,512]{1,0:T(8,128)(2,1)S(1)}, u32[]{:S(2)}, u32[]{:S(2)}) %collective-permute-start.24) | collective-permute-done | bytes 524320 | tf_op jit(solution)/shard_map/ppermute | solution.py:20
  138.3 23.7 %collective-permute-done.4 = bf16[512,512]{1,0:T(8,128)(2,1)S(1)} collective-permute-done((bf16[512,512]{1,0:T(8,128)(2,1)}, bf16[512,512]{1,0:T(8,128)(2,1)S(1)}, u32[]{:S(2)}, u32[]{:S(2)}) %collective-permute-start.4) | collective-permute-done | bytes 524320 | tf_op jit(solution)/shard_map/ppermute | solution.py:20
  178.4 13.1 %collective-permute-done.31 = bf16[512,512]{1,0:T(8,128)(2,1)S(1)} collective-permute-done((bf16[512,512]{1,0:T(8,128)(2,1)S(1)}, bf16[512,512]{1,0:T(8,128)(2,1)S(1)}, u32[]{:S(2)}, u32[]{:S(2)}) %collective-permute-start.31) | collective-permute-done | bytes 524320 | tf_op jit(solution)/shard_map/ppermute | solution.py:20
  194.3 17.2 %collective-permute-done.34 = bf16[512,512]{1,0:T(8,128)(2,1)S(1)} collective-permute-done((bf16[512,512]{1,0:T(8,128)(2,1)S(1)}, bf16[512,512]{1,0:T(8,128)(2,1)S(1)}, u32[]{:S(2)}, u32[]{:S(2)}) %collective-permute-start.34) | collective-permute-done | bytes 524320 | tf_op jit(solution)/shard_map/ppermute | solution.py:20
  214.3 7.5 %collective-permute-done.32 = bf16[512,512]{1,0:T(8,128)(2,1)S(1)} collective-permute-done((bf16[512,512]{1,0:T(8,128)(2,1)S(1)}, bf16[512,512]{1,0:T(8,128)(2,1)S(1)}, u32[]{:S(2)}, u32[]{:S(2)}) %collective-permute-start.32) | collective-permute-done | bytes 524320 | tf_op jit(solution)/shard_map/ppermute | solution.py:20
  228.8 8.7 %collective-permute-done.35 = bf16[512,512]{1,0:T(8,128)(2,1)S(1)} collective-permute-done((bf16[512,512]{1,0:T(8,128)(2,1)S(1)}, bf16[512,512]{1,0:T(8,128)(2,1)S(1)}, u32[]{:S(2)}, u32[]{:S(2)}) %collective-permute-start.35) | collective-permute-done | bytes 524320 | tf_op jit(solution)/shard_map/ppermute | solution.py:20
  237.5 10.8 %collective-permute-done.33 = bf16[512,512]{1,0:T(8,128)(2,1)S(1)} collective-permute-done((bf16[512,512]{1,0:T(8,128)(2,1)S(1)}, bf16[512,512]{1,0:T(8,128)(2,1)S(1)}, u32[]{:S(2)}, u32[]{:S(2)}) %collective-permute-start.33) | collective-permute-done | bytes 524320 | tf_op jit(solution)/shard_map/ppermute | solution.py:20
  258.0 4.9 %front.1 = (bf16[2,512,512]{2,1,0:T(8,128)(2,1)S(1)}, bf16[2,512,256]{2,1,0:T(8,128)(2,1)S(1)}, f32[2,2,128,512]{3,2,1,0:T(8,128)S(1)}) custom-call(s32[2]{0:T(128)S(1)} %add_convert_fusion.2.first_ref, bf16[544,512]{1,0:T(8,128)(2,1)S(1)} %fusion.13.xo_ref, bf16[512,512]{1,0:T(8,128)(2,1)S(1)} %fusion.15.xp_ref, ...), custom_call_target="tpu_custom_call" | custom-call | tf_op jit(solution)/shard_map/front/pallas_call | solution.py:151
  267.0 2.9 intra.1.y_ref
  275.7 4.4 %gate.1 = (bf16[2,512,512]{2,1,0:T(8,128)(2,1)S(1)}, f32[2,512,128]{2,1,0:T(8,128)S(1)}) custom-call(f32[2,512,512]{2,1,0:T(8,128)} %copy-done.2, bf16[2,512,512]{2,1,0:T(8,128)(2,1)S(1)} %get-tuple-element.16.x_ref, bf16[2,512,256]{2,1,0:T(8,128)(2,1)S(1)} %get-tuple-element.17.bc_ref, f32[2,2,128,512]{3,2,1,0:T(8,128)S(1)} %pad_maximum_fusion.1.st_ref, ...), custom_call_target="tpu_custom_call" | custom-call | tf_op jit(solution)/shard_map/gate/pallas_call | solution.py:195
  280.3 4.3 %collective-permute-start.49 = (f32[512]{0:T(512)S(1)}, f32[512]{0:T(512)S(1)}, u32[]{:S(2)}, u32[]{:S(2)}) collective-permute-start(f32[512]{0:T(512)S(1)} %get-tuple-element.27), channel_id=1, source_target_pairs={{0,8},{4,12},{8,0},{12,4},{16,24},{20,28},{24,16},{28,20},{1,9},{5... | collective-permute-start | bytes 6152 | tf_op jit(solution)/shard_map/ppermute | solution.py:20
  295.5 11.1 %collective-permute-done.43 = bf16[512,512]{0,1:T(8,128)(2,1)S(1)} collective-permute-done((bf16[512,512]{0,1:T(8,128)(2,1)S(1)}, bf16[512,512]{0,1:T(8,128)(2,1)S(1)}, u32[]{:S(2)}, u32[]{:S(2)}) %collective-permute-start.43) | collective-permute-done | bytes 524320 | tf_op jit(solution)/shard_map/ppermute | solution.py:20
  309.0 7.4 %collective-permute-done.47 = bf16[1024,512]{0,1:T(8,128)(2,1)S(1)} collective-permute-done((bf16[1024,512]{0,1:T(8,128)(2,1)S(1)}, bf16[1024,512]{0,1:T(8,128)(2,1)S(1)}, u32[]{:S(2)}, u32[]{:S(2)}) %collective-permute-start.47) | collective-permute-done | bytes 1048608 | tf_op jit(solution)/shard_map/ppermute | solution.py:20
  317.4 3.6 %collective-permute-done.40 = bf16[512,512]{0,1:T(8,128)(2,1)S(1)} collective-permute-done((bf16[512,512]{0,1:T(8,128)(2,1)S(1)}, bf16[512,512]{0,1:T(8,128)(2,1)S(1)}, u32[]{:S(2)}, u32[]{:S(2)}) %collective-permute-start.40) | collective-permute-done | bytes 524320 | tf_op jit(solution)/shard_map/ppermute | solution.py:20
  321.0 5.8 %collective-permute-done.44 = bf16[512,512]{0,1:T(8,128)(2,1)S(1)} collective-permute-done((bf16[512,512]{0,1:T(8,128)(2,1)S(1)}, bf16[512,512]{0,1:T(8,128)(2,1)S(1)}, u32[]{:S(2)}, u32[]{:S(2)}) %collective-permute-start.44) | collective-permute-done | bytes 524320 | tf_op jit(solution)/shard_map/ppermute | solution.py:20
  327.4 3.5 %collective-permute-done.48 = bf16[512,512]{0,1:T(8,128)(2,1)S(1)} collective-permute-done((bf16[512,512]{0,1:T(8,128)(2,1)S(1)}, bf16[512,512]{0,1:T(8,128)(2,1)S(1)}, u32[]{:S(2)}, u32[]{:S(2)}) %collective-permute-start.48) | collective-permute-done | bytes 524320 | tf_op jit(solution)/shard_map/ppermute | solution.py:20
  (324 shorter events, 133.7 us)
Async XLA Ops:
  3.6 100.0 %collective-permute-start.3 = (bf16[512,512]{1,0:T(8,128)(2,1)}, bf16[512,512]{1,0:T(8,128)(2,1)}, u32[]{:S(2)}, u32[]{:S(2)}) collective-permute-start(bf16[512,512]{1,0:T(8,128)(2,1)} %get-tuple-element.58), channel_id=1, source_target_pairs={{0,16},{4,20},{8,24},{12,28},{16,0},{20,4},{24,8},{28,12},{1,17},{... | collective-permute-start | bytes 1572872 | tf_op jit(solution)/shard_map/ppermute | solution.py:20
  7.6 102.1 %collective-permute-start.5 = (bf16[512,512]{1,0:T(8,128)(2,1)}, bf16[512,512]{1,0:T(8,128)(2,1)}, u32[]{:S(2)}, u32[]{:S(2)}) collective-permute-start(bf16[512,512]{1,0:T(8,128)(2,1)} %get-tuple-element.58), channel_id=1, source_target_pairs={{0,4},{4,0},{8,12},{12,8},{16,20},{20,16},{24,28},{28,24},{1,5},{5... | collective-permute-start | bytes 1572872 | tf_op jit(solution)/shard_map/ppermute | solution.py:20
  10.0 45.2 %collective-permute-start = (bf16[16,4096]{1,0:T(8,128)(2,1)S(1)}, bf16[16,4096]{1,0:T(8,128)(2,1)S(1)}, u32[]{:S(2)}, u32[]{:S(2)}) collective-permute-start(bf16[16,4096]{1,0:T(8,128)(2,1)S(1)} %slice.89), channel_id=1, source_target_pairs={{0,4},{4,8},{8,12},{12,16},{16,20},{20,24},{24,28},{1,5},{5,9},{9,... | collective-permute-start | bytes 393224 | tf_op jit(solution)/shard_map/ppermute | solution.py:25
  12.5 91.2 %collective-permute-start.2 = (bf16[512,512]{1,0:T(8,128)(2,1)}, bf16[512,512]{1,0:T(8,128)(2,1)}, u32[]{:S(2)}, u32[]{:S(2)}) collective-permute-start(bf16[512,512]{1,0:T(8,128)(2,1)} %get-tuple-element.57), channel_id=1, source_target_pairs={{0,8},{4,12},{8,0},{12,4},{16,24},{20,28},{24,16},{28,20},{1,9},{5... | collective-permute-start | bytes 1572872 | tf_op jit(solution)/shard_map/ppermute | solution.py:20
  53.1 84.2 %collective-permute-start.9 = (bf16[512,1024]{1,0:T(8,128)(2,1)}, bf16[512,1024]{1,0:T(8,128)(2,1)S(1)}, u32[]{:S(2)}, u32[]{:S(2)}) collective-permute-start(bf16[512,1024]{1,0:T(8,128)(2,1)} %constant_dynamic-slice_fusion.10), channel_id=1, source_target_pairs={{0,8},{4,12},{8,0},{12,4},{16,24},{20,28},{24,16},{28,20},{1,9},{5... | collective-permute-start | bytes 3145736 | tf_op jit(solution)/shard_map/ppermute | solution.py:20
  55.2 24.2 %collective-permute-start.14 = (bf16[2,256,128]{1,2,0:T(8,128)(2,1)S(1)}, bf16[2,256,128]{1,2,0:T(8,128)(2,1)S(1)}, u32[]{:S(2)}, u32[]{:S(2)}) collective-permute-start(bf16[2,256,128]{1,2,0:T(8,128)(2,1)S(1)} %maximum_select_fusion.3), channel_id=1, source_target_pairs={{0,8},{4,12},{8,0},{12,4},{16,24},{20,28},{24,16},{28,20},{1,9},{5... | collective-permute-start | bytes 393224 | tf_op jit(solution)/shard_map/ppermute | solution.py:20
  103.6 26.6 %collective-permute-start.25 = (bf16[512,512]{1,0:T(8,128)(2,1)S(1)}, bf16[512,512]{1,0:T(8,128)(2,1)S(1)}, u32[]{:S(2)}, u32[]{:S(2)}) collective-permute-start(bf16[512,512]{1,0:T(8,128)(2,1)S(1)} %copy-done.4), channel_id=1, source_target_pairs={{0,16},{4,20},{8,24},{12,28},{16,0},{20,4},{24,8},{28,12},{1,17},{... | collective-permute-start | bytes 1572872 | tf_op jit(solution)/shard_map/ppermute | solution.py:20
  103.7 25.7 %collective-permute-start.24 = (bf16[512,512]{1,0:T(8,128)(2,1)S(1)}, bf16[512,512]{1,0:T(8,128)(2,1)S(1)}, u32[]{:S(2)}, u32[]{:S(2)}) collective-permute-start(bf16[512,512]{1,0:T(8,128)(2,1)S(1)} %copy-done.21), channel_id=1, source_target_pairs={{0,8},{4,12},{8,0},{12,4},{16,24},{20,28},{24,16},{28,20},{1,9},{5... | collective-permute-start | bytes 1572872 | tf_op jit(solution)/shard_map/ppermute | solution.py:20
  123.5 38.5 %collective-permute-start.4 = (bf16[512,512]{1,0:T(8,128)(2,1)}, bf16[512,512]{1,0:T(8,128)(2,1)S(1)}, u32[]{:S(2)}, u32[]{:S(2)}) collective-permute-start(bf16[512,512]{1,0:T(8,128)(2,1)} %collective-permute-done.2), channel_id=1, source_target_pairs={{0,16},{4,20},{8,24},{12,28},{16,0},{20,4},{24,8},{28,12},{1,17},{... | collective-permute-start | bytes 1572872 | tf_op jit(solution)/shard_map/ppermute | solution.py:20
  129.4 40.7 %collective-permute-start.27 = (bf16[512,512]{1,0:T(8,128)(2,1)S(1)}, bf16[512,512]{1,0:T(8,128)(2,1)S(1)}, u32[]{:S(2)}, u32[]{:S(2)}) collective-permute-start(bf16[512,512]{1,0:T(8,128)(2,1)S(1)} %copy-done.4), channel_id=1, source_target_pairs={{0,4},{4,0},{8,12},{12,8},{16,20},{20,16},{24,28},{28,24},{1,5},{5... | collective-permute-start | bytes 1572872 | tf_op jit(solution)/shard_map/ppermute | solution.py:20
  130.3 43.0 %collective-permute-start.26 = (bf16[512,512]{1,0:T(8,128)(2,1)S(1)}, bf16[512,512]{1,0:T(8,128)(2,1)S(1)}, u32[]{:S(2)}, u32[]{:S(2)}) collective-permute-start(bf16[512,512]{1,0:T(8,128)(2,1)S(1)} %collective-permute-done.24), channel_id=1, source_target_pairs={{0,16},{4,20},{8,24},{12,28},{16,0},{20,4},{24,8},{28,12},{1,17},{... | collective-permute-start | bytes 1572872 | tf_op jit(solution)/shard_map/ppermute | solution.py:20
  134.7 41.2 %collective-permute-start.29 = (bf16[512,512]{1,0:T(8,128)(2,1)S(1)}, bf16[512,512]{1,0:T(8,128)(2,1)S(1)}, u32[]{:S(2)}, u32[]{:S(2)}) collective-permute-start(bf16[512,512]{1,0:T(8,128)(2,1)S(1)} %collective-permute-done.25), channel_id=1, source_target_pairs={{0,4},{4,0},{8,12},{12,8},{16,20},{20,16},{24,28},{28,24},{1,5},{5... | collective-permute-start | bytes 1572872 | tf_op jit(solution)/shard_map/ppermute | solution.py:20
  137.3 32.4 %collective-permute-start.28 = (bf16[512,512]{1,0:T(8,128)(2,1)S(1)}, bf16[512,512]{1,0:T(8,128)(2,1)S(1)}, u32[]{:S(2)}, u32[]{:S(2)}) collective-permute-start(bf16[512,512]{1,0:T(8,128)(2,1)S(1)} %collective-permute-done.24), channel_id=1, source_target_pairs={{0,4},{4,0},{8,12},{12,8},{16,20},{20,16},{24,28},{28,24},{1,5},{5... | collective-permute-start | bytes 1572872 | tf_op jit(solution)/shard_map/ppermute | solution.py:20
  162.0 50.6 %collective-permute-start.11 = (bf16[512,1024]{1,0:T(8,128)(2,1)S(1)}, bf16[512,1024]{1,0:T(8,128)(2,1)S(1)}, u32[]{:S(2)}, u32[]{:S(2)}) collective-permute-start(bf16[512,1024]{1,0:T(8,128)(2,1)S(1)} %collective-permute-done.9), channel_id=1, source_target_pairs={{0,2},{1,3},{2,0},{3,1},{4,6},{5,7},{6,4},{7,5},{8,10},{9,11},{10,... | collective-permute-start | bytes 3145736 | tf_op jit(solution)/shard_map/ppermute | solution.py:20
  173.3 38.2 %collective-permute-start.34 = (bf16[512,512]{1,0:T(8,128)(2,1)S(1)}, bf16[512,512]{1,0:T(8,128)(2,1)S(1)}, u32[]{:S(2)}, u32[]{:S(2)}) collective-permute-start(bf16[512,512]{1,0:T(8,128)(2,1)S(1)} %copy-done.16), channel_id=1, source_target_pairs={{0,16},{4,20},{8,24},{12,28},{16,0},{20,4},{24,8},{28,12},{1,17},{... | collective-permute-start | bytes 1572872 | tf_op jit(solution)/shard_map/ppermute | solution.py:20
  175.9 35.6 %collective-permute-start.30 = (bf16[512,512]{1,0:T(8,128)(2,1)S(1)}, bf16[512,512]{1,0:T(8,128)(2,1)S(1)}, u32[]{:S(2)}, u32[]{:S(2)}) collective-permute-start(bf16[512,512]{1,0:T(8,128)(2,1)S(1)} %collective-permute-done.26), channel_id=1, source_target_pairs={{0,4},{4,0},{8,12},{12,8},{16,20},{20,16},{24,28},{28,24},{1,5},{5... | collective-permute-start | bytes 1572872 | tf_op jit(solution)/shard_map/ppermute | solution.py:20
  191.6 30.2 %collective-permute-start.32 = (bf16[512,512]{1,0:T(8,128)(2,1)S(1)}, bf16[512,512]{1,0:T(8,128)(2,1)S(1)}, u32[]{:S(2)}, u32[]{:S(2)}) collective-permute-start(bf16[512,512]{1,0:T(8,128)(2,1)S(1)} %collective-permute-done.31), channel_id=1, source_target_pairs={{0,16},{4,20},{8,24},{12,28},{16,0},{20,4},{24,8},{28,12},{1,17},{... | collective-permute-start | bytes 1572872 | tf_op jit(solution)/shard_map/ppermute | solution.py:20
  191.6 31.2 %collective-permute-start.36 = (bf16[512,512]{1,0:T(8,128)(2,1)S(1)}, bf16[512,512]{1,0:T(8,128)(2,1)S(1)}, u32[]{:S(2)}, u32[]{:S(2)}) collective-permute-start(bf16[512,512]{1,0:T(8,128)(2,1)S(1)} %collective-permute-done.31), channel_id=1, source_target_pairs={{0,4},{4,0},{8,12},{12,8},{16,20},{20,16},{24,28},{28,24},{1,5},{5... | collective-permute-start | bytes 1572872 | tf_op jit(solution)/shard_map/ppermute | solution.py:20
  211.5 37.7 %collective-permute-start.10 = (bf16[512,1024]{1,0:T(8,128)(2,1)S(1)}, bf16[512,1024]{1,0:T(8,128)(2,1)S(1)}, u32[]{:S(2)}, u32[]{:S(2)}) collective-permute-start(bf16[512,1024]{1,0:T(8,128)(2,1)S(1)} %collective-permute-done.9), channel_id=1, source_target_pairs={{0,1},{1,0},{2,3},{3,2},{4,5},{5,4},{6,7},{7,6},{8,9},{9,8},{10,11... | collective-permute-start | bytes 3145736 | tf_op jit(solution)/shard_map/ppermute | solution.py:20
  212.6 36.6 %collective-permute-start.12 = (bf16[512,1024]{1,0:T(8,128)(2,1)S(1)}, bf16[512,1024]{1,0:T(8,128)(2,1)S(1)}, u32[]{:S(2)}, u32[]{:S(2)}) collective-permute-start(bf16[512,1024]{1,0:T(8,128)(2,1)S(1)} %collective-permute-done.11), channel_id=1, source_target_pairs={{0,1},{1,0},{2,3},{3,2},{4,5},{5,4},{6,7},{7,6},{8,9},{9,8},{10,11... | collective-permute-start | bytes 3145736 | tf_op jit(solution)/shard_map/ppermute | solution.py:20
  222.8 25.5 %collective-permute-start.33 = (bf16[512,512]{1,0:T(8,128)(2,1)S(1)}, bf16[512,512]{1,0:T(8,128)(2,1)S(1)}, u32[]{:S(2)}, u32[]{:S(2)}) collective-permute-start(bf16[512,512]{1,0:T(8,128)(2,1)S(1)} %collective-permute-done.32), channel_id=1, source_target_pairs={{0,4},{4,0},{8,12},{12,8},{16,20},{20,16},{24,28},{28,24},{1,5},{5... | collective-permute-start | bytes 1572872 | tf_op jit(solution)/shard_map/ppermute | solution.py:20
  227.6 30.4 %collective-permute-start.18 = (bf16[512,256]{1,0:T(8,128)(2,1)S(1)}, bf16[512,256]{1,0:T(8,128)(2,1)S(1)}, u32[]{:S(2)}, u32[]{:S(2)}) collective-permute-start(bf16[512,256]{1,0:T(8,128)(2,1)S(1)} %slice.119), channel_id=1, source_target_pairs={{0,8},{4,12},{8,0},{12,4},{16,24},{20,28},{24,16},{28,20},{1,9},{5... | collective-permute-start | bytes 786440 | tf_op jit(solution)/shard_map/ppermute | solution.py:20
  290.3 26.1 %collective-permute-start.47 = (bf16[1024,512]{0,1:T(8,128)(2,1)S(1)}, bf16[1024,512]{0,1:T(8,128)(2,1)S(1)}, u32[]{:S(2)}, u32[]{:S(2)}) collective-permute-start(bf16[1024,512]{0,1:T(8,128)(2,1)S(1)} %add_convert_fusion), channel_id=1, source_target_pairs={{0,2},{1,3},{2,0},{3,1},{4,6},{5,7},{6,4},{7,5},{8,10},{9,11},{10,... | collective-permute-start | bytes 3145736 | tf_op jit(solution)/shard_map/ppermute | solution.py:20
  293.2 24.3 %collective-permute-start.38 = (bf16[512,512]{0,1:T(8,128)(2,1)S(1)}, bf16[512,512]{0,1:T(8,128)(2,1)S(1)}, u32[]{:S(2)}, u32[]{:S(2)}) collective-permute-start(bf16[512,512]{0,1:T(8,128)(2,1)S(1)} %convolution_convert_fusion.5), channel_id=1, source_target_pairs={{0,1},{1,0},{2,3},{3,2},{4,5},{5,4},{6,7},{7,6},{8,9},{9,8},{10,11... | collective-permute-start | bytes 1572872 | tf_op jit(solution)/shard_map/ppermute | solution.py:20
  (64 other events, 732.4 us)

commit v3 on v2

--- a/solution.py
+++ b/solution.py
@@ -33,17 +33,19 @@
     return lax.optimization_barrier((value, *others))[0]
 
 
-def spread(own, other, seq_count, earlier=None):
+def spread(own, other, seq_count, gates):
     bits = [1 << b for b in range(seq_count.bit_length() - 1)]
     bits = [b for b in bits if b > PAIR] + [b for b in bits if b < PAIR]
-    if earlier is not None:
-        other = after(other, earlier[PAIR])
+    pair_gate, high_gate, low_gate = gates
+    if pair_gate is not None:
+        other = after(other, pair_gate)
     pieces = {0: own, PAIR: swapped(other, "seq", PAIR)}
     for bit in bits:
         for mask in list(pieces):
             value = pieces[mask]
-            if mask == 0 and earlier is not None:
-                value = after(value, earlier[bit] if bit > PAIR else earlier[PAIR | bit])
+            gate = high_gate if bit > PAIR else low_gate
+            if mask == 0 and gate is not None:
+                value = after(value, gate)
             pieces[mask | bit] = swapped(value, "seq", bit)
     return pieces
 
@@ -77,9 +79,9 @@
         is_first = first_ref[r] == 1
 
         def conv(own_ref, other_ref, tail_ref, k_ref):
-            halo = own_ref[r * HALO : (r + 1) * HALO].astype(F32)
+            halo = other_ref[r * HALO : (r + 1) * HALO].astype(F32)
             halo = jnp.where(is_first, tail_ref[...].astype(F32), halo)
-            body = (own_ref[2 * HALO :] if r == 0 else other_ref[...]).astype(F32)
+            body = (own_ref[...] if r == 0 else other_ref[2 * HALO :]).astype(F32)
             whole = jnp.concatenate([halo, body], axis=0)
             taps = k_ref.shape[0]
             total = jnp.zeros(body.shape, F32)
@@ -146,8 +148,8 @@
 
 
 def front(first, x_own, x_other, bc_own, bc_other, tail_x, tail_bc, conv_x, conv_bc, decay):
-    rows, chans = x_other.shape
-    bcw = bc_other.shape[1]
+    rows, chans = x_own.shape
+    bcw = bc_own.shape[1]
     return pl.pallas_call(
         front_kernel,
         in_specs=[pl.BlockSpec(memory_space=pltpu.SMEM)] + [pl.BlockSpec(memory_space=pltpu.VMEM)] * 9,
@@ -160,6 +162,31 @@
         compiler_params=pltpu.CompilerParams(vmem_limit_bytes=VMEM_LIMIT),
         name="front",
     )(first, x_own, x_other, bc_own, bc_other, tail_x, tail_bc, conv_x, conv_bc, decay)
+
+
+def project_kernel(place_ref, others_ref, *refs):
+    pieces, out_ref = refs[:-1], refs[-1]
+    depth = pieces[0].shape[0]
+    total = None
+    for k, piece in enumerate(pieces):
+        start = pl.multiple_of(place_ref[1, k], depth)
+        term = dot(others_ref[place_ref[0, k], :, pl.ds(start, depth)], piece[...])
+        total = term if total is None else total + term
+    out_ref[...] = total.astype(BF16)
+
+
+def project_others(places, others, pieces):
+    rows = others.shape[1]
+    chans = pieces[0].shape[1]
+    return pl.pallas_call(
+        project_kernel,
+        in_specs=[pl.BlockSpec(memory_space=pltpu.SMEM)]
+        + [pl.BlockSpec(memory_space=pltpu.VMEM)] * (1 + len(pieces)),
+        out_specs=pl.BlockSpec(memory_space=pltpu.VMEM),
+        out_shape=jax.ShapeDtypeStruct((rows, chans), BF16),
+        compiler_params=pltpu.CompilerParams(vmem_limit_bytes=VMEM_LIMIT),
+        name="project",
+    )(places, others, *pieces)
 
 
 def intra(x_conv, bc_conv, cum, cumt, heads):
@@ -241,58 +268,76 @@
     chans = heads * head_dim
     depth = w_xz.shape[0]
 
+    flat_w = lax.optimization_barrier(w_xz.reshape(depth, -1))
+    full = flat_w.shape[1] // 2
+    x_w, z_w = flat_w[:, :full], flat_w[:, full:]
+    high = max(b for b in (PAIR, seq_count // 2))
     share = tokens.shape[1] // head_count
     quarters = {0: swapped(cut(tokens, mine, share, 1), "seq", PAIR)}
-    before = shifted(tokens[rows - HALO :], "seq", 1)
-    before_other = swapped(before, "seq", PAIR)
+    x_pieces = spread(
+        cut(x_w, half, chans, 1), cut(x_w, 1 - half, chans, 1), seq_count, (None, None, None)
+    )
+    z_pieces = spread(
+        cut(z_w, half, chans, 1),
+        cut(z_w, 1 - half, chans, 1),
+        seq_count,
+        (quarters[0], x_pieces[high], x_pieces[PAIR | 1]),
+    )
+    out_pieces = spread(
+        cut(w_out, half, chans, 0),
+        cut(w_out, 1 - half, chans, 0),
+        seq_count,
+        (z_pieces[PAIR], z_pieces[high], z_pieces[PAIR | 1]),
+    )
+
     bit = head_count // 2
     while bit >= 1:
         for mask in list(quarters):
             quarters[mask | bit] = swapped(quarters[mask], "head", bit)
         bit //= 2
-    own = jnp.concatenate([before, before_other, tokens], axis=0)
-    others = jnp.stack([quarters[mask] for mask in range(head_count)])
-
-    flat_w = lax.optimization_barrier(w_xz.reshape(depth, -1))
-    full = flat_w.shape[1] // 2
-    x_w, z_w = flat_w[:, :full], flat_w[:, full:]
-    x_pieces = spread(cut(x_w, half, chans, 1), cut(x_w, 1 - half, chans, 1), seq_count)
-    z_pieces = spread(cut(z_w, half, chans, 1), cut(z_w, 1 - half, chans, 1), seq_count, x_pieces)
-    out_pieces = spread(cut(w_out, half, chans, 0), cut(w_out, 1 - half, chans, 0), seq_count, z_pieces)
+    before = shifted(tokens[rows - HALO :], "seq", 1)
+    before_other = swapped(after(before, x_pieces[PAIR]), "seq", PAIR)
+    halo = after(jnp.concatenate([before, before_other], axis=0), x_pieces[high])
+    others = jnp.stack(
+        [
+            jnp.concatenate([cut(halo, mine ^ mask, share, 1), quarters[mask]], axis=0)
+            for mask in range(head_count)
+        ]
+    )
 
     narrow = w_bc.shape[1] // head_count
     pack = max(1, 128 // narrow)
     some = cut(w_bc, mine, narrow, 1).reshape(pack, depth // pack, narrow)
-    some = some.transpose(1, 0, 2).reshape(1, depth // pack, pack * narrow)
-    bit = 1
-    while bit < seq_count:
-        some = natural(some, "seq", bit, 0)
-        bit *= 2
+    some = some.transpose(1, 0, 2).reshape(depth // pack, pack * narrow)
+    some = after(lax.all_gather(some, "seq", axis=0), x_pieces[high])
     some = some.reshape(seq_count, depth // pack, pack, narrow).transpose(0, 2, 1, 3)
-    bc_own = dot(own, some.reshape(-1, narrow)).astype(BF16)
+    some = some.reshape(-1, narrow)
+    bc_part = jnp.concatenate([dot(halo, some), dot(tokens, some)], axis=0).astype(BF16)
     bit = 1
     while bit < head_count:
-        bc_own = natural(bc_own, "head", bit, 1)
+        bc_part = natural(bc_part, "head", bit, 1)
         bit *= 2
-    bc_other = swapped(bc_own[2 * HALO :], "seq", PAIR)
-
-    logdec = -decay_code.astype(F32) / (16.0 * rows * seq_count)
-    ld_own = cut(logdec, half, heads, 1)
-    ld = jnp.stack([ld_own, swapped(cut(logdec, 1 - half, heads, 1), "seq", PAIR)])
+    bc_own = bc_part[2 * HALO :]
+    bc_other = jnp.concatenate([bc_part[: 2 * HALO], swapped(bc_own, "seq", PAIR)], axis=0)
+
+    logdec = -decay_code.T.astype(F32) / (16.0 * rows * seq_count)
+    ld_other = swapped(cut(logdec, 1 - half, heads, 0), "seq", PAIR)
+    ld = jnp.stack([cut(logdec, half, heads, 0), after(ld_other, x_pieces[PAIR])])
     blocks = rows // Q
-    cum = jnp.cumsum(ld.reshape(2, blocks, Q, heads), axis=2)
-    cumt = cum.transpose(0, 1, 3, 2)
+    cumt = jnp.cumsum(ld.reshape(2, heads, blocks, Q), axis=3).transpose(0, 2, 1, 3)
+    cum = cumt.transpose(0, 1, 3, 2)
     ends = cum[:, :, -1:, :]
     remaining = jnp.repeat(jnp.exp(ends - cum).reshape(2, rows, heads), head_dim, axis=2)
     block_decay = jnp.repeat(jnp.exp(ends), head_dim, axis=3)
     cum = cum.reshape(2, rows, heads)
     grown = jnp.repeat(jnp.exp(cum), head_dim, axis=2)
-    totals = jnp.sum(ld, axis=1)
+    totals = jnp.sum(ld, axis=2)
     masks = [0, PAIR]
     bit = 1
     while bit < seq_count:
         if bit != PAIR:
-            totals = jnp.concatenate([totals, swapped(totals, "seq", bit)])
+            got = after(swapped(totals, "seq", bit), x_pieces[high])
+            totals = jnp.concatenate([totals, got])
             masks = masks + [m | bit for m in masks]
         bit *= 2
     places = me ^ jnp.array(masks, jnp.int32)
@@ -302,11 +347,15 @@
         return jnp.repeat(jnp.exp(jnp.sum(chosen * totals, axis=0)), head_dim)[None, :]
 
     def own_part(mask):
-        return cut(own, me ^ mask, depth, 1)
+        return cut(tokens, me ^ mask, depth, 1)
+
+    def other_place(mask):
+        start = (me ^ mask) * depth
+        return start // share ^ mine, start % share
 
     def other_part(mask):
-        start = (me ^ mask) * depth
-        return lax.dynamic_slice(others, (start // share ^ mine, 0, start % share), (1, rows, depth))[0]
+        block, start = other_place(mask)
+        return lax.dynamic_slice(others, (block, 2 * HALO, start), (1, rows, depth))[0]
 
     def project(pieces, part):
         total = None
@@ -316,8 +365,10 @@
         return total.astype(BF16)
 
     x_own = project(x_pieces, own_part)
-    x_other = project(x_pieces, other_part)
-    z_own = project(z_pieces, lambda mask: own_part(mask)[2 * HALO :])
+    spots = [other_place(mask) for mask in x_pieces]
+    spots = jnp.stack([jnp.stack([jnp.int32(p[i]) for p in spots]) for i in range(2)])
+    x_other = project_others(spots, others, list(x_pieces.values()))
+    z_own = project(z_pieces, own_part)
     z_other = project(z_pieces, other_part)
 
     ranges = [me, me ^ PAIR]
@@ -384,46 +435,53 @@
         cut(norm_gain, half, chans, 0)[None, :],
     )
 
-    squares = squares[0, :, 0] + swapped(squares[1, :, 0], "seq", PAIR)
+    per = seq_count // head_count
+    relation = (me // per) ^ mine
+    flat = gated.reshape(2 * rows, chans)
+
+    def by_destination(low):
+        return by_xor([out_pieces[q * per + low] for q in range(head_count)], relation)
+
+    def send_far(weights):
+        far = jnp.concatenate(weights[1::2], axis=1)
+        return swapped(dot(flat, far).astype(BF16), "head", 1).astype(F32)
+
+    def fold_head(parts):
+        bit = 2
+        while len(parts) > 1:
+            sent = jnp.concatenate(parts[1::2], axis=1) if len(parts) > 2 else parts[1]
+            got = swapped(sent.astype(BF16), "head", bit).astype(F32)
+            parts = columns_added(parts[::2], got)
+            bit *= 2
+        return parts[0]
+
+    def columns_added(parts, got):
+        width = parts[0].shape[1]
+        return [part + got[:, i * width : (i + 1) * width] for i, part in enumerate(parts)]
+
+    def swap_pair(value):
+        return swapped(value.astype(BF16), "seq", PAIR).astype(F32)
+
+    done = {}
+    lows = {low: by_destination(low) for low in range(per)}
+    got_far = {low: send_far(lows[low]) for low in range(per)}
+    for low in range(0, per, 2):
+        parts = columns_added([dot(flat, w) for w in lows[low][::2]], got_far[low])
+        whole = fold_head(parts)
+        done[low] = whole[:rows] + swap_pair(whole[rows:])
+    for low in range(1, per, 2):
+        near = lows[low][::2]
+        away = swap_pair(dot(gated[1], jnp.concatenate(near, axis=1)) + got_far[low][rows:])
+        here = columns_added([dot(gated[0], w) for w in near], got_far[low][:rows])
+        done[low] = fold_head(columns_added(here, away))
+
+    squares = after(squares[:, :, 0], got_far[per - 1])
+    squares = squares[0] + swapped(squares[1], "seq", PAIR)
     bit = 1
     while bit < head_count:
         squares = squares + swapped(squares, "head", bit)
         bit *= 2
     scale = lax.rsqrt(squares / inner + 1e-05)[:, None]
-
-    per = seq_count // head_count
-    relation = (me // per) ^ mine
-
-    def by_destination(low):
-        return by_xor([out_pieces[q * per + low] for q in range(head_count)], relation)
-
-    def fold_head(parts):
-        bit = 1
-        while bit < head_count:
-            for r in list(parts):
-                if r & bit:
-                    got = swapped(parts.pop(r).astype(BF16), "head", bit)
-                    parts[r ^ bit] = parts[r ^ bit] + got.astype(F32)
-            bit *= 2
-        return parts[0]
-
-    def fold_core(weights, value):
-        sent = {r: swapped(dot(value, w).astype(BF16), "head", 1) for r, w in enumerate(weights) if r & 1}
-        return {r: dot(value, w) + sent[r | 1].astype(F32) for r, w in enumerate(weights) if not r & 1}
-
-    def fold_pair(mine_part, other_part):
-        return mine_part + swapped(other_part.astype(BF16), "seq", PAIR).astype(F32)
-
-    flat = gated.reshape(2 * rows, chans)
-    done = {}
-    for low in range(0, per, 2):
-        whole = fold_head(fold_core(by_destination(low), flat))
-        done[low] = fold_pair(whole[:rows], whole[rows:])
-    for low in range(1, per, 2):
-        weights = by_destination(low)
-        away = fold_core(weights, gated[1])
-        here = fold_core(weights, gated[0])
-        done[low] = fold_head({r: fold_pair(here[r], away[r]) for r in here})
     result = by_xor([done[low] for low in range(per)], me % per)
     return jnp.concatenate([(piece * scale).astype(BF16) for piece in result], axis=1)
 

time: 334 us -> 358 us (1.072)
  blocking collectives: 0 us -> 65.5 us
  waiting for transfers between devices: 179 us -> 115 us
  other arithmetic: 10.5 us -> 21.8 us
  local copies, waits for them, and re-layouts: 27.4 us -> 38.4 us
  Pallas kernels: 12.2 us -> 17.1 us
  matrix products: 47.8 us -> 43.4 us
    all_gather x0 -> x1, blocking collectives: none -> 65.5 us  [local(): some = after(lax.all_gather(some, 'seq', axis=0), x_pieces[high])]
    ppermute x50 -> x42, waiting for transfers between devices: 176 us -> 114 us  [swapped(): return lax.ppermute(value, axis, [(i, i ^ bit) for i in range(size)])]
    concatenate x4 -> x0, local copies, waits for them, and re-layouts: 5.15 us -> none  [the longest x1 4.67 us: local(): own = jnp.concatenate([before, before_other, tokens], axis=0)]
    pallas_call x0 -> x1, Pallas kernels: none -> 4.86 us  [project_others(): pl.pallas_call(project_kernel, in_specs=[pl.BlockSpec(memory_space=pltpu....]
    exp x8, local copies, waits for them, and re-layouts: 0.03 us -> 4.5 us  [decay_between(): jnp.exp(jnp.sum(chosen * totals, axis=0))]
    dot_general x45 -> x33, matrix products: 47.8 us -> 43.4 us  [dot(): return jnp.dot(a, b, preferred_element_type=F32)]
    ppermute x50 -> x42, starting transfers between devices: 50.8 us -> 50.9 us  [swapped(): return lax.ppermute(value, axis, [(i, i ^ bit) for i in range(size)])]
  transfers between devices with their start and end apart: 52 -> 44, of which waited for: 25 -> 16; matrix products, arithmetic and copies ran while one was open for 24% -> 26% of each run, Pallas kernels for 1% -> 4%
where the time goes in v3:
time: 358 us; the launch traced here: 357 us
  waiting for transfers between devices  115 us (32%)
  blocking collectives  65.5 us (18%)
  starting transfers between devices  54.3 us (15%)
  matrix products  43.4 us (12%)
  local copies, waits for them, and re-layouts  38.4 us (11%)
  other arithmetic  21.8 us (6%)
  Pallas kernels  17.1 us (5%)
    ppermute x42, waiting for transfers between devices, swapped(): return lax.ppermute(value, axis, [(i, i ^ bit) for i in range(size)])  114 us
    all_gather x1, blocking collectives, local(): some = after(lax.all_gather(some, 'seq', axis=0), x_pieces[high])  65.5 us
    ppermute x42, starting transfers between devices, swapped(): return lax.ppermute(value, axis, [(i, i ^ bit) for i in range(size)])  50.9 us
    dot_general x33, matrix products, dot(): return jnp.dot(a, b, preferred_element_type=F32)  43.4 us
  transfers between devices with their start and end apart: 44, of which 16 were waited for; matrix products, arithmetic and copies ran while one was open for 26% of the time, Pallas kernels for 4%

profile of v3, /device:TPU:0, one launch (start us, length us, event | category | flops | bytes accessed | tf_op | source)
XLA Modules:
  0.0 357.2 jit_solution(10145437291591984933)
XLA Ops:
  5.5 4.0 %collective-permute-start.1 = (bf16[512,512]{1,0:T(8,128)(2,1)S(1)}, bf16[512,512]{1,0:T(8,128)(2,1)S(1)}, u32[]{:S(2)}, u32[]{:S(2)}) collective-permute-start(bf16[512,512]{1,0:T(8,128)(2,1)S(1)} %get-tuple-element.68.refs_0_), channel_id=1, source_target_pairs={{0,16},{4,20},{8,24},{12,28},{16,0},{20,4},{24,8},{28,12},{1,17},{... | collective-permute-start | bytes 1572872 | tf_op jit(solution)/shard_map/ppermute | solution.py:20
  18.4 65.5 %all_gather.3 = bf16[8,256,128]{2,1,0:T(8,128)(2,1)S(1)} all-gather(bf16[1,256,128]{2,1,0:T(8,128)(2,1)S(1)} %copy.126), channel_id=1, replica_groups=mesh['seq'=8,'head'=4] {'seq'}, dimensions={0}, use_global_device_ids=true | all-gather | bytes 589824 | tf_op jit(solution)/shard_map/all_gather | solution.py:312
  83.9 2.5 fusion.79
  88.7 2.6 fusion.77
  100.3 3.3 collective-permute-start.8
  105.9 3.0 convolution_add_fusion.16
  108.8 3.6 %convolution_convert_fusion.2 = bf16[64,512]{1,0:T(8,128)(2,1)S(1)} fusion(bf16[4096,64]{0,1:T(8,128)(2,1)S(1)} %reshape.168, bf16[512,4096]{1,0:T(8,128)(2,1)} %param.13), kind=kOutput, calls=%fused_computation.41 | convolution fusion | flops 268468224 | bytes 4784128 | tf_op jit(solution)/shard_map/dot_general | solution.py:71
  113.3 2.8 convolution_add_fusion.15
  120.2 3.0 copy.135.dec_ref
  126.2 2.9 copy.142.e_ref
  164.7 9.2 %collective-permute-done.15 = bf16[512,256]{1,0:T(8,128)(2,1)S(1)} collective-permute-done((bf16[512,256]{1,0:T(8,128)(2,1)S(1)}, bf16[512,256]{1,0:T(8,128)(2,1)S(1)}, u32[]{:S(2)}, u32[]{:S(2)}) %collective-permute-start.15) | collective-permute-done | bytes 262176 | tf_op jit(solution)/shard_map/ppermute | solution.py:20
  175.0 8.1 %collective-permute-done.21 = bf16[512,512]{1,0:T(8,128)(2,1)S(1)} collective-permute-done((bf16[512,512]{1,0:T(8,128)(2,1)}, bf16[512,512]{1,0:T(8,128)(2,1)S(1)}, u32[]{:S(2)}, u32[]{:S(2)}) %collective-permute-start.21) | collective-permute-done | bytes 524320 | tf_op jit(solution)/shard_map/ppermute | solution.py:20
  191.6 20.7 %collective-permute-done.23 = bf16[512,512]{1,0:T(8,128)(2,1)S(1)} collective-permute-done((bf16[512,512]{1,0:T(8,128)(2,1)S(1)}, bf16[512,512]{1,0:T(8,128)(2,1)S(1)}, u32[]{:S(2)}, u32[]{:S(2)}) %collective-permute-start.23) | collective-permute-done | bytes 524320 | tf_op jit(solution)/shard_map/ppermute | solution.py:20
  215.6 11.6 %collective-permute-done.25 = bf16[512,512]{1,0:T(8,128)(2,1)S(1)} collective-permute-done((bf16[512,512]{1,0:T(8,128)(2,1)S(1)}, bf16[512,512]{1,0:T(8,128)(2,1)S(1)}, u32[]{:S(2)}, u32[]{:S(2)}) %collective-permute-start.25) | collective-permute-done | bytes 524320 | tf_op jit(solution)/shard_map/ppermute | solution.py:20
  229.8 8.6 %collective-permute-done.27 = bf16[512,512]{1,0:T(8,128)(2,1)S(1)} collective-permute-done((bf16[512,512]{1,0:T(8,128)(2,1)S(1)}, bf16[512,512]{1,0:T(8,128)(2,1)S(1)}, u32[]{:S(2)}, u32[]{:S(2)}) %collective-permute-start.27) | collective-permute-done | bytes 524320 | tf_op jit(solution)/shard_map/ppermute | solution.py:20
  246.7 4.9 %project.1.xp_ref = bf16[544,512]{1,0:T(8,128)(2,1)S(1)} custom-call(s32[2,8]{1,0:T(2,128)S(1)} %pad_add_fusion.place_ref, bf16[4,544,1024]{2,1,0:T(8,128)(2,1)} %pad_maximum_fusion.others_ref, bf16[512,512]{1,0:T(8,128)(2,1)S(1)} %get-tuple-element.68.refs_0_, bf16[512,512]{1,0:T(8,128)(2,1)} %collective-permute-done.refs_1_, ...), custom_call_target="tpu_custom_call" | custom-call | tf_op jit(solution)/shard_map/project/pallas_call | solution.py:181
  251.6 5.0 %front.1 = (bf16[2,512,512]{2,1,0:T(8,128)(2,1)S(1)}, bf16[2,512,256]{2,1,0:T(8,128)(2,1)S(1)}, f32[2,2,128,512]{3,2,1,0:T(8,128)S(1)}) custom-call(s32[2]{0:T(128)S(1)} %add_convert_fusion.1.first_ref, bf16[512,512]{1,0:T(8,128)(2,1)S(1)} %fusion.13.xo_ref, bf16[544,512]{1,0:T(8,128)(2,1)S(1)} %project.1.xp_ref, bf16[512,256]{1,0:T(8,128)(2,1)S(1)} %slice.127.bo_ref, ...), custom_call_target="tpu_custom_call" | custom-call | tf_op jit(solution)/shard_map/front/pallas_call | solution.py:153
  258.9 2.9 intra.1.y_ref
  268.5 19.1 %collective-permute-done.19 = bf16[2,128,512]{2,1,0:T(8,128)(2,1)S(1)} collective-permute-done((bf16[2,128,512]{2,1,0:T(8,128)(2,1)S(1)}, bf16[2,128,512]{2,1,0:T(8,128)(2,1)S(1)}, u32[]{:S(2)}, u32[]{:S(2)}) %collective-permute-start.19) | collective-permute-done | bytes 262176 | tf_op jit(solution)/shard_map/ppermute | solution.py:20
  292.5 4.3 %gate.1 = (bf16[2,512,512]{2,1,0:T(8,128)(2,1)S(1)}, f32[2,512,128]{2,1,0:T(8,128)S(1)}) custom-call(f32[2,512,512]{2,1,0:T(8,128)} %copy-done.2, bf16[2,512,512]{2,1,0:T(8,128)(2,1)S(1)} %get-tuple-element.27.x_ref, bf16[2,512,256]{2,1,0:T(8,128)(2,1)S(1)} %get-tuple-element.28.bc_ref, f32[2,2,128,512]{3,2,1,0:T(8,128)S(1)} %pad_maximum_fusion.1.st_ref, ...), custom_call_target="tpu_custom_call" | custom-call | tf_op jit(solution)/shard_map/gate/pallas_call | solution.py:222
  305.0 4.2 %collective-permute-start.36 = (bf16[512,1024]{0,1:T(8,128)(2,1)}, bf16[512,1024]{0,1:T(8,128)(2,1)}, u32[]{:S(2)}, u32[]{:S(2)}) collective-permute-start(bf16[512,1024]{0,1:T(8,128)(2,1)} %fusion.2), channel_id=1, source_target_pairs={{0,8},{4,12},{8,0},{12,4},{16,24},{20,28},{24,16},{28,20},{1,9},{5... | collective-permute-start | bytes 3145736 | tf_op jit(solution)/shard_map/ppermute | solution.py:20
  314.6 18.4 %collective-permute-done.41 = f32[512]{0:T(512)S(1)} collective-permute-done((f32[512]{0:T(512)S(1)}, f32[512]{0:T(512)S(1)}, u32[]{:S(2)}, u32[]{:S(2)}) %collective-permute-start.41) | collective-permute-done | bytes 2080 | tf_op jit(solution)/shard_map/ppermute | solution.py:20
  340.8 3.0 collective-permute-start.40
  343.8 8.1 %collective-permute-done.37 = bf16[512,512]{0,1:T(8,128)(2,1)S(1)} collective-permute-done((bf16[512,512]{0,1:T(8,128)(2,1)S(1)}, bf16[512,512]{0,1:T(8,128)(2,1)S(1)}, u32[]{:S(2)}, u32[]{:S(2)}) %collective-permute-start.37) | collective-permute-done | bytes 524320 | tf_op jit(solution)/shard_map/ppermute | solution.py:20
  (336 shorter events, 134.1 us)
Async XLA Ops:
  5.5 93.8 %collective-permute-start.1 = (bf16[512,512]{1,0:T(8,128)(2,1)S(1)}, bf16[512,512]{1,0:T(8,128)(2,1)S(1)}, u32[]{:S(2)}, u32[]{:S(2)}) collective-permute-start(bf16[512,512]{1,0:T(8,128)(2,1)S(1)} %get-tuple-element.68.refs_0_), channel_id=1, source_target_pairs={{0,16},{4,20},{8,24},{12,28},{16,0},{20,4},{24,8},{28,12},{1,17},{... | collective-permute-start | bytes 1572872 | tf_op jit(solution)/shard_map/ppermute | solution.py:20
  9.5 106.6 %collective-permute-start.3 = (bf16[512,512]{1,0:T(8,128)(2,1)S(1)}, bf16[512,512]{1,0:T(8,128)(2,1)S(1)}, u32[]{:S(2)}, u32[]{:S(2)}) collective-permute-start(bf16[512,512]{1,0:T(8,128)(2,1)S(1)} %get-tuple-element.68.refs_0_), channel_id=1, source_target_pairs={{0,4},{4,0},{8,12},{12,8},{16,20},{20,16},{24,28},{28,24},{1,5},{5... | collective-permute-start | bytes 1572872 | tf_op jit(solution)/shard_map/ppermute | solution.py:20
  13.3 140.0 %collective-permute-start.9 = (bf16[512,1024]{1,0:T(8,128)(2,1)}, bf16[512,1024]{1,0:T(8,128)(2,1)}, u32[]{:S(2)}, u32[]{:S(2)}) collective-permute-start(bf16[512,1024]{1,0:T(8,128)(2,1)} %constant_dynamic-slice_fusion.12), channel_id=1, source_target_pairs={{0,8},{4,12},{8,0},{12,4},{16,24},{20,28},{24,16},{28,20},{1,9},{5... | collective-permute-start | bytes 3145736 | tf_op jit(solution)/shard_map/ppermute | solution.py:20
  14.8 80.8 %collective-permute-start = (bf16[512,512]{1,0:T(8,128)(2,1)}, bf16[512,512]{1,0:T(8,128)(2,1)}, u32[]{:S(2)}, u32[]{:S(2)}) collective-permute-start(bf16[512,512]{1,0:T(8,128)(2,1)} %get-tuple-element.67), channel_id=1, source_target_pairs={{0,8},{4,12},{8,0},{12,4},{16,24},{20,28},{24,16},{28,20},{1,9},{5... | collective-permute-start | bytes 1572872 | tf_op jit(solution)/shard_map/ppermute | solution.py:20
  15.3 78.4 %collective-permute-start.16 = (f32[8,512]{1,0:T(8,128)S(1)}, f32[8,512]{1,0:T(8,128)S(1)}, u32[]{:S(2)}, u32[]{:S(2)}) collective-permute-start(f32[8,512]{1,0:T(8,128)S(1)} %get-tuple-element.83), channel_id=1, source_target_pairs={{0,8},{4,12},{8,0},{12,4},{16,24},{20,28},{24,16},{28,20},{1,9},{5... | collective-permute-start | bytes 49160 | tf_op jit(solution)/shard_map/ppermute | solution.py:20
  99.3 56.1 %collective-permute-start.22 = (bf16[512,512]{1,0:T(8,128)(2,1)}, bf16[512,512]{1,0:T(8,128)(2,1)}, u32[]{:S(2)}, u32[]{:S(2)}) collective-permute-start(bf16[512,512]{1,0:T(8,128)(2,1)} %get-tuple-element.34), channel_id=1, source_target_pairs={{0,16},{4,20},{8,24},{12,28},{16,0},{20,4},{24,8},{28,12},{1,17},{... | collective-permute-start | bytes 1572872 | tf_op jit(solution)/shard_map/ppermute | solution.py:20
  100.3 32.1 %collective-permute-start.8 = (bf16[16,4096]{1,0:T(8,128)(2,1)S(1)}, bf16[16,4096]{1,0:T(8,128)(2,1)}, u32[]{:S(2)}, u32[]{:S(2)}) collective-permute-start(bf16[16,4096]{1,0:T(8,128)(2,1)S(1)} %collective-permute-done.7), channel_id=1, source_target_pairs={{0,8},{4,12},{8,0},{12,4},{16,24},{20,28},{24,16},{28,20},{1,9},{5... | collective-permute-start | bytes 393224 | tf_op jit(solution)/shard_map/ppermute | solution.py:20
  131.2 25.3 %collective-permute-start.2 = (bf16[512,512]{1,0:T(8,128)(2,1)}, bf16[512,512]{1,0:T(8,128)(2,1)S(1)}, u32[]{:S(2)}, u32[]{:S(2)}) collective-permute-start(bf16[512,512]{1,0:T(8,128)(2,1)} %collective-permute-done.refs_1_), channel_id=1, source_target_pairs={{0,16},{4,20},{8,24},{12,28},{16,0},{20,4},{24,8},{28,12},{1,17},{... | collective-permute-start | bytes 1572872 | tf_op jit(solution)/shard_map/ppermute | solution.py:20
  154.4 28.7 %collective-permute-start.21 = (bf16[512,512]{1,0:T(8,128)(2,1)}, bf16[512,512]{1,0:T(8,128)(2,1)S(1)}, u32[]{:S(2)}, u32[]{:S(2)}) collective-permute-start(bf16[512,512]{1,0:T(8,128)(2,1)} %get-tuple-element.32), channel_id=1, source_target_pairs={{0,8},{4,12},{8,0},{12,4},{16,24},{20,28},{24,16},{28,20},{1,9},{5... | collective-permute-start | bytes 1572872 | tf_op jit(solution)/shard_map/ppermute | solution.py:20
  155.4 30.3 %collective-permute-start.24 = (bf16[512,512]{1,0:T(8,128)(2,1)}, bf16[512,512]{1,0:T(8,128)(2,1)S(1)}, u32[]{:S(2)}, u32[]{:S(2)}) collective-permute-start(bf16[512,512]{1,0:T(8,128)(2,1)} %get-tuple-element.34), channel_id=1, source_target_pairs={{0,4},{4,0},{8,12},{12,8},{16,20},{20,16},{24,28},{28,24},{1,5},{5... | collective-permute-start | bytes 1572872 | tf_op jit(solution)/shard_map/ppermute | solution.py:20
  156.5 57.9 %collective-permute-start.31 = (bf16[512,512]{1,0:T(8,128)(2,1)}, bf16[512,512]{1,0:T(8,128)(2,1)S(1)}, u32[]{:S(2)}, u32[]{:S(2)}) collective-permute-start(bf16[512,512]{1,0:T(8,128)(2,1)} %get-tuple-element.38), channel_id=1, source_target_pairs={{0,16},{4,20},{8,24},{12,28},{16,0},{20,4},{24,8},{28,12},{1,17},{... | collective-permute-start | bytes 1572872 | tf_op jit(solution)/shard_map/ppermute | solution.py:20
  158.9 26.2 %collective-permute-start.6 = (bf16[512,512]{1,0:T(8,128)(2,1)S(1)}, bf16[512,512]{1,0:T(8,128)(2,1)S(1)}, u32[]{:S(2)}, u32[]{:S(2)}) collective-permute-start(bf16[512,512]{1,0:T(8,128)(2,1)S(1)} %collective-permute-done.2.refs_3_), channel_id=1, source_target_pairs={{0,4},{4,0},{8,12},{12,8},{16,20},{20,16},{24,28},{28,24},{1,5},{5... | collective-permute-start | bytes 1572872 | tf_op jit(solution)/shard_map/ppermute | solution.py:20
  183.1 30.8 %collective-permute-start.11 = (bf16[512,1024]{1,0:T(8,128)(2,1)}, bf16[512,1024]{1,0:T(8,128)(2,1)S(1)}, u32[]{:S(2)}, u32[]{:S(2)}) collective-permute-start(bf16[512,1024]{1,0:T(8,128)(2,1)} %collective-permute-done.9), channel_id=1, source_target_pairs={{0,2},{1,3},{2,0},{3,1},{4,6},{5,7},{6,4},{7,5},{8,10},{9,11},{10,... | collective-permute-start | bytes 3145736 | tf_op jit(solution)/shard_map/ppermute | solution.py:20
  185.1 43.1 %collective-permute-start.10 = (bf16[512,1024]{1,0:T(8,128)(2,1)}, bf16[512,1024]{1,0:T(8,128)(2,1)S(1)}, u32[]{:S(2)}, u32[]{:S(2)}) collective-permute-start(bf16[512,1024]{1,0:T(8,128)(2,1)} %collective-permute-done.9), channel_id=1, source_target_pairs={{0,1},{1,0},{2,3},{3,2},{4,5},{5,4},{6,7},{7,6},{8,9},{9,8},{10,11... | collective-permute-start | bytes 3145736 | tf_op jit(solution)/shard_map/ppermute | solution.py:20
  185.7 26.6 %collective-permute-start.23 = (bf16[512,512]{1,0:T(8,128)(2,1)S(1)}, bf16[512,512]{1,0:T(8,128)(2,1)S(1)}, u32[]{:S(2)}, u32[]{:S(2)}) collective-permute-start(bf16[512,512]{1,0:T(8,128)(2,1)S(1)} %collective-permute-done.21), channel_id=1, source_target_pairs={{0,16},{4,20},{8,24},{12,28},{16,0},{20,4},{24,8},{28,12},{1,17},{... | collective-permute-start | bytes 1572872 | tf_op jit(solution)/shard_map/ppermute | solution.py:20
  213.9 30.4 %collective-permute-start.12 = (bf16[512,1024]{1,0:T(8,128)(2,1)S(1)}, bf16[512,1024]{1,0:T(8,128)(2,1)S(1)}, u32[]{:S(2)}, u32[]{:S(2)}) collective-permute-start(bf16[512,1024]{1,0:T(8,128)(2,1)S(1)} %collective-permute-done.11), channel_id=1, source_target_pairs={{0,1},{1,0},{2,3},{3,2},{4,5},{5,4},{6,7},{7,6},{8,9},{9,8},{10,11... | collective-permute-start | bytes 3145736 | tf_op jit(solution)/shard_map/ppermute | solution.py:20
  215.5 26.1 %collective-permute-start.29 = (bf16[512,512]{1,0:T(8,128)(2,1)}, bf16[512,512]{1,0:T(8,128)(2,1)}, u32[]{:S(2)}, u32[]{:S(2)}) collective-permute-start(bf16[512,512]{1,0:T(8,128)(2,1)} %collective-permute-done.28), channel_id=1, source_target_pairs={{0,16},{4,20},{8,24},{12,28},{16,0},{20,4},{24,8},{28,12},{1,17},{... | collective-permute-start | bytes 1572872 | tf_op jit(solution)/shard_map/ppermute | solution.py:20
  227.2 62.2 %collective-permute-start.32 = (bf16[512,512]{1,0:T(8,128)(2,1)S(1)}, bf16[512,512]{1,0:T(8,128)(2,1)}, u32[]{:S(2)}, u32[]{:S(2)}) collective-permute-start(bf16[512,512]{1,0:T(8,128)(2,1)S(1)} %collective-permute-done.31), channel_id=1, source_target_pairs={{0,4},{4,0},{8,12},{12,8},{16,20},{20,16},{24,28},{28,24},{1,5},{5... | collective-permute-start | bytes 1572872 | tf_op jit(solution)/shard_map/ppermute | solution.py:20
  228.3 61.2 %collective-permute-start.34 = (bf16[512,512]{1,0:T(8,128)(2,1)S(1)}, bf16[512,512]{1,0:T(8,128)(2,1)}, u32[]{:S(2)}, u32[]{:S(2)}) collective-permute-start(bf16[512,512]{1,0:T(8,128)(2,1)S(1)} %copy-done.10), channel_id=1, source_target_pairs={{0,4},{4,0},{8,12},{12,8},{16,20},{20,16},{24,28},{28,24},{1,5},{5... | collective-permute-start | bytes 1572872 | tf_op jit(solution)/shard_map/ppermute | solution.py:20
  238.4 51.0 %collective-permute-start.33 = (bf16[512,512]{1,0:T(8,128)(2,1)}, bf16[512,512]{1,0:T(8,128)(2,1)}, u32[]{:S(2)}, u32[]{:S(2)}) collective-permute-start(bf16[512,512]{1,0:T(8,128)(2,1)} %collective-permute-done.28), channel_id=1, source_target_pairs={{0,4},{4,0},{8,12},{12,8},{16,20},{20,16},{24,28},{28,24},{1,5},{5... | collective-permute-start | bytes 1572872 | tf_op jit(solution)/shard_map/ppermute | solution.py:20
  241.6 47.9 %collective-permute-start.30 = (bf16[512,512]{1,0:T(8,128)(2,1)}, bf16[512,512]{1,0:T(8,128)(2,1)}, u32[]{:S(2)}, u32[]{:S(2)}) collective-permute-start(bf16[512,512]{1,0:T(8,128)(2,1)} %collective-permute-done.29), channel_id=1, source_target_pairs={{0,4},{4,0},{8,12},{12,8},{16,20},{20,16},{24,28},{28,24},{1,5},{5... | collective-permute-start | bytes 1572872 | tf_op jit(solution)/shard_map/ppermute | solution.py:20
  256.8 30.9 %collective-permute-start.19 = (bf16[2,128,512]{2,1,0:T(8,128)(2,1)S(1)}, bf16[2,128,512]{2,1,0:T(8,128)(2,1)S(1)}, u32[]{:S(2)}, u32[]{:S(2)}) collective-permute-start(bf16[2,128,512]{2,1,0:T(8,128)(2,1)S(1)} %get-tuple-element.55), channel_id=1, source_target_pairs={{0,4},{4,0},{8,12},{12,8},{16,20},{20,16},{24,28},{28,24},{1,5},{5... | collective-permute-start | bytes 786440 | tf_op jit(solution)/shard_map/ppermute | solution.py:20
  305.0 29.6 %collective-permute-start.36 = (bf16[512,1024]{0,1:T(8,128)(2,1)}, bf16[512,1024]{0,1:T(8,128)(2,1)}, u32[]{:S(2)}, u32[]{:S(2)}) collective-permute-start(bf16[512,1024]{0,1:T(8,128)(2,1)} %fusion.2), channel_id=1, source_target_pairs={{0,8},{4,12},{8,0},{12,4},{16,24},{20,28},{24,16},{28,20},{1,9},{5... | collective-permute-start | bytes 3145736 | tf_op jit(solution)/shard_map/ppermute | solution.py:20
  312.1 27.7 %collective-permute-start.39 = (bf16[1024,512]{0,1:T(8,128)(2,1)}, bf16[1024,512]{0,1:T(8,128)(2,1)S(1)}, u32[]{:S(2)}, u32[]{:S(2)}) collective-permute-start(bf16[1024,512]{0,1:T(8,128)(2,1)} %fusion), channel_id=1, source_target_pairs={{0,2},{1,3},{2,0},{3,1},{4,6},{5,7},{6,4},{7,5},{8,10},{9,11},{10,... | collective-permute-start | bytes 3145736 | tf_op jit(solution)/shard_map/ppermute | solution.py:20
  (71 other events, 876.2 us)

commit v4 on v3

--- a/solution.py
+++ b/solution.py
@@ -13,6 +13,7 @@
 F32 = jnp.float32
 BF16 = jnp.bfloat16
 VMEM_LIMIT = 48 * 1024 * 1024
+LIGHT = pl.CostEstimate(flops=1, bytes_accessed=1, transcendentals=0)
 
 
 def swapped(value, axis, bit):
@@ -33,21 +34,54 @@
     return lax.optimization_barrier((value, *others))[0]
 
 
-def spread(own, other, seq_count, gates):
-    bits = [1 << b for b in range(seq_count.bit_length() - 1)]
-    bits = [b for b in bits if b > PAIR] + [b for b in bits if b < PAIR]
-    pair_gate, high_gate, low_gate = gates
-    if pair_gate is not None:
-        other = after(other, pair_gate)
-    pieces = {0: own, PAIR: swapped(other, "seq", PAIR)}
-    for bit in bits:
-        for mask in list(pieces):
-            value = pieces[mask]
-            gate = high_gate if bit > PAIR else low_gate
-            if mask == 0 and gate is not None:
-                value = after(value, gate)
-            pieces[mask | bit] = swapped(value, "seq", bit)
-    return pieces
+ROUNDS = (
+    (("x", 4), ("x", 6), ("x", 3), ("x", 5), ("t", 0)),
+    (("z", 4), ("z", 2), ("x", 7), ("z", 1), ("t", 1)),
+    (("z", 6), ("z", 3), ("z", 5), ("w", 2), ("t", 2)),
+    (("w", 4), ("z", 7), ("w", 1)),
+    (("w", 6), ("w", 3), ("w", 5)),
+)
+WAITS = {send: ROUNDS[i] for i in range(len(ROUNDS) - 1) for send in ROUNDS[i + 1]}
+WAITS[("t", 0)] = (("x", 2),)
+
+
+class Sends:
+    def __init__(self, own, given, quarter):
+        self.own, self.given, self.quarter = own, given, quarter
+        self.made = {}
+
+    def get(self, kind, mask):
+        name = (kind, mask)
+        if name not in self.made:
+            self.made[name] = self.tokens(mask) if kind == "t" else self.piece(kind, mask)
+        return self.made[name]
+
+    def waiting(self, name, value):
+        others = [self.get(*other) for other in WAITS.get(name, ())]
+        return after(value, *others) if others else value
+
+    def piece(self, kind, mask):
+        if mask == 0:
+            return self.own[kind]
+        if mask == PAIR:
+            bit, value = PAIR, self.given[kind]
+        else:
+            bit = 1 if mask & 1 else 1 << (mask.bit_length() - 1)
+            value = self.get(kind, mask ^ bit)
+        return swapped(self.waiting((kind, mask), value), "seq", bit)
+
+    def tokens(self, step):
+        if step == 0:
+            return swapped(self.waiting(("t", 0), self.quarter), "seq", PAIR)
+        if step == 1:
+            value = self.get("t", 0)[None]
+            bit = lax.axis_size("head") // 2
+            while bit > 1:
+                got = swapped(self.waiting(("t", 1), value), "head", bit)
+                value = jnp.concatenate([value, got])
+                bit //= 2
+            return value
+        return swapped(self.waiting(("t", 2), self.get("t", 1)), "head", 1)
 
 
 def natural(value, axis_name, bit, axis):
@@ -72,16 +106,15 @@
 
 
 def front_kernel(
-    first_ref, xo_ref, xp_ref, bo_ref, bp_ref, tx_ref, tbc_ref, kx_ref, kbc_ref, dec_ref, xc_ref, bcc_ref, f_ref
+    first_ref, x_ref, bc_ref, tx_ref, tbc_ref, kx_ref, kbc_ref, dec_ref, xc_ref, bcc_ref, f_ref
 ):
     rows = xc_ref.shape[1]
     for r in range(2):
         is_first = first_ref[r] == 1
 
-        def conv(own_ref, other_ref, tail_ref, k_ref):
-            halo = other_ref[r * HALO : (r + 1) * HALO].astype(F32)
-            halo = jnp.where(is_first, tail_ref[...].astype(F32), halo)
-            body = (own_ref[...] if r == 0 else other_ref[2 * HALO :]).astype(F32)
+        def conv(pre_ref, tail_ref, k_ref):
+            halo = jnp.where(is_first, tail_ref[...].astype(F32), pre_ref[r, :HALO].astype(F32))
+            body = pre_ref[r, HALO:].astype(F32)
             whole = jnp.concatenate([halo, body], axis=0)
             taps = k_ref.shape[0]
             total = jnp.zeros(body.shape, F32)
@@ -90,8 +123,8 @@
                 total = total + k_ref[k : k + 1, :] * whole[start : start + rows]
             return (total * jax.nn.sigmoid(total)).astype(BF16)
 
-        x_val = conv(xo_ref, xp_ref, tx_ref, kx_ref)
-        bc_val = conv(bo_ref, bp_ref, tbc_ref, kbc_ref)
+        x_val = conv(x_ref, tx_ref, kx_ref)
+        bc_val = conv(bc_ref, tbc_ref, kbc_ref)
         xc_ref[r] = x_val
         bcc_ref[r] = bc_val
         decayed = (x_val.astype(F32) * dec_ref[r]).astype(BF16)
@@ -147,12 +180,12 @@
     return pl.BlockSpec(shape, lambda *_: (0,) * len(shape))
 
 
-def front(first, x_own, x_other, bc_own, bc_other, tail_x, tail_bc, conv_x, conv_bc, decay):
-    rows, chans = x_own.shape
-    bcw = bc_own.shape[1]
+def front(first, x_pre, bc_pre, tail_x, tail_bc, conv_x, conv_bc, decay):
+    rows, chans = x_pre.shape[1] - HALO, x_pre.shape[2]
+    bcw = bc_pre.shape[2]
     return pl.pallas_call(
         front_kernel,
-        in_specs=[pl.BlockSpec(memory_space=pltpu.SMEM)] + [pl.BlockSpec(memory_space=pltpu.VMEM)] * 9,
+        in_specs=[pl.BlockSpec(memory_space=pltpu.SMEM)] + [pl.BlockSpec(memory_space=pltpu.VMEM)] * 7,
         out_specs=[pl.BlockSpec(memory_space=pltpu.VMEM)] * 3,
         out_shape=[
             jax.ShapeDtypeStruct((2, rows, chans), BF16),
@@ -160,33 +193,49 @@
             jax.ShapeDtypeStruct((2, rows // Q, bcw // 2, chans), F32),
         ],
         compiler_params=pltpu.CompilerParams(vmem_limit_bytes=VMEM_LIMIT),
+        cost_estimate=LIGHT,
         name="front",
-    )(first, x_own, x_other, bc_own, bc_other, tail_x, tail_bc, conv_x, conv_bc, decay)
-
-
-def project_kernel(place_ref, others_ref, *refs):
-    pieces, out_ref = refs[:-1], refs[-1]
-    depth = pieces[0].shape[0]
-    total = None
-    for k, piece in enumerate(pieces):
-        start = pl.multiple_of(place_ref[1, k], depth)
-        term = dot(others_ref[place_ref[0, k], :, pl.ds(start, depth)], piece[...])
-        total = term if total is None else total + term
-    out_ref[...] = total.astype(BF16)
-
-
-def project_others(places, others, pieces):
-    rows = others.shape[1]
-    chans = pieces[0].shape[1]
+    )(first, x_pre, bc_pre, tail_x, tail_bc, conv_x, conv_bc, decay)
+
+
+def project_kernel(depth, with_halo, one_weight, place_ref, *refs):
+    refs = list(refs)
+    out_ref = refs.pop()
+    halo_ref = refs.pop(0) if with_halo else None
+    tokens_ref, others_ref = refs[:2]
+    rows = tokens_ref.shape[0]
+    lead = HALO if with_halo else 0
+    totals = [None] * 3
+    for k in range(place_ref.shape[1]):
+        start = pl.multiple_of(place_ref[0, k], depth)
+        place = pl.multiple_of(place_ref[2, k], depth)
+        weight = refs[2][pl.ds(start, depth), :] if one_weight else refs[2 + k][:depth]
+        lefts = [tokens_ref[:, pl.ds(start, depth)], others_ref[place_ref[1, k], :rows, pl.ds(place, depth)]]
+        if with_halo:
+            lefts.append(halo_ref[:, pl.ds(start, depth)])
+        for i, left in enumerate(lefts):
+            term = dot(left, weight)
+            totals[i] = term if totals[i] is None else totals[i] + term
+    for r in range(2):
+        out_ref[r, lead:] = totals[r].astype(BF16)
+        if with_halo:
+            out_ref[r, :lead] = totals[2][r * HALO : (r + 1) * HALO].astype(BF16)
+
+
+def project(places, depth, tokens, others, weights, halo=None):
+    rows = tokens.shape[0] + (0 if halo is None else HALO)
+    chans = weights[0].shape[1]
+    operands = ([] if halo is None else [halo]) + [tokens, others] + list(weights)
     return pl.pallas_call(
-        project_kernel,
+        functools.partial(project_kernel, depth, halo is not None, len(weights) == 1),
         in_specs=[pl.BlockSpec(memory_space=pltpu.SMEM)]
-        + [pl.BlockSpec(memory_space=pltpu.VMEM)] * (1 + len(pieces)),
+        + [pl.BlockSpec(memory_space=pltpu.VMEM)] * len(operands),
         out_specs=pl.BlockSpec(memory_space=pltpu.VMEM),
-        out_shape=jax.ShapeDtypeStruct((rows, chans), BF16),
+        out_shape=jax.ShapeDtypeStruct((2, rows, chans), BF16),
         compiler_params=pltpu.CompilerParams(vmem_limit_bytes=VMEM_LIMIT),
+        cost_estimate=LIGHT,
         name="project",
-    )(places, others, *pieces)
+    )(places, *operands)
 
 
 def intra(x_conv, bc_conv, cum, cumt, heads):
@@ -197,7 +246,6 @@
     def tile(w):
         return pl.BlockSpec((1, Q, w), lambda r, i: (r, i, 0))
 
-    work = 2 * rows * Q
     return pl.pallas_call(
         functools.partial(intra_kernel, heads),
         grid=(2, blocks),
@@ -205,9 +253,7 @@
         out_specs=tile(chans),
         out_shape=jax.ShapeDtypeStruct((2, rows, chans), F32),
         compiler_params=params(2),
-        cost_estimate=pl.CostEstimate(
-            flops=2 * work * (chans + bcw // 2), bytes_accessed=12 * rows * chans, transcendentals=work * heads
-        ),
+        cost_estimate=LIGHT,
         name="intra",
     )(x_conv, bc_conv, cum, cumt)
 
@@ -238,6 +284,7 @@
             jax.ShapeDtypeStruct((2, rows, 128), F32),
         ],
         compiler_params=params(2),
+        cost_estimate=LIGHT,
         name="gate",
     )(y_in, x_conv, bc_conv, state, grown, skip, z_val, gain)
 
@@ -268,61 +315,67 @@
     chans = heads * head_dim
     depth = w_xz.shape[0]
 
+    lag = conv_x.shape[0] - 1
+    code_sums = jnp.sum(decay_code, axis=0)
+    digits = jnp.stack([(code_sums >> (8 * j)) & 255 for j in range(4)]).reshape(1, -1).astype(BF16)
+    last_rows = tokens[rows - lag :].reshape(-1, chans)
+    halo_rows = last_rows.shape[0]
+    spare = -(halo_rows + 1) % 16
+    extra = jnp.concatenate(
+        [last_rows, jnp.pad(digits, ((0, spare), (0, chans - digits.shape[1])))], axis=0
+    )
+
+    share = tokens.shape[1] // head_count
+    codes = decay_code.T
+    given = cut(codes, 1 - half, heads, 0)
+    given = jnp.stack([(given >> (8 * j)) & 255 for j in range(3)]).reshape(-1, share).astype(BF16)
+    code_rows = given.shape[0]
+    given = jnp.pad(given, ((0, -code_rows % 16), (0, 0)))
+
     flat_w = lax.optimization_barrier(w_xz.reshape(depth, -1))
     full = flat_w.shape[1] // 2
     x_w, z_w = flat_w[:, :full], flat_w[:, full:]
     high = max(b for b in (PAIR, seq_count // 2))
-    share = tokens.shape[1] // head_count
-    quarters = {0: swapped(cut(tokens, mine, share, 1), "seq", PAIR)}
-    x_pieces = spread(
-        cut(x_w, half, chans, 1), cut(x_w, 1 - half, chans, 1), seq_count, (None, None, None)
-    )
-    z_pieces = spread(
-        cut(z_w, half, chans, 1),
-        cut(z_w, 1 - half, chans, 1),
-        seq_count,
-        (quarters[0], x_pieces[high], x_pieces[PAIR | 1]),
-    )
-    out_pieces = spread(
-        cut(w_out, half, chans, 0),
-        cut(w_out, 1 - half, chans, 0),
-        seq_count,
-        (z_pieces[PAIR], z_pieces[high], z_pieces[PAIR | 1]),
-    )
-
-    bit = head_count // 2
-    while bit >= 1:
-        for mask in list(quarters):
-            quarters[mask | bit] = swapped(quarters[mask], "head", bit)
-        bit //= 2
-    before = shifted(tokens[rows - HALO :], "seq", 1)
-    before_other = swapped(after(before, x_pieces[PAIR]), "seq", PAIR)
-    halo = after(jnp.concatenate([before, before_other], axis=0), x_pieces[high])
-    others = jnp.stack(
-        [
-            jnp.concatenate([cut(halo, mine ^ mask, share, 1), quarters[mask]], axis=0)
-            for mask in range(head_count)
-        ]
-    )
-
-    narrow = w_bc.shape[1] // head_count
-    pack = max(1, 128 // narrow)
-    some = cut(w_bc, mine, narrow, 1).reshape(pack, depth // pack, narrow)
-    some = some.transpose(1, 0, 2).reshape(depth // pack, pack * narrow)
-    some = after(lax.all_gather(some, "seq", axis=0), x_pieces[high])
-    some = some.reshape(seq_count, depth // pack, pack, narrow).transpose(0, 2, 1, 3)
-    some = some.reshape(-1, narrow)
-    bc_part = jnp.concatenate([dot(halo, some), dot(tokens, some)], axis=0).astype(BF16)
-    bit = 1
-    while bit < head_count:
-        bc_part = natural(bc_part, "head", bit, 1)
-        bit *= 2
-    bc_own = bc_part[2 * HALO :]
-    bc_other = jnp.concatenate([bc_part[: 2 * HALO], swapped(bc_own, "seq", PAIR)], axis=0)
-
-    logdec = -decay_code.T.astype(F32) / (16.0 * rows * seq_count)
-    ld_other = swapped(cut(logdec, 1 - half, heads, 0), "seq", PAIR)
-    ld = jnp.stack([cut(logdec, half, heads, 0), after(ld_other, x_pieces[PAIR])])
+    own = {
+        "x": jnp.concatenate([cut(x_w, half, chans, 1), extra], axis=0),
+        "z": cut(z_w, half, chans, 1),
+        "w": cut(w_out, half, chans, 0),
+    }
+    given_away = {
+        "x": jnp.concatenate([cut(x_w, 1 - half, chans, 1), extra], axis=0),
+        "z": cut(z_w, 1 - half, chans, 1),
+        "w": cut(w_out, 1 - half, chans, 0),
+    }
+    sends = Sends(own, given_away, jnp.concatenate([cut(tokens, mine, share, 1), given], axis=0))
+    masks = list(range(seq_count))
+    x_pieces, z_pieces, out_pieces = [{mask: sends.get(kind, mask) for mask in masks} for kind in "xzw"]
+
+    others = jnp.concatenate([sends.get("t", 1), sends.get("t", 2)])
+    ranges = [me, me ^ PAIR]
+    extras = jnp.stack([x_pieces[mask][depth:] for mask in range(seq_count)])
+
+    def rows_before(place):
+        got = lax.dynamic_index_in_dim(extras, (me ^ (place - 1)) & (seq_count - 1), 0, keepdims=False)
+        return jnp.pad(got[:halo_rows].reshape(lag, -1), ((HALO - lag, 0), (0, 0)))
+
+    halo = jnp.concatenate([rows_before(place) for place in ranges], axis=0)
+
+    starts = [(me ^ mask) * depth for mask in masks]
+    blocks = [a // share ^ mine for a in starts]
+    blocks = [(b >> 1) + (b & 1) * (head_count // 2) for b in blocks]
+    spots = [starts, blocks, [a % share for a in starts]]
+    spots = jnp.stack([jnp.stack([jnp.int32(a) for a in row]) for row in spots])
+
+    part = depth // head_count
+    w_bc_all = lax.all_gather(cut(w_bc, mine, part, 0), ("seq", "head"), axis=0, tiled=True)
+    bc_pre = project(spots, depth, tokens, others, [w_bc_all], halo)
+    x_pre = project(spots, depth, tokens, others, list(x_pieces.values()), halo)
+    z_val = project(spots, depth, tokens, others, list(z_pieces.values()))
+
+    per_code = -1.0 / (16.0 * rows * seq_count)
+    got = sends.get("t", 0)[rows : rows + code_rows].astype(F32).reshape(3, heads, rows)
+    other_codes = got[0] + 256.0 * got[1] + 65536.0 * got[2]
+    ld = jnp.stack([cut(codes, half, heads, 0).astype(F32), other_codes]) * per_code
     blocks = rows // Q
     cumt = jnp.cumsum(ld.reshape(2, heads, blocks, Q), axis=3).transpose(0, 2, 1, 3)
     cum = cumt.transpose(0, 1, 3, 2)
@@ -331,47 +384,16 @@
     block_decay = jnp.repeat(jnp.exp(ends), head_dim, axis=3)
     cum = cum.reshape(2, rows, heads)
     grown = jnp.repeat(jnp.exp(cum), head_dim, axis=2)
-    totals = jnp.sum(ld, axis=2)
-    masks = [0, PAIR]
-    bit = 1
-    while bit < seq_count:
-        if bit != PAIR:
-            got = after(swapped(totals, "seq", bit), x_pieces[high])
-            totals = jnp.concatenate([totals, got])
-            masks = masks + [m | bit for m in masks]
-        bit *= 2
+    totals = jnp.stack([x_pieces[mask][depth + halo_rows] for mask in masks])
+    totals = totals[:, : 4 * all_heads].astype(F32).reshape(-1, 4, all_heads)
+    totals = sum(totals[:, j] * 256.0**j for j in range(4)) * per_code
+    totals = cut(totals, half, heads, 1)
     places = me ^ jnp.array(masks, jnp.int32)
 
     def decay_between(low, high):
         chosen = jnp.where((places >= low) & (places < high), 1.0, 0.0)[:, None]
         return jnp.repeat(jnp.exp(jnp.sum(chosen * totals, axis=0)), head_dim)[None, :]
 
-    def own_part(mask):
-        return cut(tokens, me ^ mask, depth, 1)
-
-    def other_place(mask):
-        start = (me ^ mask) * depth
-        return start // share ^ mine, start % share
-
-    def other_part(mask):
-        block, start = other_place(mask)
-        return lax.dynamic_slice(others, (block, 2 * HALO, start), (1, rows, depth))[0]
-
-    def project(pieces, part):
-        total = None
-        for mask, piece in pieces.items():
-            term = dot(part(mask), piece)
-            total = term if total is None else total + term
-        return total.astype(BF16)
-
-    x_own = project(x_pieces, own_part)
-    spots = [other_place(mask) for mask in x_pieces]
-    spots = jnp.stack([jnp.stack([jnp.int32(p[i]) for p in spots]) for i in range(2)])
-    x_other = project_others(spots, others, list(x_pieces.values()))
-    z_own = project(z_pieces, own_part)
-    z_other = project(z_pieces, other_part)
-
-    ranges = [me, me ^ PAIR]
     first = jnp.stack([(r == 0).astype(jnp.int32) for r in ranges])
 
     def padded(tail):
@@ -379,10 +401,8 @@
 
     x_conv, bc_conv, added = front(
         first,
-        x_own,
-        x_other,
-        bc_own,
-        bc_other,
+        x_pre,
+        bc_pre,
         padded(cut(tail_x, half, chans, 1)),
         padded(tail_bc),
         cut(conv_x, half, chans, 1),
@@ -431,7 +451,7 @@
         jnp.stack(states, axis=1),
         grown,
         jnp.repeat(cut(skip_gain, half, heads, 0), head_dim)[None, :],
-        jnp.stack([z_own, z_other]),
+        z_val,
         cut(norm_gain, half, chans, 0)[None, :],
     )
 

time: 358 us -> 302 us (0.84)
  blocking collectives: 65.5 us -> 0 us
  matrix products: 43.4 us -> 11.3 us
  waiting for transfers between devices: 115 us -> 94.9 us
  starting transfers between devices: 54.3 us -> 73.6 us
  Pallas kernels: 17.1 us -> 35.7 us
  between operations: 1.71 us -> 15.1 us
  other arithmetic: 21.8 us -> 28.5 us
    all_gather x1 -> x0, blocking collectives: 65.5 us -> none  [local(): some = after(lax.all_gather(some, 'seq', axis=0), x_pieces[high])]
    dot_general x33 -> x7, matrix products: 43.4 us -> 11.3 us  [dot(): return jnp.dot(a, b, preferred_element_type=F32)]
    ppermute x42 -> x34, starting transfers between devices: 50.9 us -> 71.4 us  [swapped(): return lax.ppermute(value, axis, [(i, i ^ bit) for i in range(size)])]
    ppermute x42 -> x34, waiting for transfers between devices: 114 us -> 94.9 us  [swapped(): return lax.ppermute(value, axis, [(i, i ^ bit) for i in range(size)])]
    pallas_call x1 -> x3, Pallas kernels: 4.86 us -> 23.9 us  [project(): pl.pallas_call(functools.partial(project_kernel, depth, halo is not None,...]
    concatenate x4 -> x5, other arithmetic: 1.97 us -> 7.89 us  [the longest x1 3.81 us: local(): others = jnp.concatenate([sends.get('t', 1), sends.get('t', 2)])]
    exp x8, local copies, waits for them, and re-layouts: 4.5 us -> 0.03 us  [decay_between(): jnp.exp(jnp.sum(chosen * totals, axis=0))]
    unnamed x101 -> x161, local copies, waits for them, and re-layouts: 5.38 us -> 8.08 us
  transfers between devices with their start and end apart: 44 -> 36, of which waited for: 16 -> 15; matrix products, arithmetic and copies ran while one was open for 26% -> 22% of each run, Pallas kernels for 4% -> 12%
where the time goes in v4:
time: 302 us; the launch traced here: 300 us
  waiting for transfers between devices  94.9 us (31%)
  starting transfers between devices  73.6 us (24%)
  local copies, waits for them, and re-layouts  41.4 us (14%)
  Pallas kernels  35.7 us (12%)
  other arithmetic  28.5 us (9%)
  between operations  15.1 us (5%)
  matrix products  11.3 us (4%)
    ppermute x34, waiting for transfers between devices, swapped(): return lax.ppermute(value, axis, [(i, i ^ bit) for i in range(size)])  94.9 us
    ppermute x34, starting transfers between devices, swapped(): return lax.ppermute(value, axis, [(i, i ^ bit) for i in range(size)])  71.4 us
    pallas_call x3, Pallas kernels, project(): pl.pallas_call(functools.partial(project_kernel, depth, halo is not None,...  23.9 us
    dot_general x7, matrix products, dot(): return jnp.dot(a, b, preferred_element_type=F32)  11.3 us
    dynamic_slice x10, local copies, waits for them, and re-layouts, cut(): return lax.dynamic_slice_in_dim(value, index * size, size, axis)  8.53 us
    unnamed x161, local copies, waits for them, and re-layouts  8.08 us
  transfers between devices with their start and end apart: 36, of which 15 were waited for; matrix products, arithmetic and copies ran while one was open for 22% of the time, Pallas kernels for 12%

profile of v4, /device:TPU:0, one launch (start us, length us, event | category | flops | bytes accessed | tf_op | source)
XLA Modules:
  0.0 300.4 jit_solution(9168290266643433898)
XLA Ops:
  12.1 4.0 %collective-permute-start.3 = (bf16[544,512]{1,0:T(8,128)(2,1)S(1)}, bf16[544,512]{1,0:T(8,128)(2,1)S(1)}, u32[]{:S(2)}, u32[]{:S(2)}) collective-permute-start(bf16[544,512]{1,0:T(8,128)(2,1)S(1)} %get-tuple-element.87.refs_3_), channel_id=1, source_target_pairs={{0,16},{4,20},{8,24},{12,28},{16,0},{20,4},{24,8},{28,12},{1,17},{... | collective-permute-start | bytes 1671176 | tf_op jit(solution)/shard_map/ppermute | solution.py:21
  36.6 7.3 %collective-permute-done.1.refs_5_ = bf16[544,512]{1,0:T(8,128)(2,1)S(1)} collective-permute-done((bf16[544,512]{1,0:T(8,128)(2,1)}, bf16[544,512]{1,0:T(8,128)(2,1)S(1)}, u32[]{:S(2)}, u32[]{:S(2)}) %collective-permute-start.1) | collective-permute-done | bytes 557088 | tf_op jit(solution)/shard_map/ppermute | solution.py:21
  49.6 11.6 %collective-permute-done.2.refs_6_ = bf16[544,512]{1,0:T(8,128)(2,1)S(1)} collective-permute-done((bf16[544,512]{1,0:T(8,128)(2,1)S(1)}, bf16[544,512]{1,0:T(8,128)(2,1)S(1)}, u32[]{:S(2)}, u32[]{:S(2)}) %collective-permute-start.2) | collective-permute-done | bytes 557088 | tf_op jit(solution)/shard_map/ppermute | solution.py:21
  61.2 7.3 %collective-permute-done.4.refs_8_ = bf16[544,512]{1,0:T(8,128)(2,1)S(1)} collective-permute-done((bf16[544,512]{1,0:T(8,128)(2,1)S(1)}, bf16[544,512]{1,0:T(8,128)(2,1)S(1)}, u32[]{:S(2)}, u32[]{:S(2)}) %collective-permute-start.4) | collective-permute-done | bytes 557088 | tf_op jit(solution)/shard_map/ppermute | solution.py:21
  68.5 3.5 %collective-permute-done.5.refs_9_ = bf16[544,512]{1,0:T(8,128)(2,1)} collective-permute-done((bf16[544,512]{1,0:T(8,128)(2,1)S(1)}, bf16[544,512]{1,0:T(8,128)(2,1)}, u32[]{:S(2)}, u32[]{:S(2)}) %collective-permute-start.5) | collective-permute-done | bytes 557088 | tf_op jit(solution)/shard_map/ppermute | solution.py:21
  75.2 13.8 %collective-permute-done.6 = bf16[528,1024]{1,0:T(8,128)(2,1)} collective-permute-done((bf16[528,1024]{1,0:T(8,128)(2,1)S(1)}, bf16[528,1024]{1,0:T(8,128)(2,1)}, u32[]{:S(2)}, u32[]{:S(2)}) %collective-permute-start.6) | collective-permute-done | bytes 1081376 | tf_op jit(solution)/shard_map/ppermute | solution.py:21
  104.5 3.0 copy.38.dec_ref
  109.2 2.9 copy.49.e_ref
  114.2 3.1 %pad_maximum_fusion.1 = bf16[2,528,1024]{2,1,0:T(8,128)(2,1)} fusion(bf16[1,528,1024]{2,1,0:T(8,128)(2,1)} %collective-permute-done.8, bf16[1,528,1024]{2,1,0:T(8,128)(2,1)} %bitcast.47), kind=kLoop, calls=%fused_computation.2 | loop fusion | flops 1081344 | bytes 4325376 | tf_op jit(solution)/shard_map/concatenate | solution.py:81
  126.7 3.8 %pad_maximum_fusion.refs_2_.refs_1_ = bf16[4,528,1024]{2,1,0:T(8,128)(2,1)} fusion(bf16[2,528,1024]{2,1,0:T(8,128)(2,1)} %collective-permute-done.12, bf16[1,528,1024]{2,1,0:T(8,128)(2,1)} %collective-permute-done.8, bf16[1,528,1024]{2,1,0:T(8,128)(2,1)} %bitcast.47), kind=kLoop, calls=%fused_computation | loop fusion | flops 4325376 | bytes 8650752 | tf_op jit(solution)/shard_map/concatenate | solution.py:353
  130.7 8.9 %project.3.x_ref = bf16[2,528,512]{2,1,0:T(8,128)(2,1)S(1)} custom-call(s32[3,8]{1,0:T(4,128)S(1)} %copy-done.21, bf16[32,4096]{1,0:T(8,128)(2,1)S(1)} %fusion.43.refs_0_, bf16[512,4096]{1,0:T(8,128)(2,1)} %refs_0_.1, bf16[4,528,1024]{2,1,0:T(8,128)(2,1)} %pad_maximum_fusion.refs_2_.refs_1_, bf16[544,512]{1,0:T(8,128)(2,1)S(1)} %get-tuple-element.87.refs_3_, ...), custom_call_target="tpu_custom_call" | custom-call | flops 1 | bytes 1 | tf_op jit(solution)/shard_map/project/pallas_call | solution.py:229
  141.2 6.2 %project.4.bc_ref = bf16[2,528,256]{2,1,0:T(8,128)(2,1)S(1)} custom-call(s32[3,8]{1,0:T(4,128)S(1)} %copy-done.22, bf16[32,4096]{1,0:T(8,128)(2,1)S(1)} %fusion.43.refs_0_, bf16[512,4096]{1,0:T(8,128)(2,1)} %refs_0_.1, bf16[4,528,1024]{2,1,0:T(8,128)(2,1)} %pad_maximum_fusion.refs_2_.refs_1_, bf16[4096,256]{1,0:T(8,128)(2,1)S(1)} %copy-done.5), custom_call_target="tpu_custom_call" | custom-call | flops 1 | bytes 1 | tf_op jit(solution)/shard_map/project/pallas_call | solution.py:229
  147.6 4.8 %front.1 = (bf16[2,512,512]{2,1,0:T(8,128)(2,1)S(1)}, bf16[2,512,256]{2,1,0:T(8,128)(2,1)S(1)}, f32[2,2,128,512]{3,2,1,0:T(8,128)S(1)}) custom-call(s32[2]{0:T(128)S(1)} %copy-done.26, bf16[2,528,512]{2,1,0:T(8,128)(2,1)S(1)} %project.3.x_ref, bf16[2,528,256]{2,1,0:T(8,128)(2,1)S(1)} %project.4.bc_ref, bf16[16,512]{1,0:T(8,128)(2,1)S(1)} %pad.27.tx_ref, ...), custom_call_target="tpu_custom_call" | custom-call | flops 1 | bytes 1 | tf_op jit(solution)/shard_map/front/pallas_call | solution.py:186
  160.2 3.4 %collective-permute-done.13 = bf16[2,128,512]{2,1,0:T(8,128)(2,1)} collective-permute-done((bf16[2,128,512]{2,1,0:T(8,128)(2,1)S(1)}, bf16[2,128,512]{2,1,0:T(8,128)(2,1)}, u32[]{:S(2)}, u32[]{:S(2)}) %collective-permute-start.13) | collective-permute-done | bytes 262176 | tf_op jit(solution)/shard_map/ppermute | solution.py:21
  172.3 10.9 %collective-permute-done.20 = bf16[512,512]{1,0:T(8,128)(2,1)} collective-permute-done((bf16[512,512]{1,0:T(8,128)(2,1)}, bf16[512,512]{1,0:T(8,128)(2,1)}, u32[]{:S(2)}, u32[]{:S(2)}) %collective-permute-start.20) | collective-permute-done | bytes 524320 | tf_op jit(solution)/shard_map/ppermute | solution.py:21
  188.3 8.8 %project.5.z_ref = bf16[2,512,512]{2,1,0:T(8,128)(2,1)S(1)} custom-call(s32[3,8]{1,0:T(4,128)S(1)} %copy-done.22, bf16[512,4096]{1,0:T(8,128)(2,1)} %refs_0_.1, bf16[4,528,1024]{2,1,0:T(8,128)(2,1)} %pad_maximum_fusion.refs_2_.refs_1_, bf16[512,512]{1,0:T(8,128)(2,1)S(1)} %copy-done.4, bf16[512,512]{1,0:T(8,128)(2,1)S(1)} %copy-done.17, ...), custom_call_target="tpu_custom_call" | custom-call | flops 1 | bytes 1 | tf_op jit(solution)/shard_map/project/pallas_call | solution.py:229
  197.2 4.1 %gate.1 = (bf16[2,512,512]{2,1,0:T(8,128)(2,1)S(1)}, f32[2,512,128]{2,1,0:T(8,128)S(1)}) custom-call(f32[2,512,512]{2,1,0:T(8,128)} %copy-done.2, bf16[2,512,512]{2,1,0:T(8,128)(2,1)S(1)} %get-tuple-element.30.x_ref, bf16[2,512,256]{2,1,0:T(8,128)(2,1)S(1)} %copy-done.8, f32[2,2,128,512]{3,2,1,0:T(8,128)S(1)} %pad_maximum_fusion.2.st_ref, ...), custom_call_target="tpu_custom_call" | custom-call | flops 1 | bytes 1 | tf_op jit(solution)/shard_map/gate/pallas_call | solution.py:268
  204.9 7.7 %collective-permute-done.24 = bf16[512,512]{1,0:T(8,128)(2,1)S(1)} collective-permute-done((bf16[512,512]{1,0:T(8,128)(2,1)}, bf16[512,512]{1,0:T(8,128)(2,1)S(1)}, u32[]{:S(2)}, u32[]{:S(2)}) %collective-permute-start.24) | collective-permute-done | bytes 524320 | tf_op jit(solution)/shard_map/ppermute | solution.py:21
  212.6 8.4 %collective-permute-done.23 = bf16[512,512]{1,0:T(8,128)(2,1)S(1)} collective-permute-done((bf16[512,512]{1,0:T(8,128)(2,1)S(1)}, bf16[512,512]{1,0:T(8,128)(2,1)S(1)}, u32[]{:S(2)}, u32[]{:S(2)}) %collective-permute-start.23) | collective-permute-done | bytes 524320 | tf_op jit(solution)/shard_map/ppermute | solution.py:21
  229.0 18.2 %collective-permute-start.27 = (bf16[512,1024]{0,1:T(8,128)(2,1)S(1)}, bf16[512,1024]{0,1:T(8,128)(2,1)S(1)}, u32[]{:S(2)}, u32[]{:S(2)}) collective-permute-start(bf16[512,1024]{0,1:T(8,128)(2,1)S(1)} %fusion.3), channel_id=1, source_target_pairs={{0,8},{4,12},{8,0},{12,4},{16,24},{20,28},{24,16},{28,20},{1,9},{5... | collective-permute-start | bytes 3145736 | tf_op jit(solution)/shard_map/ppermute | solution.py:21
  247.1 4.4 %collective-permute-done.30 = bf16[1024,512]{0,1:T(8,128)(2,1)S(1)} collective-permute-done((bf16[1024,512]{0,1:T(8,128)(2,1)S(1)}, bf16[1024,512]{0,1:T(8,128)(2,1)S(1)}, u32[]{:S(2)}, u32[]{:S(2)}) %collective-permute-start.30) | collective-permute-done | bytes 1048608 | tf_op jit(solution)/shard_map/ppermute | solution.py:21
  254.4 18.1 %collective-permute-start.31 = (bf16[512,512]{0,1:T(8,128)(2,1)}, bf16[512,512]{0,1:T(8,128)(2,1)}, u32[]{:S(2)}, u32[]{:S(2)}) collective-permute-start(bf16[512,512]{0,1:T(8,128)(2,1)} %slice.375), channel_id=1, source_target_pairs={{0,8},{4,12},{8,0},{12,4},{16,24},{20,28},{24,16},{28,20},{1,9},{5... | collective-permute-start | bytes 1572872 | tf_op jit(solution)/shard_map/ppermute | solution.py:21
  275.0 9.6 %collective-permute-done.32 = f32[512]{0:T(512)S(1)} collective-permute-done((f32[512]{0:T(512)S(1)}, f32[512]{0:T(512)S(1)}, u32[]{:S(2)}, u32[]{:S(2)}) %collective-permute-start.32) | collective-permute-done | bytes 2080 | tf_op jit(solution)/shard_map/ppermute | solution.py:21
  286.2 3.2 %collective-permute-done.34 = f32[512]{0:T(512)S(1)} collective-permute-done((f32[512]{0:T(512)S(1)}, f32[512]{0:T(512)S(1)}, u32[]{:S(2)}, u32[]{:S(2)}) %collective-permute-start.34) | collective-permute-done | bytes 2080 | tf_op jit(solution)/shard_map/ppermute | solution.py:21
  (373 shorter events, 108.3 us)
Async XLA Ops:
  6.5 133.1 %all-gather.2.cloned.1.call-start = ((), (), s32[]{:S(2)}) async-start(), calls=%async_computation | async-start | bytes 2162688 | tf_op jit(solution)/shard_map/all_gather | solution.py:370
  12.1 33.2 %collective-permute-start.3 = (bf16[544,512]{1,0:T(8,128)(2,1)S(1)}, bf16[544,512]{1,0:T(8,128)(2,1)S(1)}, u32[]{:S(2)}, u32[]{:S(2)}) collective-permute-start(bf16[544,512]{1,0:T(8,128)(2,1)S(1)} %get-tuple-element.87.refs_3_), channel_id=1, source_target_pairs={{0,16},{4,20},{8,24},{12,28},{16,0},{20,4},{24,8},{28,12},{1,17},{... | collective-permute-start | bytes 1671176 | tf_op jit(solution)/shard_map/ppermute | solution.py:21
  16.2 33.4 %collective-permute-start = (bf16[544,512]{1,0:T(8,128)(2,1)S(1)}, bf16[544,512]{1,0:T(8,128)(2,1)S(1)}, u32[]{:S(2)}, u32[]{:S(2)}) collective-permute-start(bf16[544,512]{1,0:T(8,128)(2,1)S(1)} %get-tuple-element.87.refs_3_), channel_id=1, source_target_pairs={{0,4},{4,0},{8,12},{12,8},{16,20},{20,16},{24,28},{28,24},{1,5},{5... | collective-permute-start | bytes 1671176 | tf_op jit(solution)/shard_map/ppermute | solution.py:21
  17.7 26.2 %collective-permute-start.1 = (bf16[544,512]{1,0:T(8,128)(2,1)}, bf16[544,512]{1,0:T(8,128)(2,1)S(1)}, u32[]{:S(2)}, u32[]{:S(2)}) collective-permute-start(bf16[544,512]{1,0:T(8,128)(2,1)} %get-tuple-element.86), channel_id=1, source_target_pairs={{0,8},{4,12},{8,0},{12,4},{16,24},{20,28},{24,16},{28,20},{1,9},{5... | collective-permute-start | bytes 1671176 | tf_op jit(solution)/shard_map/ppermute | solution.py:21
  44.4 27.6 %collective-permute-start.5 = (bf16[544,512]{1,0:T(8,128)(2,1)S(1)}, bf16[544,512]{1,0:T(8,128)(2,1)}, u32[]{:S(2)}, u32[]{:S(2)}) collective-permute-start(bf16[544,512]{1,0:T(8,128)(2,1)S(1)} %collective-permute-done.1.refs_5_), channel_id=1, source_target_pairs={{0,16},{4,20},{8,24},{12,28},{16,0},{20,4},{24,8},{28,12},{1,17},{... | collective-permute-start | bytes 1671176 | tf_op jit(solution)/shard_map/ppermute | solution.py:21
  45.3 23.2 %collective-permute-start.4 = (bf16[544,512]{1,0:T(8,128)(2,1)S(1)}, bf16[544,512]{1,0:T(8,128)(2,1)S(1)}, u32[]{:S(2)}, u32[]{:S(2)}) collective-permute-start(bf16[544,512]{1,0:T(8,128)(2,1)S(1)} %collective-permute-done.3.refs_7_), channel_id=1, source_target_pairs={{0,4},{4,0},{8,12},{12,8},{16,20},{20,16},{24,28},{28,24},{1,5},{5... | collective-permute-start | bytes 1671176 | tf_op jit(solution)/shard_map/ppermute | solution.py:21
  47.2 41.8 %collective-permute-start.6 = (bf16[528,1024]{1,0:T(8,128)(2,1)S(1)}, bf16[528,1024]{1,0:T(8,128)(2,1)}, u32[]{:S(2)}, u32[]{:S(2)}) collective-permute-start(bf16[528,1024]{1,0:T(8,128)(2,1)S(1)} %fusion.8), channel_id=1, source_target_pairs={{0,8},{4,12},{8,0},{12,4},{16,24},{20,28},{24,16},{28,20},{1,9},{5... | collective-permute-start | bytes 3244040 | tf_op jit(solution)/shard_map/ppermute | solution.py:21
  89.0 28.3 %collective-permute-start.11 = (bf16[512,512]{1,0:T(8,128)(2,1)S(1)}, bf16[512,512]{1,0:T(8,128)(2,1)S(1)}, u32[]{:S(2)}, u32[]{:S(2)}) collective-permute-start(bf16[512,512]{1,0:T(8,128)(2,1)S(1)} %get-tuple-element.27.refs_2_), channel_id=1, source_target_pairs={{0,4},{4,0},{8,12},{12,8},{16,20},{20,16},{24,28},{28,24},{1,5},{5... | collective-permute-start | bytes 1572872 | tf_op jit(solution)/shard_map/ppermute | solution.py:21
  90.8 26.5 %collective-permute-start.9 = (bf16[512,512]{1,0:T(8,128)(2,1)S(1)}, bf16[512,512]{1,0:T(8,128)(2,1)}, u32[]{:S(2)}, u32[]{:S(2)}) collective-permute-start(bf16[512,512]{1,0:T(8,128)(2,1)S(1)} %get-tuple-element.27.refs_2_), channel_id=1, source_target_pairs={{0,16},{4,20},{8,24},{12,28},{16,0},{20,4},{24,8},{28,12},{1,17},{... | collective-permute-start | bytes 1572872 | tf_op jit(solution)/shard_map/ppermute | solution.py:21
  92.2 22.0 %collective-permute-start.8 = (bf16[1,528,1024]{2,1,0:T(8,128)(2,1)}, bf16[1,528,1024]{2,1,0:T(8,128)(2,1)}, u32[]{:S(2)}, u32[]{:S(2)}) collective-permute-start(bf16[1,528,1024]{2,1,0:T(8,128)(2,1)} %bitcast.47), channel_id=1, source_target_pairs={{0,2},{1,3},{2,0},{3,1},{4,6},{5,7},{6,4},{7,5},{8,10},{9,11},{10,... | collective-permute-start | bytes 3244040 | tf_op jit(solution)/shard_map/ppermute | solution.py:21
  122.4 35.6 %collective-permute-start.15 = (bf16[512,512]{1,0:T(8,128)(2,1)}, bf16[512,512]{1,0:T(8,128)(2,1)}, u32[]{:S(2)}, u32[]{:S(2)}) collective-permute-start(bf16[512,512]{1,0:T(8,128)(2,1)} %collective-permute-done.10.refs_4_), channel_id=1, source_target_pairs={{0,4},{4,0},{8,12},{12,8},{16,20},{20,16},{24,28},{28,24},{1,5},{5... | collective-permute-start | bytes 1572872 | tf_op jit(solution)/shard_map/ppermute | solution.py:21
  123.7 34.3 %collective-permute-start.17 = (bf16[512,512]{1,0:T(8,128)(2,1)}, bf16[512,512]{1,0:T(8,128)(2,1)}, u32[]{:S(2)}, u32[]{:S(2)}) collective-permute-start(bf16[512,512]{1,0:T(8,128)(2,1)} %collective-permute-done.10.refs_4_), channel_id=1, source_target_pairs={{0,16},{4,20},{8,24},{12,28},{16,0},{20,4},{24,8},{28,12},{1,17},{... | collective-permute-start | bytes 1572872 | tf_op jit(solution)/shard_map/ppermute | solution.py:21
  124.2 33.8 %collective-permute-start.18 = (bf16[512,512]{1,0:T(8,128)(2,1)}, bf16[512,512]{1,0:T(8,128)(2,1)}, u32[]{:S(2)}, u32[]{:S(2)}) collective-permute-start(bf16[512,512]{1,0:T(8,128)(2,1)} %get-tuple-element.35), channel_id=1, source_target_pairs={{0,8},{4,12},{8,0},{12,4},{16,24},{20,28},{24,16},{28,20},{1,9},{5... | collective-permute-start | bytes 1572872 | tf_op jit(solution)/shard_map/ppermute | solution.py:21
  130.5 27.4 %collective-permute-start.16 = (bf16[512,512]{1,0:T(8,128)(2,1)}, bf16[512,512]{1,0:T(8,128)(2,1)}, u32[]{:S(2)}, u32[]{:S(2)}) collective-permute-start(bf16[512,512]{1,0:T(8,128)(2,1)} %collective-permute-done.9.refs_6_), channel_id=1, source_target_pairs={{0,4},{4,0},{8,12},{12,8},{16,20},{20,16},{24,28},{28,24},{1,5},{5... | collective-permute-start | bytes 1572872 | tf_op jit(solution)/shard_map/ppermute | solution.py:21
  158.0 25.3 %collective-permute-start.20 = (bf16[512,512]{1,0:T(8,128)(2,1)}, bf16[512,512]{1,0:T(8,128)(2,1)}, u32[]{:S(2)}, u32[]{:S(2)}) collective-permute-start(bf16[512,512]{1,0:T(8,128)(2,1)} %get-tuple-element.38), channel_id=1, source_target_pairs={{0,16},{4,20},{8,24},{12,28},{16,0},{20,4},{24,8},{28,12},{1,17},{... | collective-permute-start | bytes 1572872 | tf_op jit(solution)/shard_map/ppermute | solution.py:21
  158.2 25.1 %collective-permute-start.21 = (bf16[512,512]{1,0:T(8,128)(2,1)}, bf16[512,512]{1,0:T(8,128)(2,1)}, u32[]{:S(2)}, u32[]{:S(2)}) collective-permute-start(bf16[512,512]{1,0:T(8,128)(2,1)} %get-tuple-element.38), channel_id=1, source_target_pairs={{0,4},{4,0},{8,12},{12,8},{16,20},{20,16},{24,28},{28,24},{1,5},{5... | collective-permute-start | bytes 1572872 | tf_op jit(solution)/shard_map/ppermute | solution.py:21
  159.3 25.3 %collective-permute-start.19 = (bf16[512,512]{1,0:T(8,128)(2,1)}, bf16[512,512]{1,0:T(8,128)(2,1)}, u32[]{:S(2)}, u32[]{:S(2)}) collective-permute-start(bf16[512,512]{1,0:T(8,128)(2,1)} %collective-permute-done.17.refs_8_), channel_id=1, source_target_pairs={{0,4},{4,0},{8,12},{12,8},{16,20},{20,16},{24,28},{28,24},{1,5},{5... | collective-permute-start | bytes 1572872 | tf_op jit(solution)/shard_map/ppermute | solution.py:21
  186.2 26.4 %collective-permute-start.25 = (bf16[512,512]{1,0:T(8,128)(2,1)}, bf16[512,512]{1,0:T(8,128)(2,1)S(1)}, u32[]{:S(2)}, u32[]{:S(2)}) collective-permute-start(bf16[512,512]{1,0:T(8,128)(2,1)} %collective-permute-done.18), channel_id=1, source_target_pairs={{0,4},{4,0},{8,12},{12,8},{16,20},{20,16},{24,28},{28,24},{1,5},{5... | collective-permute-start | bytes 1572872 | tf_op jit(solution)/shard_map/ppermute | solution.py:21
  187.3 25.3 %collective-permute-start.24 = (bf16[512,512]{1,0:T(8,128)(2,1)}, bf16[512,512]{1,0:T(8,128)(2,1)S(1)}, u32[]{:S(2)}, u32[]{:S(2)}) collective-permute-start(bf16[512,512]{1,0:T(8,128)(2,1)} %collective-permute-done.20), channel_id=1, source_target_pairs={{0,4},{4,0},{8,12},{12,8},{16,20},{20,16},{24,28},{28,24},{1,5},{5... | collective-permute-start | bytes 1572872 | tf_op jit(solution)/shard_map/ppermute | solution.py:21
  201.3 19.7 %collective-permute-start.23 = (bf16[512,512]{1,0:T(8,128)(2,1)S(1)}, bf16[512,512]{1,0:T(8,128)(2,1)S(1)}, u32[]{:S(2)}, u32[]{:S(2)}) collective-permute-start(bf16[512,512]{1,0:T(8,128)(2,1)S(1)} %collective-permute-done.22), channel_id=1, source_target_pairs={{0,4},{4,0},{8,12},{12,8},{16,20},{20,16},{24,28},{28,24},{1,5},{5... | collective-permute-start | bytes 1572872 | tf_op jit(solution)/shard_map/ppermute | solution.py:21
  204.8 18.8 %collective-permute-start.29 = (bf16[1024,1024]{0,1:T(8,128)(2,1)S(1)}, bf16[1024,1024]{0,1:T(8,128)(2,1)S(1)}, u32[]{:S(2)}, u32[]{:S(2)}) collective-permute-start(bf16[1024,1024]{0,1:T(8,128)(2,1)S(1)} %convolution_convert_fusion), channel_id=1, source_target_pairs={{0,1},{1,0},{2,3},{3,2},{4,5},{5,4},{6,7},{7,6},{8,9},{9,8},{10,11... | collective-permute-start | bytes 6291464 | tf_op jit(solution)/shard_map/ppermute | solution.py:21
  225.9 25.6 %collective-permute-start.30 = (bf16[1024,512]{0,1:T(8,128)(2,1)S(1)}, bf16[1024,512]{0,1:T(8,128)(2,1)S(1)}, u32[]{:S(2)}, u32[]{:S(2)}) collective-permute-start(bf16[1024,512]{0,1:T(8,128)(2,1)S(1)} %fusion.1), channel_id=1, source_target_pairs={{0,2},{1,3},{2,0},{3,1},{4,6},{5,7},{6,4},{7,5},{8,10},{9,11},{10,... | collective-permute-start | bytes 3145736 | tf_op jit(solution)/shard_map/ppermute | solution.py:21
  229.0 43.5 %collective-permute-start.27 = (bf16[512,1024]{0,1:T(8,128)(2,1)S(1)}, bf16[512,1024]{0,1:T(8,128)(2,1)S(1)}, u32[]{:S(2)}, u32[]{:S(2)}) collective-permute-start(bf16[512,1024]{0,1:T(8,128)(2,1)S(1)} %fusion.3), channel_id=1, source_target_pairs={{0,8},{4,12},{8,0},{12,4},{16,24},{20,28},{24,16},{28,20},{1,9},{5... | collective-permute-start | bytes 3145736 | tf_op jit(solution)/shard_map/ppermute | solution.py:21
  254.4 35.0 %collective-permute-start.31 = (bf16[512,512]{0,1:T(8,128)(2,1)}, bf16[512,512]{0,1:T(8,128)(2,1)}, u32[]{:S(2)}, u32[]{:S(2)}) collective-permute-start(bf16[512,512]{0,1:T(8,128)(2,1)} %slice.375), channel_id=1, source_target_pairs={{0,8},{4,12},{8,0},{12,4},{16,24},{20,28},{24,16},{28,20},{1,9},{5... | collective-permute-start | bytes 1572872 | tf_op jit(solution)/shard_map/ppermute | solution.py:21
  (89 other events, 938.0 us)
Sparse Core Ops, SparseCore 0:
  20.9 71.8 all-gather.1

commit v5 on v4

--- a/solution.py
+++ b/solution.py
@@ -34,15 +34,16 @@
     return lax.optimization_barrier((value, *others))[0]
 
 
-ROUNDS = (
-    (("x", 4), ("x", 6), ("x", 3), ("x", 5), ("t", 0)),
-    (("z", 4), ("z", 2), ("x", 7), ("z", 1), ("t", 1)),
-    (("z", 6), ("z", 3), ("z", 5), ("w", 2), ("t", 2)),
-    (("w", 4), ("z", 7), ("w", 1)),
-    (("w", 6), ("w", 3), ("w", 5)),
+ORDER = (
+    ("x6 z4 x3 x5", "x1 x2 x4 z1"),
+    ("t1 z2 w1 w4", "x3 x5 x6 t0"),
+    ("x7 w2 z5", "z2 w1 z4"),
+    ("t2 z6 z3 w5", "t1 x7 w2 z5 w4"),
+    ("w6", "w4 w2"),
+    ("z7", "z6 z3 w5 t2"),
+    ("w3", "z7"),
 )
-WAITS = {send: ROUNDS[i] for i in range(len(ROUNDS) - 1) for send in ROUNDS[i + 1]}
-WAITS[("t", 0)] = (("x", 2),)
+WAITS = {send: waits.split() for sends, waits in ORDER for send in sends.split()}
 
 
 class Sends:
@@ -51,13 +52,13 @@
         self.made = {}
 
     def get(self, kind, mask):
-        name = (kind, mask)
+        name = f"{kind}{mask}"
         if name not in self.made:
             self.made[name] = self.tokens(mask) if kind == "t" else self.piece(kind, mask)
         return self.made[name]
 
-    def waiting(self, name, value):
-        others = [self.get(*other) for other in WAITS.get(name, ())]
+    def waiting(self, kind, mask, value):
+        others = [self.get(name[0], int(name[1:])) for name in WAITS.get(f"{kind}{mask}", ())]
         return after(value, *others) if others else value
 
     def piece(self, kind, mask):
@@ -68,20 +69,20 @@
         else:
             bit = 1 if mask & 1 else 1 << (mask.bit_length() - 1)
             value = self.get(kind, mask ^ bit)
-        return swapped(self.waiting((kind, mask), value), "seq", bit)
+        return swapped(self.waiting(kind, mask, value), "seq", bit)
 
     def tokens(self, step):
         if step == 0:
-            return swapped(self.waiting(("t", 0), self.quarter), "seq", PAIR)
+            return swapped(self.waiting("t", 0, self.quarter), "seq", PAIR)
         if step == 1:
             value = self.get("t", 0)[None]
             bit = lax.axis_size("head") // 2
             while bit > 1:
-                got = swapped(self.waiting(("t", 1), value), "head", bit)
+                got = swapped(self.waiting("t", 1, value), "head", bit)
                 value = jnp.concatenate([value, got])
                 bit //= 2
             return value
-        return swapped(self.waiting(("t", 2), self.get("t", 1)), "head", 1)
+        return swapped(self.waiting("t", 2, self.get("t", 1)), "head", 1)
 
 
 def natural(value, axis_name, bit, axis):
@@ -335,18 +336,17 @@
     flat_w = lax.optimization_barrier(w_xz.reshape(depth, -1))
     full = flat_w.shape[1] // 2
     x_w, z_w = flat_w[:, :full], flat_w[:, full:]
-    high = max(b for b in (PAIR, seq_count // 2))
     own = {
-        "x": jnp.concatenate([cut(x_w, half, chans, 1), extra], axis=0),
+        "x": jnp.concatenate([cut(x_w, half, chans, 1), extra]),
         "z": cut(z_w, half, chans, 1),
         "w": cut(w_out, half, chans, 0),
     }
-    given_away = {
-        "x": jnp.concatenate([cut(x_w, 1 - half, chans, 1), extra], axis=0),
+    other_half = {
+        "x": jnp.concatenate([cut(x_w, 1 - half, chans, 1), extra]),
         "z": cut(z_w, 1 - half, chans, 1),
         "w": cut(w_out, 1 - half, chans, 0),
     }
-    sends = Sends(own, given_away, jnp.concatenate([cut(tokens, mine, share, 1), given], axis=0))
+    sends = Sends(own, other_half, jnp.concatenate([cut(tokens, mine, share, 1), given]))
     masks = list(range(seq_count))
     x_pieces, z_pieces, out_pieces = [{mask: sends.get(kind, mask) for mask in masks} for kind in "xzw"]
 
@@ -400,7 +400,7 @@
         return jnp.pad(tail, ((HALO - tail.shape[0], 0), (0, 0)))
 
     x_conv, bc_conv, added = front(
-        first,
+        after(first, sends.get("w", PAIR)),
         x_pre,
         bc_pre,
         padded(cut(tail_x, half, chans, 1)),
@@ -452,7 +452,7 @@
         grown,
         jnp.repeat(cut(skip_gain, half, heads, 0), head_dim)[None, :],
         z_val,
-        cut(norm_gain, half, chans, 0)[None, :],
+        after(cut(norm_gain, half, chans, 0)[None, :], out_pieces[PAIR | 1]),
     )
 
     per = seq_count // head_count
@@ -482,26 +482,32 @@
     def swap_pair(value):
         return swapped(value.astype(BF16), "seq", PAIR).astype(F32)
 
+    squares = squares[0, :, 0] + swapped(squares[1, :, 0], "seq", PAIR)
+    paired = squares
+    bit = head_count // 2
+    while bit >= 1:
+        upper = squares
+        squares = squares + swapped(squares, "head", bit)
+        bit //= 2
+    scale = lax.rsqrt(squares / inner + 1e-05)[:, None]
+
     done = {}
-    lows = {low: by_destination(low) for low in range(per)}
-    got_far = {low: send_far(lows[low]) for low in range(per)}
     for low in range(0, per, 2):
-        parts = columns_added([dot(flat, w) for w in lows[low][::2]], got_far[low])
+        weights = by_destination(low)
+        got_far = send_far(weights)
+        parts = columns_added([dot(flat, w) for w in weights[::2]], got_far)
+        parts = [after(part, upper) if i else part for i, part in enumerate(parts)]
         whole = fold_head(parts)
         done[low] = whole[:rows] + swap_pair(whole[rows:])
+    flat = after(flat, paired)
     for low in range(1, per, 2):
-        near = lows[low][::2]
-        away = swap_pair(dot(gated[1], jnp.concatenate(near, axis=1)) + got_far[low][rows:])
-        here = columns_added([dot(gated[0], w) for w in near], got_far[low][:rows])
+        weights = by_destination(low)
+        got_far = send_far(weights)
+        near = weights[::2]
+        away = swap_pair(dot(gated[1], jnp.concatenate(near, axis=1)) + got_far[rows:])
+        here = columns_added([dot(gated[0], w) for w in near], got_far[:rows])
         done[low] = fold_head(columns_added(here, away))
 
-    squares = after(squares[:, :, 0], got_far[per - 1])
-    squares = squares[0] + swapped(squares[1], "seq", PAIR)
-    bit = 1
-    while bit < head_count:
-        squares = squares + swapped(squares, "head", bit)
-        bit *= 2
-    scale = lax.rsqrt(squares / inner + 1e-05)[:, None]
     result = by_xor([done[low] for low in range(per)], me % per)
     return jnp.concatenate([(piece * scale).astype(BF16) for piece in result], axis=1)
 

time: 302 us -> 292 us (0.967)
  starting transfers between devices: 73.6 us -> 39.6 us
  waiting for transfers between devices: 94.9 us -> 114 us
  local copies, waits for them, and re-layouts: 41.4 us -> 49.7 us
  other arithmetic: 28.5 us -> 25 us
    ppermute x34, starting transfers between devices: 71.4 us -> 35.9 us  [swapped(): return lax.ppermute(value, axis, [(i, i ^ bit) for i in range(size)])]
    ppermute x34, waiting for transfers between devices: 94.9 us -> 114 us  [swapped(): return lax.ppermute(value, axis, [(i, i ^ bit) for i in range(size)])]
    unnamed x161 -> x125, local copies, waits for them, and re-layouts: 8.08 us -> 13.2 us
  transfers between devices with their start and end apart: 36 -> 36, of which waited for: 15 -> 16; matrix products, arithmetic and copies ran while one was open for 22% -> 24% of each run, Pallas kernels for 12% -> 12%
where the time goes in v5:
time: 292 us; the launch traced here: 291 us
  waiting for transfers between devices  114 us (39%)
  local copies, waits for them, and re-layouts  49.7 us (17%)
  starting transfers between devices  39.6 us (14%)
  Pallas kernels  35.9 us (12%)
  other arithmetic  25 us (9%)
  between operations  14.5 us (5%)
  matrix products  11.5 us (4%)
    ppermute x34, waiting for transfers between devices, swapped(): return lax.ppermute(value, axis, [(i, i ^ bit) for i in range(size)])  114 us
    ppermute x34, starting transfers between devices, swapped(): return lax.ppermute(value, axis, [(i, i ^ bit) for i in range(size)])  35.9 us
    pallas_call x3, Pallas kernels, project(): pl.pallas_call(functools.partial(project_kernel, depth, halo is not None,...  23.9 us
    unnamed x125, local copies, waits for them, and re-layouts  13.2 us
    dot_general x7, matrix products, dot(): return jnp.dot(a, b, preferred_element_type=F32)  11.5 us
    dynamic_slice x10, local copies, waits for them, and re-layouts, cut(): return lax.dynamic_slice_in_dim(value, index * size, size, axis)  9.33 us
  transfers between devices with their start and end apart: 36, of which 16 were waited for; matrix products, arithmetic and copies ran while one was open for 24% of the time, Pallas kernels for 12%

profile of v5, /device:TPU:0, one launch (start us, length us, event | category | flops | bytes accessed | tf_op | source)
XLA Modules:
  0.0 290.5 jit_solution(14828170002551128459)
XLA Ops:
  12.2 2.9 %collective-permute-start.1 = (bf16[544,512]{1,0:T(8,128)(2,1)S(1)}, bf16[544,512]{1,0:T(8,128)(2,1)S(1)}, u32[]{:S(2)}, u32[]{:S(2)}) collective-permute-start(bf16[544,512]{1,0:T(8,128)(2,1)S(1)} %get-tuple-element.98.refs_3_), channel_id=1, source_target_pairs={{0,4},{4,0},{8,12},{12,8},{16,20},{20,16},{24,28},{28,24},{1,5},{5... | collective-permute-start | bytes 1671176 | tf_op jit(solution)/shard_map/ppermute | solution.py:21
  15.1 2.6 collective-permute-start.2
  40.9 4.4 %collective-permute-done.refs_5_ = bf16[544,512]{1,0:T(8,128)(2,1)} collective-permute-done((bf16[544,512]{1,0:T(8,128)(2,1)}, bf16[544,512]{1,0:T(8,128)(2,1)}, u32[]{:S(2)}, u32[]{:S(2)}) %collective-permute-start) | collective-permute-done | bytes 557088 | tf_op jit(solution)/shard_map/ppermute | solution.py:21
  46.3 2.4 collective-permute-start.10
  52.5 38.2 %collective-permute-done.7 = bf16[528,1024]{1,0:T(8,128)(2,1)} collective-permute-done((bf16[528,1024]{1,0:T(8,128)(2,1)}, bf16[528,1024]{1,0:T(8,128)(2,1)}, u32[]{:S(2)}, u32[]{:S(2)}) %collective-permute-start.7) | collective-permute-done | bytes 1081376 | tf_op jit(solution)/shard_map/ppermute | solution.py:21
  92.2 2.3 reduce-window.6
  99.3 3.0 %copy.38.dec_ref = f32[2,512,512]{2,1,0:T(8,128)} copy(f32[2,512,512]{1,2,0:T(8,128)} %bitcast.238) | data formatting | bytes 4194304 | tf_op jit(solution)/shard_map/reshape | solution.py:383
  104.0 3.2 %copy.49.e_ref = f32[2,512,512]{2,1,0:T(8,128)} copy(f32[2,512,512]{1,2,0:T(8,128)} %bitcast.239) | data formatting | bytes 4194304 | tf_op jit(solution)/shard_map/reshape | solution.py:386
  120.2 14.3 %collective-permute-done.11 = bf16[512,512]{1,0:T(8,128)(2,1)} collective-permute-done((bf16[512,512]{1,0:T(8,128)(2,1)S(1)}, bf16[512,512]{1,0:T(8,128)(2,1)}, u32[]{:S(2)}, u32[]{:S(2)}) %collective-permute-start.11) | collective-permute-done | bytes 524320 | tf_op jit(solution)/shard_map/ppermute | solution.py:21
  134.5 2.6 collective-permute-done.15
  138.8 3.2 %pad_maximum_fusion.1 = bf16[2,528,1024]{2,1,0:T(8,128)(2,1)} fusion(bf16[1,528,1024]{2,1,0:T(8,128)(2,1)S(1)} %collective-permute-done.13, bf16[1,528,1024]{2,1,0:T(8,128)(2,1)} %bitcast.47), kind=kLoop, calls=%fused_computation.2 | loop fusion | flops 1081344 | bytes 4325376 | tf_op jit(solution)/shard_map/concatenate | solution.py:82
  147.3 2.6 collective-permute-done.16
  150.0 3.8 %pad_maximum_fusion.refs_2_.refs_1_ = bf16[4,528,1024]{2,1,0:T(8,128)(2,1)} fusion(bf16[2,528,1024]{2,1,0:T(8,128)(2,1)} %collective-permute-done.16, bf16[1,528,1024]{2,1,0:T(8,128)(2,1)} %copy-done.26, bf16[1,528,1024]{2,1,0:T(8,128)(2,1)} %bitcast.47), kind=kLoop, calls=%fused_computation | loop fusion | flops 4325376 | bytes 8650752 | tf_op jit(solution)/shard_map/concatenate | solution.py:353
  154.8 9.3 %project.3.x_ref = bf16[2,528,512]{2,1,0:T(8,128)(2,1)S(1)} custom-call(s32[3,8]{1,0:T(4,128)S(1)} %copy-done.18, bf16[32,4096]{1,0:T(8,128)(2,1)S(1)} %fusion.42.refs_0_, bf16[512,4096]{1,0:T(8,128)(2,1)} %refs_0_.1, bf16[4,528,1024]{2,1,0:T(8,128)(2,1)} %pad_maximum_fusion.refs_2_.refs_1_, bf16[544,512]{1,0:T(8,128)(2,1)S(1)} %get-tuple-element.98.refs_3_, ...), custom_call_target="tpu_custom_call" | custom-call | flops 1 | bytes 1 | tf_op jit(solution)/shard_map/project/pallas_call | solution.py:230
  165.7 6.2 %project.4.bc_ref = bf16[2,528,256]{2,1,0:T(8,128)(2,1)S(1)} custom-call(s32[3,8]{1,0:T(4,128)S(1)} %copy-done.18, bf16[32,4096]{1,0:T(8,128)(2,1)S(1)} %fusion.42.refs_0_, bf16[512,4096]{1,0:T(8,128)(2,1)} %refs_0_.1, bf16[4,528,1024]{2,1,0:T(8,128)(2,1)} %pad_maximum_fusion.refs_2_.refs_1_, bf16[4096,256]{1,0:T(8,128)(2,1)S(1)} %copy-done.5), custom_call_target="tpu_custom_call" | custom-call | flops 1 | bytes 1 | tf_op jit(solution)/shard_map/project/pallas_call | solution.py:230
  172.0 4.8 %front.1 = (bf16[2,512,512]{2,1,0:T(8,128)(2,1)S(1)}, bf16[2,512,256]{2,1,0:T(8,128)(2,1)S(1)}, f32[2,2,128,512]{3,2,1,0:T(8,128)S(1)}) custom-call(s32[2]{0:T(128)S(1)} %copy-done.22, bf16[2,528,512]{2,1,0:T(8,128)(2,1)S(1)} %project.3.x_ref, bf16[2,528,256]{2,1,0:T(8,128)(2,1)S(1)} %project.4.bc_ref, bf16[16,512]{1,0:T(8,128)(2,1)S(1)} %pad.27.tx_ref, ...), custom_call_target="tpu_custom_call" | custom-call | flops 1 | bytes 1 | tf_op jit(solution)/shard_map/front/pallas_call | solution.py:187
  187.2 3.7 %collective-permute-start.18 = (bf16[128,512]{1,0:T(8,128)(2,1)S(1)}, bf16[128,512]{1,0:T(8,128)(2,1)S(1)}, u32[]{:S(2)}, u32[]{:S(2)}) collective-permute-start(bf16[128,512]{1,0:T(8,128)(2,1)S(1)} %add_convert_fusion), channel_id=1, source_target_pairs={{0,16},{4,20},{8,24},{12,28},{1,17},{5,21},{9,25},{13,29},{2,18},{... | collective-permute-start | bytes 393224 | tf_op jit(solution)/shard_map/ppermute | solution.py:26
  192.3 3.1 %intra.1.y_ref = f32[2,512,512]{2,1,0:T(8,128)S(1)} custom-call(bf16[2,512,512]{2,1,0:T(8,128)(2,1)S(1)} %get-tuple-element.40.x_ref, bf16[2,512,256]{2,1,0:T(8,128)(2,1)S(1)} %copy-done.7, f32[2,512,8]{2,1,0:T(8,128)S(1)} %copy-done.8, f32[2,2,8,256]{3,2,1,0:T(8,128)S(1)} %copy-done.15), custom_call_target="tpu_custom_call" | custom-call | flops 1 | bytes 1 | tf_op jit(solution)/shard_map/intra/pallas_call | solution.py:250
  195.6 13.0 %collective-permute-done.22.refs_9_ = bf16[512,512]{1,0:T(8,128)(2,1)S(1)} collective-permute-done((bf16[512,512]{1,0:T(8,128)(2,1)}, bf16[512,512]{1,0:T(8,128)(2,1)S(1)}, u32[]{:S(2)}, u32[]{:S(2)}) %collective-permute-start.22) | collective-permute-done | bytes 524320 | tf_op jit(solution)/shard_map/ppermute | solution.py:21
  211.8 8.5 %project.5.z_ref = bf16[2,512,512]{2,1,0:T(8,128)(2,1)S(1)} custom-call(s32[3,8]{1,0:T(4,128)S(1)} %copy-done.18, bf16[512,4096]{1,0:T(8,128)(2,1)} %refs_0_.1, bf16[4,528,1024]{2,1,0:T(8,128)(2,1)} %pad_maximum_fusion.refs_2_.refs_1_, bf16[512,512]{1,0:T(8,128)(2,1)S(1)} %copy-done.4, bf16[512,512]{1,0:T(8,128)(2,1)S(1)} %copy-done.12, ...), custom_call_target="tpu_custom_call" | custom-call | flops 1 | bytes 1 | tf_op jit(solution)/shard_map/project/pallas_call | solution.py:230
  222.0 4.0 %gate.1 = (bf16[2,512,512]{2,1,0:T(8,128)(2,1)S(1)}, f32[2,512,128]{2,1,0:T(8,128)S(1)}) custom-call(f32[2,512,512]{2,1,0:T(8,128)} %copy-done.2, bf16[2,512,512]{2,1,0:T(8,128)(2,1)S(1)} %get-tuple-element.40.x_ref, bf16[2,512,256]{2,1,0:T(8,128)(2,1)S(1)} %copy-done.7, f32[2,2,128,512]{3,2,1,0:T(8,128)S(1)} %pad_maximum_fusion.2.st_ref, ...), custom_call_target="tpu_custom_call" | custom-call | flops 1 | bytes 1 | tf_op jit(solution)/shard_map/gate/pallas_call | solution.py:269
  241.7 20.1 %collective-permute-done.32 = bf16[1024,512]{0,1:T(8,128)(2,1)S(1)} collective-permute-done((bf16[1024,512]{0,1:T(8,128)(2,1)S(1)}, bf16[1024,512]{0,1:T(8,128)(2,1)S(1)}, u32[]{:S(2)}, u32[]{:S(2)}) %collective-permute-start.32) | collective-permute-done | bytes 1048608 | tf_op jit(solution)/shard_map/ppermute | solution.py:21
  270.3 7.1 %collective-permute-done.33 = bf16[512,512]{0,1:T(8,128)(2,1)} collective-permute-done((bf16[512,512]{0,1:T(8,128)(2,1)}, bf16[512,512]{0,1:T(8,128)(2,1)}, u32[]{:S(2)}, u32[]{:S(2)}) %collective-permute-start.33) | collective-permute-done | bytes 524320 | tf_op jit(solution)/shard_map/ppermute | solution.py:21
  279.5 2.7 multiply_convert_fusion.1
  (336 shorter events, 108.0 us)
Async XLA Ops:
  6.5 157.6 %all-gather.2.cloned.1.call-start = ((), (), s32[]{:S(2)}) async-start(), calls=%async_computation | async-start | bytes 2162688 | tf_op jit(solution)/shard_map/all_gather | solution.py:370
  12.2 33.2 %collective-permute-start.1 = (bf16[544,512]{1,0:T(8,128)(2,1)S(1)}, bf16[544,512]{1,0:T(8,128)(2,1)S(1)}, u32[]{:S(2)}, u32[]{:S(2)}) collective-permute-start(bf16[544,512]{1,0:T(8,128)(2,1)S(1)} %get-tuple-element.98.refs_3_), channel_id=1, source_target_pairs={{0,4},{4,0},{8,12},{12,8},{16,20},{20,16},{24,28},{28,24},{1,5},{5... | collective-permute-start | bytes 1671176 | tf_op jit(solution)/shard_map/ppermute | solution.py:21
  15.1 30.2 %collective-permute-start.2 = (bf16[544,512]{1,0:T(8,128)(2,1)S(1)}, bf16[544,512]{1,0:T(8,128)(2,1)S(1)}, u32[]{:S(2)}, u32[]{:S(2)}) collective-permute-start(bf16[544,512]{1,0:T(8,128)(2,1)S(1)} %get-tuple-element.98.refs_3_), channel_id=1, source_target_pairs={{0,16},{4,20},{8,24},{12,28},{16,0},{20,4},{24,8},{28,12},{1,17},{... | collective-permute-start | bytes 1671176 | tf_op jit(solution)/shard_map/ppermute | solution.py:21
  17.7 27.6 %collective-permute-start = (bf16[544,512]{1,0:T(8,128)(2,1)}, bf16[544,512]{1,0:T(8,128)(2,1)}, u32[]{:S(2)}, u32[]{:S(2)}) collective-permute-start(bf16[544,512]{1,0:T(8,128)(2,1)} %get-tuple-element.99), channel_id=1, source_target_pairs={{0,8},{4,12},{8,0},{12,4},{16,24},{20,28},{24,16},{28,20},{1,9},{5... | collective-permute-start | bytes 1671176 | tf_op jit(solution)/shard_map/ppermute | solution.py:21
  20.2 20.7 %collective-permute-start.3 = (bf16[512,512]{1,0:T(8,128)(2,1)S(1)}, bf16[512,512]{1,0:T(8,128)(2,1)S(1)}, u32[]{:S(2)}, u32[]{:S(2)}) collective-permute-start(bf16[512,512]{1,0:T(8,128)(2,1)S(1)} %get-tuple-element.33.refs_2_), channel_id=1, source_target_pairs={{0,4},{4,0},{8,12},{12,8},{16,20},{20,16},{24,28},{28,24},{1,5},{5... | collective-permute-start | bytes 1572872 | tf_op jit(solution)/shard_map/ppermute | solution.py:21
  23.8 66.9 %collective-permute-start.7 = (bf16[528,1024]{1,0:T(8,128)(2,1)}, bf16[528,1024]{1,0:T(8,128)(2,1)}, u32[]{:S(2)}, u32[]{:S(2)}) collective-permute-start(bf16[528,1024]{1,0:T(8,128)(2,1)} %fusion.7), channel_id=1, source_target_pairs={{0,8},{4,12},{8,0},{12,4},{16,24},{20,28},{24,16},{28,20},{1,9},{5... | collective-permute-start | bytes 3244040 | tf_op jit(solution)/shard_map/ppermute | solution.py:21
  45.3 50.6 %collective-permute-start.4 = (bf16[544,512]{1,0:T(8,128)(2,1)}, bf16[544,512]{1,0:T(8,128)(2,1)}, u32[]{:S(2)}, u32[]{:S(2)}) collective-permute-start(bf16[544,512]{1,0:T(8,128)(2,1)} %collective-permute-done.refs_5_), channel_id=1, source_target_pairs={{0,4},{4,0},{8,12},{12,8},{16,20},{20,16},{24,28},{28,24},{1,5},{5... | collective-permute-start | bytes 1671176 | tf_op jit(solution)/shard_map/ppermute | solution.py:21
  45.8 50.1 %collective-permute-start.6 = (bf16[544,512]{1,0:T(8,128)(2,1)}, bf16[544,512]{1,0:T(8,128)(2,1)}, u32[]{:S(2)}, u32[]{:S(2)}) collective-permute-start(bf16[544,512]{1,0:T(8,128)(2,1)} %collective-permute-done.refs_5_), channel_id=1, source_target_pairs={{0,16},{4,20},{8,24},{12,28},{16,0},{20,4},{24,8},{28,12},{1,17},{... | collective-permute-start | bytes 1671176 | tf_op jit(solution)/shard_map/ppermute | solution.py:21
  46.3 65.2 %collective-permute-start.10 = (bf16[512,512]{1,0:T(8,128)(2,1)S(1)}, bf16[512,512]{1,0:T(8,128)(2,1)}, u32[]{:S(2)}, u32[]{:S(2)}) collective-permute-start(bf16[512,512]{1,0:T(8,128)(2,1)S(1)} %get-tuple-element.33.refs_2_), channel_id=1, source_target_pairs={{0,16},{4,20},{8,24},{12,28},{16,0},{20,4},{24,8},{28,12},{1,17},{... | collective-permute-start | bytes 1572872 | tf_op jit(solution)/shard_map/ppermute | solution.py:21
  48.7 47.2 %collective-permute-start.5 = (bf16[544,512]{1,0:T(8,128)(2,1)S(1)}, bf16[544,512]{1,0:T(8,128)(2,1)}, u32[]{:S(2)}, u32[]{:S(2)}) collective-permute-start(bf16[544,512]{1,0:T(8,128)(2,1)S(1)} %collective-permute-done.2.refs_7_), channel_id=1, source_target_pairs={{0,4},{4,0},{8,12},{12,8},{16,20},{20,16},{24,28},{28,24},{1,5},{5... | collective-permute-start | bytes 1671176 | tf_op jit(solution)/shard_map/ppermute | solution.py:21
  96.0 16.6 %collective-permute-start.8 = (bf16[512,512]{1,0:T(8,128)(2,1)}, bf16[512,512]{1,0:T(8,128)(2,1)}, u32[]{:S(2)}, u32[]{:S(2)}) collective-permute-start(bf16[512,512]{1,0:T(8,128)(2,1)} %get-tuple-element.31), channel_id=1, source_target_pairs={{0,8},{4,12},{8,0},{12,4},{16,24},{20,28},{24,16},{28,20},{1,9},{5... | collective-permute-start | bytes 1572872 | tf_op jit(solution)/shard_map/ppermute | solution.py:21
  107.2 31.7 %collective-permute-start.13 = (bf16[1,528,1024]{2,1,0:T(8,128)(2,1)}, bf16[1,528,1024]{2,1,0:T(8,128)(2,1)S(1)}, u32[]{:S(2)}, u32[]{:S(2)}) collective-permute-start(bf16[1,528,1024]{2,1,0:T(8,128)(2,1)} %bitcast.47), channel_id=1, source_target_pairs={{0,2},{1,3},{2,0},{3,1},{4,6},{5,7},{6,4},{7,5},{8,10},{9,11},{10,... | collective-permute-start | bytes 3244040 | tf_op jit(solution)/shard_map/ppermute | solution.py:21
  109.2 27.9 %collective-permute-start.15 = (bf16[512,512]{1,0:T(8,128)(2,1)}, bf16[512,512]{1,0:T(8,128)(2,1)}, u32[]{:S(2)}, u32[]{:S(2)}) collective-permute-start(bf16[512,512]{1,0:T(8,128)(2,1)} %get-tuple-element.32), channel_id=1, source_target_pairs={{0,16},{4,20},{8,24},{12,28},{16,0},{20,4},{24,8},{28,12},{1,17},{... | collective-permute-start | bytes 1572872 | tf_op jit(solution)/shard_map/ppermute | solution.py:21
  112.6 21.9 %collective-permute-start.11 = (bf16[512,512]{1,0:T(8,128)(2,1)S(1)}, bf16[512,512]{1,0:T(8,128)(2,1)}, u32[]{:S(2)}, u32[]{:S(2)}) collective-permute-start(bf16[512,512]{1,0:T(8,128)(2,1)S(1)} %copy-done.31), channel_id=1, source_target_pairs={{0,8},{4,12},{8,0},{12,4},{16,24},{20,28},{24,16},{28,20},{1,9},{5... | collective-permute-start | bytes 1572872 | tf_op jit(solution)/shard_map/ppermute | solution.py:21
  115.4 26.7 %collective-permute-start.14 = (bf16[512,512]{1,0:T(8,128)(2,1)}, bf16[512,512]{1,0:T(8,128)(2,1)S(1)}, u32[]{:S(2)}, u32[]{:S(2)}) collective-permute-start(bf16[512,512]{1,0:T(8,128)(2,1)} %collective-permute-done.10.refs_6_), channel_id=1, source_target_pairs={{0,4},{4,0},{8,12},{12,8},{16,20},{20,16},{24,28},{28,24},{1,5},{5... | collective-permute-start | bytes 1572872 | tf_op jit(solution)/shard_map/ppermute | solution.py:21
  117.1 24.9 %collective-permute-start.12 = (bf16[544,512]{1,0:T(8,128)(2,1)}, bf16[544,512]{1,0:T(8,128)(2,1)S(1)}, u32[]{:S(2)}, u32[]{:S(2)}) collective-permute-start(bf16[544,512]{1,0:T(8,128)(2,1)} %collective-permute-done.6.refs_9_), channel_id=1, source_target_pairs={{0,4},{4,0},{8,12},{12,8},{16,20},{20,16},{24,28},{28,24},{1,5},{5... | collective-permute-start | bytes 1671176 | tf_op jit(solution)/shard_map/ppermute | solution.py:21
  137.1 44.5 %collective-permute-start.24 = (bf16[512,512]{1,0:T(8,128)(2,1)}, bf16[512,512]{1,0:T(8,128)(2,1)}, u32[]{:S(2)}, u32[]{:S(2)}) collective-permute-start(bf16[512,512]{1,0:T(8,128)(2,1)} %collective-permute-done.11), channel_id=1, source_target_pairs={{0,16},{4,20},{8,24},{12,28},{16,0},{20,4},{24,8},{28,12},{1,17},{... | collective-permute-start | bytes 1572872 | tf_op jit(solution)/shard_map/ppermute | solution.py:21
  142.0 40.0 %collective-permute-start.19 = (bf16[512,512]{1,0:T(8,128)(2,1)}, bf16[512,512]{1,0:T(8,128)(2,1)}, u32[]{:S(2)}, u32[]{:S(2)}) collective-permute-start(bf16[512,512]{1,0:T(8,128)(2,1)} %collective-permute-done.8.refs_4_), channel_id=1, source_target_pairs={{0,4},{4,0},{8,12},{12,8},{16,20},{20,16},{24,28},{28,24},{1,5},{5... | collective-permute-start | bytes 1572872 | tf_op jit(solution)/shard_map/ppermute | solution.py:21
  143.8 40.5 %collective-permute-start.20 = (bf16[512,512]{1,0:T(8,128)(2,1)}, bf16[512,512]{1,0:T(8,128)(2,1)}, u32[]{:S(2)}, u32[]{:S(2)}) collective-permute-start(bf16[512,512]{1,0:T(8,128)(2,1)} %collective-permute-done.8.refs_4_), channel_id=1, source_target_pairs={{0,16},{4,20},{8,24},{12,28},{16,0},{20,4},{24,8},{28,12},{1,17},{... | collective-permute-start | bytes 1572872 | tf_op jit(solution)/shard_map/ppermute | solution.py:21
  145.0 37.1 %collective-permute-start.21 = (bf16[512,512]{1,0:T(8,128)(2,1)}, bf16[512,512]{1,0:T(8,128)(2,1)}, u32[]{:S(2)}, u32[]{:S(2)}) collective-permute-start(bf16[512,512]{1,0:T(8,128)(2,1)} %collective-permute-done.15), channel_id=1, source_target_pairs={{0,4},{4,0},{8,12},{12,8},{16,20},{20,16},{24,28},{28,24},{1,5},{5... | collective-permute-start | bytes 1572872 | tf_op jit(solution)/shard_map/ppermute | solution.py:21
  181.6 46.5 %collective-permute-start.25 = (bf16[512,512]{1,0:T(8,128)(2,1)}, bf16[512,512]{1,0:T(8,128)(2,1)S(1)}, u32[]{:S(2)}, u32[]{:S(2)}) collective-permute-start(bf16[512,512]{1,0:T(8,128)(2,1)} %collective-permute-done.24), channel_id=1, source_target_pairs={{0,4},{4,0},{8,12},{12,8},{16,20},{20,16},{24,28},{28,24},{1,5},{5... | collective-permute-start | bytes 1572872 | tf_op jit(solution)/shard_map/ppermute | solution.py:21
  184.3 24.3 %collective-permute-start.22 = (bf16[512,512]{1,0:T(8,128)(2,1)}, bf16[512,512]{1,0:T(8,128)(2,1)S(1)}, u32[]{:S(2)}, u32[]{:S(2)}) collective-permute-start(bf16[512,512]{1,0:T(8,128)(2,1)} %collective-permute-done.20.refs_8_), channel_id=1, source_target_pairs={{0,4},{4,0},{8,12},{12,8},{16,20},{20,16},{24,28},{28,24},{1,5},{5... | collective-permute-start | bytes 1572872 | tf_op jit(solution)/shard_map/ppermute | solution.py:21
  237.4 24.4 %collective-permute-start.32 = (bf16[1024,512]{0,1:T(8,128)(2,1)S(1)}, bf16[1024,512]{0,1:T(8,128)(2,1)S(1)}, u32[]{:S(2)}, u32[]{:S(2)}) collective-permute-start(bf16[1024,512]{0,1:T(8,128)(2,1)S(1)} %slice_add_fusion), channel_id=1, source_target_pairs={{0,2},{1,3},{2,0},{3,1},{4,6},{5,7},{6,4},{7,5},{8,10},{9,11},{10,... | collective-permute-start | bytes 3145736 | tf_op jit(solution)/shard_map/ppermute | solution.py:21
  240.2 25.8 %collective-permute-start.28 = (bf16[512,1024]{0,1:T(8,128)(2,1)S(1)}, bf16[512,1024]{0,1:T(8,128)(2,1)S(1)}, u32[]{:S(2)}, u32[]{:S(2)}) collective-permute-start(bf16[512,1024]{0,1:T(8,128)(2,1)S(1)} %fusion.2), channel_id=1, source_target_pairs={{0,8},{4,12},{8,0},{12,4},{16,24},{20,28},{24,16},{28,20},{1,9},{5... | collective-permute-start | bytes 3145736 | tf_op jit(solution)/shard_map/ppermute | solution.py:21
  (71 other events, 882.5 us)
Sparse Core Ops, SparseCore 0:
  25.8 103.8 all-gather.1

commit v6 on v5

--- a/solution.py
+++ b/solution.py
@@ -35,13 +35,25 @@
 
 
 ORDER = (
-    ("x6 z4 x3 x5", "x1 x2 x4 z1"),
-    ("t1 z2 w1 w4", "x3 x5 x6 t0"),
-    ("x7 w2 z5", "z2 w1 z4"),
-    ("t2 z6 z3 w5", "t1 x7 w2 z5 w4"),
-    ("w6", "w4 w2"),
-    ("z7", "z6 z3 w5 t2"),
+    ("front", "t2"),
+    ("t1", "t0 x3 x5 x6"),
+    ("t2", "t1 w2 w4 x7 z5"),
+    ("w1", "t0 x3 x5 x6"),
+    ("w2", "w1 z2 z4"),
     ("w3", "z7"),
+    ("w4", "t0 x3 x5 x6"),
+    ("w5", "t1 w2 w4 x7 z5"),
+    ("w6", "w2 w4"),
+    ("x3", "x2 x4 z1"),
+    ("x5", "x1 x2 x4 z1"),
+    ("x6", "x1 x2 x4 z1"),
+    ("x7", "w1 z2 z4"),
+    ("z2", "t0 x3 x5 x6"),
+    ("z3", "t1 w2 w4 x7 z5"),
+    ("z4", "x1 x2 x4 z1"),
+    ("z5", "w1 z4"),
+    ("z6", "t1 w2 w4 x7 z5"),
+    ("z7", "t2 w5 z3 z6"),
 )
 WAITS = {send: waits.split() for sends, waits in ORDER for send in sends.split()}
 
@@ -57,9 +69,12 @@
             self.made[name] = self.tokens(mask) if kind == "t" else self.piece(kind, mask)
         return self.made[name]
 
+    def held(self, name, value):
+        others = [self.get(other[0], int(other[1:])) for other in WAITS.get(name, ())]
+        return after(value, *others) if others else value
+
     def waiting(self, kind, mask, value):
-        others = [self.get(name[0], int(name[1:])) for name in WAITS.get(f"{kind}{mask}", ())]
-        return after(value, *others) if others else value
+        return self.held(f"{kind}{mask}", value)
 
     def piece(self, kind, mask):
         if mask == 0:
@@ -85,14 +100,6 @@
         return swapped(self.waiting("t", 2, self.get("t", 1)), "head", 1)
 
 
-def natural(value, axis_name, bit, axis):
-    other = swapped(value, axis_name, bit)
-    low = (lax.axis_index(axis_name) & bit) == 0
-    return jnp.where(
-        low, jnp.concatenate([value, other], axis=axis), jnp.concatenate([other, value], axis=axis)
-    )
-
-
 def by_xor(values, index):
     bit = 1
     while bit < len(values):
@@ -106,8 +113,27 @@
     return jnp.dot(a, b, preferred_element_type=F32)
 
 
+def by_lanes(value, head_dim):
+    heads = value.shape[1]
+    pair = 128 // head_dim
+    lane = lax.broadcasted_iota(jnp.int32, (value.shape[0], 128), 1) // head_dim
+    wide = []
+    for start in range(0, heads, pair):
+        part = jnp.broadcast_to(value[:, start : start + 1], lane.shape)
+        for h in range(1, pair):
+            part = jnp.where(lane == h, value[:, start + h : start + h + 1], part)
+        wide.append(part)
+    return jnp.concatenate(wide, axis=1)
+
+
+def slice_of_others(even_ref, odd_ref, place_ref, k, rows, depth):
+    columns = pl.ds(pl.multiple_of(place_ref[2, k], depth), depth)
+    block = place_ref[1, k]
+    return jnp.where(place_ref[3, k] == 1, odd_ref[block, rows, columns], even_ref[block, rows, columns])
+
+
 def front_kernel(
-    first_ref, x_ref, bc_ref, tx_ref, tbc_ref, kx_ref, kbc_ref, dec_ref, xc_ref, bcc_ref, f_ref
+    first_ref, x_ref, bc_ref, tx_ref, tbc_ref, kx_ref, kbc_ref, cum_ref, xc_ref, bcc_ref, f_ref
 ):
     rows = xc_ref.shape[1]
     for r in range(2):
@@ -128,12 +154,15 @@
         bc_val = conv(bc_ref, tbc_ref, kbc_ref)
         xc_ref[r] = x_val
         bcc_ref[r] = bc_val
-        decayed = (x_val.astype(F32) * dec_ref[r]).astype(BF16)
         nstate = bc_val.shape[1] // 2
+        head_dim = x_val.shape[1] // cum_ref.shape[2]
         for start in range(0, rows, Q):
+            cum = cum_ref[r, start : start + Q]
+            remaining = by_lanes(jnp.exp(cum[Q - 1 :] - cum), head_dim)
+            decayed = (x_val[start : start + Q].astype(F32) * remaining).astype(BF16)
             f_ref[r, start // Q] = lax.dot_general(
                 bc_val[start : start + Q, :nstate],
-                decayed[start : start + Q],
+                decayed,
                 (((0,), (0,)), ((), ())),
                 preferred_element_type=F32,
             )
@@ -158,15 +187,24 @@
         y_ref[0, :, start * head_dim : (start + pair) * head_dim] = jnp.concatenate(outs, axis=1)
 
 
-def gate_kernel(y_ref, x_ref, bc_ref, st_ref, e_ref, skip_ref, z_ref, gain_ref, g_ref, ss_ref):
+def gate_kernel(
+    place_ref, y_ref, x_ref, bc_ref, st_ref, cum_ref, skip_ref, z_ref, gain_ref, tokens_ref, even_ref, odd_ref,
+    w_ref, g_ref, ss_ref
+):
     nstate = st_ref.shape[2]
+    depth = w_ref.shape[0]
+    rows = pl.ds(pl.multiple_of(pl.program_id(1) * Q, Q), Q)
+    own = tokens_ref[rows, pl.ds(pl.multiple_of(place_ref[0, 0], depth), depth)]
+    other = slice_of_others(even_ref, odd_ref, place_ref, 0, rows, depth)
+    left = jnp.where(pl.program_id(0) == 0, own, other)
+    z_val = (z_ref[0] + dot(left, w_ref[...])).astype(BF16).astype(F32)
     c_val = bc_ref[0, :, nstate:]
     state = st_ref[0, 0]
     high = state.astype(BF16)
     low = (state - high.astype(F32)).astype(BF16)
     carried = dot(c_val, high) + dot(c_val, low)
-    y_val = (y_ref[0] + e_ref[0] * carried) / nstate + skip_ref[...] * x_ref[0].astype(F32)
-    z_val = z_ref[0].astype(F32)
+    grown = by_lanes(jnp.exp(cum_ref[0]), x_ref.shape[2] // cum_ref.shape[2])
+    y_val = (y_ref[0] + grown * carried) / nstate + skip_ref[...] * x_ref[0].astype(F32)
     gated = y_val * (z_val * jax.nn.sigmoid(z_val))
     g_ref[0] = (gated * gain_ref[...]).astype(BF16)
     total = jnp.sum(gated * gated, axis=1, keepdims=True)
@@ -181,7 +219,7 @@
     return pl.BlockSpec(shape, lambda *_: (0,) * len(shape))
 
 
-def front(first, x_pre, bc_pre, tail_x, tail_bc, conv_x, conv_bc, decay):
+def front(first, x_pre, bc_pre, tail_x, tail_bc, conv_x, conv_bc, cum):
     rows, chans = x_pre.shape[1] - HALO, x_pre.shape[2]
     bcw = bc_pre.shape[2]
     return pl.pallas_call(
@@ -196,43 +234,45 @@
         compiler_params=pltpu.CompilerParams(vmem_limit_bytes=VMEM_LIMIT),
         cost_estimate=LIGHT,
         name="front",
-    )(first, x_pre, bc_pre, tail_x, tail_bc, conv_x, conv_bc, decay)
+    )(first, x_pre, bc_pre, tail_x, tail_bc, conv_x, conv_bc, cum)
 
 
 def project_kernel(depth, with_halo, one_weight, place_ref, *refs):
     refs = list(refs)
     out_ref = refs.pop()
     halo_ref = refs.pop(0) if with_halo else None
-    tokens_ref, others_ref = refs[:2]
+    tokens_ref, even_ref, odd_ref = refs[:3]
     rows = tokens_ref.shape[0]
     lead = HALO if with_halo else 0
     totals = [None] * 3
     for k in range(place_ref.shape[1]):
         start = pl.multiple_of(place_ref[0, k], depth)
-        place = pl.multiple_of(place_ref[2, k], depth)
-        weight = refs[2][pl.ds(start, depth), :] if one_weight else refs[2 + k][:depth]
-        lefts = [tokens_ref[:, pl.ds(start, depth)], others_ref[place_ref[1, k], :rows, pl.ds(place, depth)]]
+        weight = refs[3][pl.ds(start, depth), :] if one_weight else refs[3 + k][:depth]
+        lefts = [
+            tokens_ref[:, pl.ds(start, depth)],
+            slice_of_others(even_ref, odd_ref, place_ref, k, pl.ds(0, rows), depth),
+        ]
         if with_halo:
             lefts.append(halo_ref[:, pl.ds(start, depth)])
         for i, left in enumerate(lefts):
             term = dot(left, weight)
             totals[i] = term if totals[i] is None else totals[i] + term
     for r in range(2):
-        out_ref[r, lead:] = totals[r].astype(BF16)
+        out_ref[r, lead:] = totals[r].astype(out_ref.dtype)
         if with_halo:
             out_ref[r, :lead] = totals[2][r * HALO : (r + 1) * HALO].astype(BF16)
 
 
-def project(places, depth, tokens, others, weights, halo=None):
+def project(places, depth, tokens, others, weights, halo=None, dtype=BF16):
     rows = tokens.shape[0] + (0 if halo is None else HALO)
     chans = weights[0].shape[1]
-    operands = ([] if halo is None else [halo]) + [tokens, others] + list(weights)
+    operands = ([] if halo is None else [halo]) + [tokens, *others] + list(weights)
     return pl.pallas_call(
         functools.partial(project_kernel, depth, halo is not None, len(weights) == 1),
         in_specs=[pl.BlockSpec(memory_space=pltpu.SMEM)]
         + [pl.BlockSpec(memory_space=pltpu.VMEM)] * len(operands),
         out_specs=pl.BlockSpec(memory_space=pltpu.VMEM),
-        out_shape=jax.ShapeDtypeStruct((2, rows, chans), BF16),
+        out_shape=jax.ShapeDtypeStruct((2, rows, chans), dtype),
         compiler_params=pltpu.CompilerParams(vmem_limit_bytes=VMEM_LIMIT),
         cost_estimate=LIGHT,
         name="project",
@@ -259,7 +299,7 @@
     )(x_conv, bc_conv, cum, cumt)
 
 
-def gate(y_in, x_conv, bc_conv, state, grown, skip, z_val, gain):
+def gate(places, y_in, x_conv, bc_conv, state, cum, skip, z_part, gain, tokens, others, z_weight):
     _, rows, chans = x_conv.shape
     bcw = bc_conv.shape[2]
 
@@ -270,15 +310,17 @@
         gate_kernel,
         grid=(2, rows // Q),
         in_specs=[
+            pl.BlockSpec(memory_space=pltpu.SMEM),
             tile(chans),
             tile(chans),
             tile(bcw),
             pl.BlockSpec((1, 1, bcw // 2, chans), lambda r, i: (r, i, 0, 0)),
-            tile(chans),
+            tile(cum.shape[2]),
             whole_block((1, chans)),
             tile(chans),
             whole_block((1, chans)),
-        ],
+        ]
+        + [pl.BlockSpec(memory_space=pltpu.VMEM)] * 4,
         out_specs=[tile(chans), tile(128)],
         out_shape=[
             jax.ShapeDtypeStruct((2, rows, chans), BF16),
@@ -287,7 +329,7 @@
         compiler_params=params(2),
         cost_estimate=LIGHT,
         name="gate",
-    )(y_in, x_conv, bc_conv, state, grown, skip, z_val, gain)
+    )(places, y_in, x_conv, bc_conv, state, cum, skip, z_part, gain, tokens, *others, z_weight)
 
 
 def local(
@@ -350,40 +392,39 @@
     masks = list(range(seq_count))
     x_pieces, z_pieces, out_pieces = [{mask: sends.get(kind, mask) for mask in masks} for kind in "xzw"]
 
-    others = jnp.concatenate([sends.get("t", 1), sends.get("t", 2)])
+    others = (sends.get("t", 1), sends.get("t", 2))
     ranges = [me, me ^ PAIR]
-    extras = jnp.stack([x_pieces[mask][depth:] for mask in range(seq_count)])
+    extras = [x_pieces[mask][depth:] for mask in range(seq_count)]
 
     def rows_before(place):
-        got = lax.dynamic_index_in_dim(extras, (me ^ (place - 1)) & (seq_count - 1), 0, keepdims=False)
-        return jnp.pad(got[:halo_rows].reshape(lag, -1), ((HALO - lag, 0), (0, 0)))
+        got = by_xor([extra[:halo_rows] for extra in extras], (me ^ (place - 1)) & (seq_count - 1))[0]
+        return jnp.pad(got.reshape(lag, -1), ((HALO - lag, 0), (0, 0)))
 
     halo = jnp.concatenate([rows_before(place) for place in ranges], axis=0)
 
     starts = [(me ^ mask) * depth for mask in masks]
     blocks = [a // share ^ mine for a in starts]
-    blocks = [(b >> 1) + (b & 1) * (head_count // 2) for b in blocks]
-    spots = [starts, blocks, [a % share for a in starts]]
+    spots = [starts, [b >> 1 for b in blocks], [a % share for a in starts], [b & 1 for b in blocks]]
     spots = jnp.stack([jnp.stack([jnp.int32(a) for a in row]) for row in spots])
 
     part = depth // head_count
     w_bc_all = lax.all_gather(cut(w_bc, mine, part, 0), ("seq", "head"), axis=0, tiled=True)
-    bc_pre = project(spots, depth, tokens, others, [w_bc_all], halo)
-    x_pre = project(spots, depth, tokens, others, list(x_pieces.values()), halo)
-    z_val = project(spots, depth, tokens, others, list(z_pieces.values()))
+    bc_pre = project(sends.held("project_x", spots), depth, tokens, others, [w_bc_all], halo)
+    x_pre = project(sends.held("project_x", spots), depth, tokens, others, list(x_pieces.values()), halo)
+    z_part = project(
+        sends.held("project_z", spots[:, :-1]), depth, tokens, others, list(z_pieces.values())[:-1], dtype=F32
+    )
 
     per_code = -1.0 / (16.0 * rows * seq_count)
-    got = sends.get("t", 0)[rows : rows + code_rows].astype(F32).reshape(3, heads, rows)
+    got = sends.held("decays", sends.get("t", 0))[rows : rows + code_rows].astype(F32).reshape(3, heads, rows)
     other_codes = got[0] + 256.0 * got[1] + 65536.0 * got[2]
     ld = jnp.stack([cut(codes, half, heads, 0).astype(F32), other_codes]) * per_code
     blocks = rows // Q
     cumt = jnp.cumsum(ld.reshape(2, heads, blocks, Q), axis=3).transpose(0, 2, 1, 3)
     cum = cumt.transpose(0, 1, 3, 2)
     ends = cum[:, :, -1:, :]
-    remaining = jnp.repeat(jnp.exp(ends - cum).reshape(2, rows, heads), head_dim, axis=2)
     block_decay = jnp.repeat(jnp.exp(ends), head_dim, axis=3)
     cum = cum.reshape(2, rows, heads)
-    grown = jnp.repeat(jnp.exp(cum), head_dim, axis=2)
     totals = jnp.stack([x_pieces[mask][depth + halo_rows] for mask in masks])
     totals = totals[:, : 4 * all_heads].astype(F32).reshape(-1, 4, all_heads)
     totals = sum(totals[:, j] * 256.0**j for j in range(4)) * per_code
@@ -400,14 +441,14 @@
         return jnp.pad(tail, ((HALO - tail.shape[0], 0), (0, 0)))
 
     x_conv, bc_conv, added = front(
-        after(first, sends.get("w", PAIR)),
+        sends.held("front", first),
         x_pre,
         bc_pre,
         padded(cut(tail_x, half, chans, 1)),
         padded(tail_bc),
         cut(conv_x, half, chans, 1),
         conv_bc,
-        remaining,
+        cum,
     )
 
     inside = [jnp.zeros_like(added[:, 0])]
@@ -445,14 +486,18 @@
 
     y_in = intra(x_conv, bc_conv, cum, cumt, heads)
     gated, squares = gate(
+        spots[:, -1:],
         y_in,
         x_conv,
         bc_conv,
         jnp.stack(states, axis=1),
-        grown,
+        cum,
         jnp.repeat(cut(skip_gain, half, heads, 0), head_dim)[None, :],
-        z_val,
-        after(cut(norm_gain, half, chans, 0)[None, :], out_pieces[PAIR | 1]),
+        z_part,
+        sends.held("gate", cut(norm_gain, half, chans, 0)[None, :]),
+        tokens,
+        others,
+        z_pieces[masks[-1]],
     )
 
     per = seq_count // head_count

time: 292 us -> 296 us (1.014)
  waiting for transfers between devices: 114 us -> 131 us
  local copies, waits for them, and re-layouts: 49.7 us -> 45 us
  starting transfers between devices: 39.6 us -> 35.5 us
  other arithmetic: 25 us -> 21.5 us
    ppermute x34, waiting for transfers between devices: 114 us -> 131 us  [swapped(): return lax.ppermute(value, axis, [(i, i ^ bit) for i in range(size)])]
    unnamed x125 -> x139, local copies, waits for them, and re-layouts: 13.2 us -> 21.1 us
    reshape x5 -> x2, local copies, waits for them, and re-layouts: 7.29 us -> 1.25 us  [rows_before(): return jnp.pad(got.reshape(lag, -1), ((HALO - lag, 0), (0, 0)))]
    ppermute x34, starting transfers between devices: 35.9 us -> 30.4 us  [swapped(): return lax.ppermute(value, axis, [(i, i ^ bit) for i in range(size)])]
    select_n x7, other arithmetic: 4 us -> 0.06 us  [decay_between(): chosen = jnp.where((places >= low) & (places < high), 1.0, 0.0)[:, None]]
    concatenate x1 -> x0, other arithmetic: 3.77 us -> none  [local(): others = jnp.concatenate([sends.get('t', 1), sends.get('t', 2)])]
    broadcast_in_dim x2 -> x0, local copies, waits for them, and re-layouts: 3.19 us -> none  [the longest x1 1.61 us: local(): grown = jnp.repeat(jnp.exp(cum), head_dim, axis=2)]
    pallas_call x1, Pallas kernels: 4.03 us -> 7.19 us  [gate(): pl.pallas_call(gate_kernel, grid=(2, rows // Q), in_specs=[pl.BlockSpec(m...]
  transfers between devices with their start and end apart: 36 -> 36, of which waited for: 16 -> 18; matrix products, arithmetic and copies ran while one was open for 24% -> 17% of each run, Pallas kernels for 12% -> 12%
where the time goes in v6:
time: 296 us; the launch traced here: 295 us
  waiting for transfers between devices  131 us (44%)
  local copies, waits for them, and re-layouts  45 us (15%)
  Pallas kernels  36.5 us (12%)
  starting transfers between devices  35.5 us (12%)
  other arithmetic  21.5 us (7%)
  between operations  14.9 us (5%)
  matrix products  10.5 us (4%)
    ppermute x34, waiting for transfers between devices, swapped(): return lax.ppermute(value, axis, [(i, i ^ bit) for i in range(size)])  131 us
    ppermute x34, starting transfers between devices, swapped(): return lax.ppermute(value, axis, [(i, i ^ bit) for i in range(size)])  30.4 us
    pallas_call x3, Pallas kernels, project(): pl.pallas_call(functools.partial(project_kernel, depth, halo is not None,...  22.4 us
    unnamed x139, local copies, waits for them, and re-layouts  21.1 us
    dot_general x7, matrix products, dot(): return jnp.dot(a, b, preferred_element_type=F32)  10.5 us
    dynamic_slice x10, local copies, waits for them, and re-layouts, cut(): return lax.dynamic_slice_in_dim(value, index * size, size, axis)  8.08 us
    pallas_call x1, Pallas kernels, gate(): pl.pallas_call(gate_kernel, grid=(2, rows // Q), in_specs=[pl.BlockSpec(m...  7.19 us
  transfers between devices with their start and end apart: 36, of which 18 were waited for; matrix products, arithmetic and copies ran while one was open for 17% of the time, Pallas kernels for 12%

profile of v6, /device:TPU:0, one launch (start us, length us, event | category | flops | bytes accessed | tf_op | source)
XLA Modules:
  0.0 294.5 jit_solution(5611324060344621174)
XLA Ops:
  12.1 4.0 %collective-permute-start.2 = (bf16[544,512]{1,0:T(8,128)(2,1)S(1)}, bf16[544,512]{1,0:T(8,128)(2,1)S(1)}, u32[]{:S(2)}, u32[]{:S(2)}) collective-permute-start(bf16[544,512]{1,0:T(8,128)(2,1)S(1)} %get-tuple-element.93.refs_4_), channel_id=1, source_target_pairs={{0,16},{4,20},{8,24},{12,28},{16,0},{20,4},{24,8},{28,12},{1,17},{... | collective-permute-start | bytes 1671176 | tf_op jit(solution)/shard_map/ppermute | solution.py:21
  31.3 10.8 %collective-permute-done.3.refs_4_ = bf16[512,512]{1,0:T(8,128)(2,1)} collective-permute-done((bf16[512,512]{1,0:T(8,128)(2,1)S(1)}, bf16[512,512]{1,0:T(8,128)(2,1)}, u32[]{:S(2)}, u32[]{:S(2)}) %collective-permute-start.3) | collective-permute-done | bytes 524320 | tf_op jit(solution)/shard_map/ppermute | solution.py:21
  42.1 15.1 %collective-permute-done.1.refs_6_ = bf16[544,512]{1,0:T(8,128)(2,1)S(1)} collective-permute-done((bf16[544,512]{1,0:T(8,128)(2,1)}, bf16[544,512]{1,0:T(8,128)(2,1)S(1)}, u32[]{:S(2)}, u32[]{:S(2)}) %collective-permute-start.1) | collective-permute-done | bytes 557088 | tf_op jit(solution)/shard_map/ppermute | solution.py:21
  62.8 2.8 collective-permute-start.11
  65.7 19.5 %collective-permute-done = bf16[528,1024]{1,0:T(8,128)(2,1)} collective-permute-done((bf16[528,1024]{1,0:T(8,128)(2,1)}, bf16[528,1024]{1,0:T(8,128)(2,1)}, u32[]{:S(2)}, u32[]{:S(2)}) %collective-permute-start) | collective-permute-done | bytes 1081376 | tf_op jit(solution)/shard_map/ppermute | solution.py:21
  85.9 7.3 %collective-permute-done.7.refs_10_ = bf16[544,512]{1,0:T(8,128)(2,1)S(1)} collective-permute-done((bf16[544,512]{1,0:T(8,128)(2,1)S(1)}, bf16[544,512]{1,0:T(8,128)(2,1)S(1)}, u32[]{:S(2)}, u32[]{:S(2)}) %collective-permute-start.7) | collective-permute-done | bytes 557088 | tf_op jit(solution)/shard_map/ppermute | solution.py:21
  96.7 2.3 reduce-window.6
  100.8 3.0 %collective-permute-done.9 = bf16[512,512]{1,0:T(8,128)(2,1)} collective-permute-done((bf16[512,512]{1,0:T(8,128)(2,1)}, bf16[512,512]{1,0:T(8,128)(2,1)}, u32[]{:S(2)}, u32[]{:S(2)}) %collective-permute-start.9) | collective-permute-done | bytes 524320 | tf_op jit(solution)/shard_map/ppermute | solution.py:21
  103.8 17.1 %collective-permute-done.10.refs_5_ = bf16[512,512]{1,0:T(8,128)(2,1)} collective-permute-done((bf16[512,512]{1,0:T(8,128)(2,1)}, bf16[512,512]{1,0:T(8,128)(2,1)}, u32[]{:S(2)}, u32[]{:S(2)}) %collective-permute-start.10) | collective-permute-done | bytes 524320 | tf_op jit(solution)/shard_map/ppermute | solution.py:21
  127.7 10.0 %collective-permute-done.12 = bf16[512,512]{1,0:T(8,128)(2,1)} collective-permute-done((bf16[512,512]{1,0:T(8,128)(2,1)}, bf16[512,512]{1,0:T(8,128)(2,1)}, u32[]{:S(2)}, u32[]{:S(2)}) %collective-permute-start.12) | collective-permute-done | bytes 524320 | tf_op jit(solution)/shard_map/ppermute | solution.py:21
  140.3 5.1 %collective-permute-done.14.refs_11_ = bf16[544,512]{1,0:T(8,128)(2,1)S(1)} collective-permute-done((bf16[544,512]{1,0:T(8,128)(2,1)}, bf16[544,512]{1,0:T(8,128)(2,1)S(1)}, u32[]{:S(2)}, u32[]{:S(2)}) %collective-permute-start.14) | collective-permute-done | bytes 557088 | tf_op jit(solution)/shard_map/ppermute | solution.py:21
  162.5 8.7 %project.3.x_ref = bf16[2,528,512]{2,1,0:T(8,128)(2,1)S(1)} custom-call(s32[4,8]{1,0:T(4,128)S(1)} %copy-done.30, bf16[32,4096]{1,0:T(8,128)(2,1)S(1)} %fusion.42.refs_0_, bf16[512,4096]{1,0:T(8,128)(2,1)} %tokens_ref.1, bf16[2,528,1024]{2,1,0:T(8,128)(2,1)} %copy-done.2, bf16[2,528,1024]{2,1,0:T(8,128)(2,1)} %collective-permute-done.16.refs_3_.refs_2_.odd_ref, ...), custom_call_target="tpu_custom_call" | custom-call | flops 1 | bytes 1 | tf_op jit(solution)/shard_map/project/pallas_call | solution.py:270
  176.2 5.6 %project.4.bc_ref = bf16[2,528,256]{2,1,0:T(8,128)(2,1)S(1)} custom-call(s32[4,8]{1,0:T(4,128)S(1)} %copy-done.31, bf16[32,4096]{1,0:T(8,128)(2,1)S(1)} %fusion.42.refs_0_, bf16[512,4096]{1,0:T(8,128)(2,1)} %tokens_ref.1, bf16[2,528,1024]{2,1,0:T(8,128)(2,1)S(1)} %copy-done.3, bf16[2,528,1024]{2,1,0:T(8,128)(2,1)} %collective-permute-done.16.refs_3_.refs_2_.odd_ref, ...), custom_call_target="tpu_custom_call" | custom-call | flops 1 | bytes 1 | tf_op jit(solution)/shard_map/project/pallas_call | solution.py:270
  182.0 4.0 %front.1 = (bf16[2,512,512]{2,1,0:T(8,128)(2,1)S(1)}, bf16[2,512,256]{2,1,0:T(8,128)(2,1)S(1)}, f32[2,2,128,512]{3,2,1,0:T(8,128)S(1)}) custom-call(s32[2]{0:T(128)S(1)} %copy-done.39, bf16[2,528,512]{2,1,0:T(8,128)(2,1)S(1)} %copy-done.7, bf16[2,528,256]{2,1,0:T(8,128)(2,1)S(1)} %project.4.bc_ref, bf16[16,512]{1,0:T(8,128)(2,1)S(1)} %pad.27.tx_ref, ...), custom_call_target="tpu_custom_call" | custom-call | flops 1 | bytes 1 | tf_op jit(solution)/shard_map/front/pallas_call | solution.py:225
  191.3 4.9 %collective-permute-done.17 = bf16[2,128,512]{2,1,0:T(8,128)(2,1)} collective-permute-done((bf16[2,128,512]{2,1,0:T(8,128)(2,1)S(1)}, bf16[2,128,512]{2,1,0:T(8,128)(2,1)}, u32[]{:S(2)}, u32[]{:S(2)}) %collective-permute-start.17) | collective-permute-done | bytes 262176 | tf_op jit(solution)/shard_map/ppermute | solution.py:21
  198.4 5.1 %collective-permute-start.18 = (bf16[128,512]{1,0:T(8,128)(2,1)S(1)}, bf16[128,512]{1,0:T(8,128)(2,1)S(1)}, u32[]{:S(2)}, u32[]{:S(2)}) collective-permute-start(bf16[128,512]{1,0:T(8,128)(2,1)S(1)} %add_convert_fusion), channel_id=1, source_target_pairs={{0,16},{4,20},{8,24},{12,28},{1,17},{5,21},{9,25},{13,29},{2,18},{... | collective-permute-start | bytes 393224 | tf_op jit(solution)/shard_map/ppermute | solution.py:26
  205.0 2.9 intra.1.y_ref
  209.2 8.0 %project.5.z_ref = f32[2,512,512]{2,1,0:T(8,128)S(1)} custom-call(s32[4,7]{1,0:T(4,128)S(1)} %bitcast.212, bf16[512,4096]{1,0:T(8,128)(2,1)} %tokens_ref.1, bf16[2,528,1024]{2,1,0:T(8,128)(2,1)} %copy-done.2, bf16[2,528,1024]{2,1,0:T(8,128)(2,1)} %collective-permute-done.16.refs_3_.refs_2_.odd_ref, bf16[512,512]{1,0:T(8,128)(2,1)S(1)} %copy-done.10, ...), custom_call_target="tpu_custom_call" | custom-call | flops 1 | bytes 1 | tf_op jit(solution)/shard_map/project/pallas_call | solution.py:270
  220.9 7.2 %gate.1 = (bf16[2,512,512]{2,1,0:T(8,128)(2,1)S(1)}, f32[2,512,128]{2,1,0:T(8,128)S(1)}) custom-call(s32[4,1]{1,0:T(4,128)S(1)} %copy-done.37, f32[2,512,512]{2,1,0:T(8,128)} %copy-done.4, bf16[2,512,512]{2,1,0:T(8,128)(2,1)S(1)} %get-tuple-element.41.x_ref, bf16[2,512,256]{2,1,0:T(8,128)(2,1)S(1)} %get-tuple-element.42.bc_ref, ...), custom_call_target="tpu_custom_call" | custom-call | flops 1 | bytes 1 | tf_op jit(solution)/shard_map/gate/pallas_call | solution.py:309
  235.9 2.6 collective-permute-done.31
  244.6 20.9 %collective-permute-done.32 = bf16[1024,512]{0,1:T(8,128)(2,1)S(1)} collective-permute-done((bf16[1024,512]{0,1:T(8,128)(2,1)S(1)}, bf16[1024,512]{0,1:T(8,128)(2,1)S(1)}, u32[]{:S(2)}, u32[]{:S(2)}) %collective-permute-start.32) | collective-permute-done | bytes 1048608 | tf_op jit(solution)/shard_map/ppermute | solution.py:21
  273.6 7.3 %collective-permute-done.33 = bf16[512,512]{0,1:T(8,128)(2,1)S(1)} collective-permute-done((bf16[512,512]{0,1:T(8,128)(2,1)}, bf16[512,512]{0,1:T(8,128)(2,1)S(1)}, u32[]{:S(2)}, u32[]{:S(2)}) %collective-permute-start.33) | collective-permute-done | bytes 524320 | tf_op jit(solution)/shard_map/ppermute | solution.py:21
  280.9 2.8 collective-permute-done.29
  283.7 2.6 multiply_convert_fusion.1
  (344 shorter events, 100.1 us)
Async XLA Ops:
  6.5 165.7 %all-gather.2.cloned.1.call-start = ((), (), s32[]{:S(2)}) async-start(), calls=%async_computation | async-start | bytes 2162688 | tf_op jit(solution)/shard_map/all_gather | solution.py:411
  12.1 45.0 %collective-permute-start.2 = (bf16[544,512]{1,0:T(8,128)(2,1)S(1)}, bf16[544,512]{1,0:T(8,128)(2,1)S(1)}, u32[]{:S(2)}, u32[]{:S(2)}) collective-permute-start(bf16[544,512]{1,0:T(8,128)(2,1)S(1)} %get-tuple-element.93.refs_4_), channel_id=1, source_target_pairs={{0,16},{4,20},{8,24},{12,28},{16,0},{20,4},{24,8},{28,12},{1,17},{... | collective-permute-start | bytes 1671176 | tf_op jit(solution)/shard_map/ppermute | solution.py:21
  16.2 41.0 %collective-permute-start.5 = (bf16[544,512]{1,0:T(8,128)(2,1)S(1)}, bf16[544,512]{1,0:T(8,128)(2,1)S(1)}, u32[]{:S(2)}, u32[]{:S(2)}) collective-permute-start(bf16[544,512]{1,0:T(8,128)(2,1)S(1)} %get-tuple-element.93.refs_4_), channel_id=1, source_target_pairs={{0,4},{4,0},{8,12},{12,8},{16,20},{20,16},{24,28},{28,24},{1,5},{5... | collective-permute-start | bytes 1671176 | tf_op jit(solution)/shard_map/ppermute | solution.py:21
  17.7 39.5 %collective-permute-start.1 = (bf16[544,512]{1,0:T(8,128)(2,1)}, bf16[544,512]{1,0:T(8,128)(2,1)S(1)}, u32[]{:S(2)}, u32[]{:S(2)}) collective-permute-start(bf16[544,512]{1,0:T(8,128)(2,1)} %get-tuple-element.94), channel_id=1, source_target_pairs={{0,8},{4,12},{8,0},{12,4},{16,24},{20,28},{24,16},{28,20},{1,9},{5... | collective-permute-start | bytes 1671176 | tf_op jit(solution)/shard_map/ppermute | solution.py:21
  20.2 21.9 %collective-permute-start.3 = (bf16[512,512]{1,0:T(8,128)(2,1)S(1)}, bf16[512,512]{1,0:T(8,128)(2,1)}, u32[]{:S(2)}, u32[]{:S(2)}) collective-permute-start(bf16[512,512]{1,0:T(8,128)(2,1)S(1)} %get-tuple-element.35.refs_3_), channel_id=1, source_target_pairs={{0,4},{4,0},{8,12},{12,8},{16,20},{20,16},{24,28},{28,24},{1,5},{5... | collective-permute-start | bytes 1572872 | tf_op jit(solution)/shard_map/ppermute | solution.py:21
  23.2 62.0 %collective-permute-start = (bf16[528,1024]{1,0:T(8,128)(2,1)}, bf16[528,1024]{1,0:T(8,128)(2,1)}, u32[]{:S(2)}, u32[]{:S(2)}) collective-permute-start(bf16[528,1024]{1,0:T(8,128)(2,1)} %fusion.7), channel_id=1, source_target_pairs={{0,8},{4,12},{8,0},{12,4},{16,24},{20,28},{24,16},{28,20},{1,9},{5... | collective-permute-start | bytes 3244040 | tf_op jit(solution)/shard_map/ppermute | solution.py:21
  57.2 36.1 %collective-permute-start.7 = (bf16[544,512]{1,0:T(8,128)(2,1)S(1)}, bf16[544,512]{1,0:T(8,128)(2,1)S(1)}, u32[]{:S(2)}, u32[]{:S(2)}) collective-permute-start(bf16[544,512]{1,0:T(8,128)(2,1)S(1)} %collective-permute-done.1.refs_6_), channel_id=1, source_target_pairs={{0,16},{4,20},{8,24},{12,28},{16,0},{20,4},{24,8},{28,12},{1,17},{... | collective-permute-start | bytes 1671176 | tf_op jit(solution)/shard_map/ppermute | solution.py:21
  57.3 36.0 %collective-permute-start.6 = (bf16[544,512]{1,0:T(8,128)(2,1)S(1)}, bf16[544,512]{1,0:T(8,128)(2,1)S(1)}, u32[]{:S(2)}, u32[]{:S(2)}) collective-permute-start(bf16[544,512]{1,0:T(8,128)(2,1)S(1)} %collective-permute-done.2.refs_8_), channel_id=1, source_target_pairs={{0,4},{4,0},{8,12},{12,8},{16,20},{20,16},{24,28},{28,24},{1,5},{5... | collective-permute-start | bytes 1671176 | tf_op jit(solution)/shard_map/ppermute | solution.py:21
  57.3 35.9 %collective-permute-start.4 = (bf16[544,512]{1,0:T(8,128)(2,1)S(1)}, bf16[544,512]{1,0:T(8,128)(2,1)S(1)}, u32[]{:S(2)}, u32[]{:S(2)}) collective-permute-start(bf16[544,512]{1,0:T(8,128)(2,1)S(1)} %collective-permute-done.1.refs_6_), channel_id=1, source_target_pairs={{0,4},{4,0},{8,12},{12,8},{16,20},{20,16},{24,28},{28,24},{1,5},{5... | collective-permute-start | bytes 1671176 | tf_op jit(solution)/shard_map/ppermute | solution.py:21
  62.8 38.0 %collective-permute-start.11 = (bf16[512,512]{1,0:T(8,128)(2,1)S(1)}, bf16[512,512]{1,0:T(8,128)(2,1)S(1)}, u32[]{:S(2)}, u32[]{:S(2)}) collective-permute-start(bf16[512,512]{1,0:T(8,128)(2,1)S(1)} %get-tuple-element.35.refs_3_), channel_id=1, source_target_pairs={{0,16},{4,20},{8,24},{12,28},{16,0},{20,4},{24,8},{28,12},{1,17},{... | collective-permute-start | bytes 1572872 | tf_op jit(solution)/shard_map/ppermute | solution.py:21
  94.9 26.0 %collective-permute-start.10 = (bf16[512,512]{1,0:T(8,128)(2,1)}, bf16[512,512]{1,0:T(8,128)(2,1)}, u32[]{:S(2)}, u32[]{:S(2)}) collective-permute-start(bf16[512,512]{1,0:T(8,128)(2,1)} %get-tuple-element.34), channel_id=1, source_target_pairs={{0,8},{4,12},{8,0},{12,4},{16,24},{20,28},{24,16},{28,20},{1,9},{5... | collective-permute-start | bytes 1572872 | tf_op jit(solution)/shard_map/ppermute | solution.py:21
  95.0 42.7 %collective-permute-start.8 = (bf16[1,528,1024]{2,1,0:T(8,128)(2,1)}, bf16[1,528,1024]{2,1,0:T(8,128)(2,1)}, u32[]{:S(2)}, u32[]{:S(2)}) collective-permute-start(bf16[1,528,1024]{2,1,0:T(8,128)(2,1)} %bitcast.44), channel_id=1, source_target_pairs={{0,2},{1,3},{2,0},{3,1},{4,6},{5,7},{6,4},{7,5},{8,10},{9,11},{10,... | collective-permute-start | bytes 3244040 | tf_op jit(solution)/shard_map/ppermute | solution.py:21
  99.2 28.4 %collective-permute-start.13 = (bf16[512,512]{1,0:T(8,128)(2,1)}, bf16[512,512]{1,0:T(8,128)(2,1)}, u32[]{:S(2)}, u32[]{:S(2)}) collective-permute-start(bf16[512,512]{1,0:T(8,128)(2,1)} %get-tuple-element.33), channel_id=1, source_target_pairs={{0,16},{4,20},{8,24},{12,28},{16,0},{20,4},{24,8},{28,12},{1,17},{... | collective-permute-start | bytes 1572872 | tf_op jit(solution)/shard_map/ppermute | solution.py:21
  120.9 16.8 %collective-permute-start.12 = (bf16[512,512]{1,0:T(8,128)(2,1)}, bf16[512,512]{1,0:T(8,128)(2,1)}, u32[]{:S(2)}, u32[]{:S(2)}) collective-permute-start(bf16[512,512]{1,0:T(8,128)(2,1)} %get-tuple-element.36), channel_id=1, source_target_pairs={{0,8},{4,12},{8,0},{12,4},{16,24},{20,28},{24,16},{28,20},{1,9},{5... | collective-permute-start | bytes 1572872 | tf_op jit(solution)/shard_map/ppermute | solution.py:21
  121.4 18.0 %collective-permute-start.15 = (bf16[512,512]{1,0:T(8,128)(2,1)}, bf16[512,512]{1,0:T(8,128)(2,1)S(1)}, u32[]{:S(2)}, u32[]{:S(2)}) collective-permute-start(bf16[512,512]{1,0:T(8,128)(2,1)} %copy-done.25), channel_id=1, source_target_pairs={{0,4},{4,0},{8,12},{12,8},{16,20},{20,16},{24,28},{28,24},{1,5},{5... | collective-permute-start | bytes 1572872 | tf_op jit(solution)/shard_map/ppermute | solution.py:21
  121.7 23.7 %collective-permute-start.14 = (bf16[544,512]{1,0:T(8,128)(2,1)}, bf16[544,512]{1,0:T(8,128)(2,1)S(1)}, u32[]{:S(2)}, u32[]{:S(2)}) collective-permute-start(bf16[544,512]{1,0:T(8,128)(2,1)} %copy-done.17), channel_id=1, source_target_pairs={{0,4},{4,0},{8,12},{12,8},{16,20},{20,16},{24,28},{28,24},{1,5},{5... | collective-permute-start | bytes 1671176 | tf_op jit(solution)/shard_map/ppermute | solution.py:21
  137.7 51.6 %collective-permute-start.23 = (bf16[512,512]{1,0:T(8,128)(2,1)}, bf16[512,512]{1,0:T(8,128)(2,1)}, u32[]{:S(2)}, u32[]{:S(2)}) collective-permute-start(bf16[512,512]{1,0:T(8,128)(2,1)} %collective-permute-done.12), channel_id=1, source_target_pairs={{0,16},{4,20},{8,24},{12,28},{16,0},{20,4},{24,8},{28,12},{1,17},{... | collective-permute-start | bytes 1572872 | tf_op jit(solution)/shard_map/ppermute | solution.py:21
  145.5 59.3 %collective-permute-start.19 = (bf16[512,512]{1,0:T(8,128)(2,1)}, bf16[512,512]{1,0:T(8,128)(2,1)}, u32[]{:S(2)}, u32[]{:S(2)}) collective-permute-start(bf16[512,512]{1,0:T(8,128)(2,1)} %collective-permute-done.10.refs_5_), channel_id=1, source_target_pairs={{0,4},{4,0},{8,12},{12,8},{16,20},{20,16},{24,28},{28,24},{1,5},{5... | collective-permute-start | bytes 1572872 | tf_op jit(solution)/shard_map/ppermute | solution.py:21
  145.5 59.3 %collective-permute-start.20 = (bf16[512,512]{1,0:T(8,128)(2,1)}, bf16[512,512]{1,0:T(8,128)(2,1)}, u32[]{:S(2)}, u32[]{:S(2)}) collective-permute-start(bf16[512,512]{1,0:T(8,128)(2,1)} %collective-permute-done.10.refs_5_), channel_id=1, source_target_pairs={{0,16},{4,20},{8,24},{12,28},{16,0},{20,4},{24,8},{28,12},{1,17},{... | collective-permute-start | bytes 1572872 | tf_op jit(solution)/shard_map/ppermute | solution.py:21
  145.5 59.3 %collective-permute-start.21 = (bf16[512,512]{1,0:T(8,128)(2,1)}, bf16[512,512]{1,0:T(8,128)(2,1)}, u32[]{:S(2)}, u32[]{:S(2)}) collective-permute-start(bf16[512,512]{1,0:T(8,128)(2,1)} %collective-permute-done.13), channel_id=1, source_target_pairs={{0,4},{4,0},{8,12},{12,8},{16,20},{20,16},{24,28},{28,24},{1,5},{5... | collective-permute-start | bytes 1572872 | tf_op jit(solution)/shard_map/ppermute | solution.py:21
  189.3 42.7 %collective-permute-start.24 = (bf16[512,512]{1,0:T(8,128)(2,1)}, bf16[512,512]{1,0:T(8,128)(2,1)S(1)}, u32[]{:S(2)}, u32[]{:S(2)}) collective-permute-start(bf16[512,512]{1,0:T(8,128)(2,1)} %collective-permute-done.23), channel_id=1, source_target_pairs={{0,4},{4,0},{8,12},{12,8},{16,20},{20,16},{24,28},{28,24},{1,5},{5... | collective-permute-start | bytes 1572872 | tf_op jit(solution)/shard_map/ppermute | solution.py:21
  198.4 18.9 %collective-permute-start.18 = (bf16[128,512]{1,0:T(8,128)(2,1)S(1)}, bf16[128,512]{1,0:T(8,128)(2,1)S(1)}, u32[]{:S(2)}, u32[]{:S(2)}) collective-permute-start(bf16[128,512]{1,0:T(8,128)(2,1)S(1)} %add_convert_fusion), channel_id=1, source_target_pairs={{0,16},{4,20},{8,24},{12,28},{1,17},{5,21},{9,25},{13,29},{2,18},{... | collective-permute-start | bytes 393224 | tf_op jit(solution)/shard_map/ppermute | solution.py:26
  241.0 24.4 %collective-permute-start.32 = (bf16[1024,512]{0,1:T(8,128)(2,1)S(1)}, bf16[1024,512]{0,1:T(8,128)(2,1)S(1)}, u32[]{:S(2)}, u32[]{:S(2)}) collective-permute-start(bf16[1024,512]{0,1:T(8,128)(2,1)S(1)} %slice_add_fusion), channel_id=1, source_target_pairs={{0,2},{1,3},{2,0},{3,1},{4,6},{5,7},{6,4},{7,5},{8,10},{9,11},{10,... | collective-permute-start | bytes 3145736 | tf_op jit(solution)/shard_map/ppermute | solution.py:21
  243.3 26.7 %collective-permute-start.28 = (bf16[512,1024]{0,1:T(8,128)(2,1)S(1)}, bf16[512,1024]{0,1:T(8,128)(2,1)S(1)}, u32[]{:S(2)}, u32[]{:S(2)}) collective-permute-start(bf16[512,1024]{0,1:T(8,128)(2,1)S(1)} %fusion.2), channel_id=1, source_target_pairs={{0,8},{4,12},{8,0},{12,4},{16,24},{20,28},{24,16},{28,20},{1,9},{5... | collective-permute-start | bytes 3145736 | tf_op jit(solution)/shard_map/ppermute | solution.py:21
  (81 other events, 841.5 us)
Sparse Core Ops, SparseCore 0:
  25.2 104.1 all-gather.1

commit v7 on v5

--- a/solution.py
+++ b/solution.py
@@ -35,15 +35,15 @@
 
 
 ORDER = (
-    ("x6 z4 x3 x5", "x1 x2 x4 z1"),
-    ("t1 z2 w1 w4", "x3 x5 x6 t0"),
-    ("x7 w2 z5", "z2 w1 z4"),
-    ("t2 z6 z3 w5", "t1 x7 w2 z5 w4"),
-    ("w6", "w4 w2"),
-    ("z7", "z6 z3 w5 t2"),
-    ("w3", "z7"),
+    (("x6", "z4", "x3", "x5"), ("x1", "x2", "x4", "z1")),
+    (("t1", "z2", "w1", "w4"), ("x3", "x5", "x6", "t0")),
+    (("x7", "w2", "z5"), ("z2", "w1", "z4")),
+    (("t2", "z6", "z3", "w5"), ("t1", "x7", "w2", "z5", "w4")),
+    (("w6",), ("w4", "w2")),
+    (("z7",), ("z6", "z3", "w5", "t2")),
+    (("w3",), ("z7",)),
 )
-WAITS = {send: waits.split() for sends, waits in ORDER for send in sends.split()}
+WAITS = {send: waits for sends, waits in ORDER for send in sends}
 
 
 class Sends:

time: 292 us -> 292 us (level)
  no operation moved by 1% of the time
where the time goes in v7:
time: 292 us; the launch traced here: 291 us
  waiting for transfers between devices  114 us (39%)
  local copies, waits for them, and re-layouts  49.7 us (17%)
  starting transfers between devices  39.6 us (14%)
  Pallas kernels  35.9 us (12%)
  other arithmetic  25 us (9%)
  between operations  14.5 us (5%)
  matrix products  11.5 us (4%)
    ppermute x34, waiting for transfers between devices, swapped(): return lax.ppermute(value, axis, [(i, i ^ bit) for i in range(size)])  114 us
    ppermute x34, starting transfers between devices, swapped(): return lax.ppermute(value, axis, [(i, i ^ bit) for i in range(size)])  35.9 us
    pallas_call x3, Pallas kernels, project(): pl.pallas_call(functools.partial(project_kernel, depth, halo is not None,...  23.9 us
    unnamed x125, local copies, waits for them, and re-layouts  13.2 us
    dot_general x7, matrix products, dot(): return jnp.dot(a, b, preferred_element_type=F32)  11.5 us
    dynamic_slice x10, local copies, waits for them, and re-layouts, cut(): return lax.dynamic_slice_in_dim(value, index * size, size, axis)  9.33 us
  transfers between devices with their start and end apart: 36, of which 16 were waited for; matrix products, arithmetic and copies ran while one was open for 24% of the time, Pallas kernels for 12%

profile of v7, /device:TPU:0, one launch (start us, length us, event | category | flops | bytes accessed | tf_op | source)
XLA Modules:
  0.0 290.5 jit_solution(14828170002551128459)
XLA Ops:
  12.2 2.9 %collective-permute-start.1 = (bf16[544,512]{1,0:T(8,128)(2,1)S(1)}, bf16[544,512]{1,0:T(8,128)(2,1)S(1)}, u32[]{:S(2)}, u32[]{:S(2)}) collective-permute-start(bf16[544,512]{1,0:T(8,128)(2,1)S(1)} %get-tuple-element.98.refs_3_), channel_id=1, source_target_pairs={{0,4},{4,0},{8,12},{12,8},{16,20},{20,16},{24,28},{28,24},{1,5},{5... | collective-permute-start | bytes 1671176 | tf_op jit(solution)/shard_map/ppermute | solution.py:21
  15.1 2.6 collective-permute-start.2
  40.9 4.4 %collective-permute-done.refs_5_ = bf16[544,512]{1,0:T(8,128)(2,1)} collective-permute-done((bf16[544,512]{1,0:T(8,128)(2,1)}, bf16[544,512]{1,0:T(8,128)(2,1)}, u32[]{:S(2)}, u32[]{:S(2)}) %collective-permute-start) | collective-permute-done | bytes 557088 | tf_op jit(solution)/shard_map/ppermute | solution.py:21
  46.3 2.4 collective-permute-start.10
  52.5 38.2 %collective-permute-done.7 = bf16[528,1024]{1,0:T(8,128)(2,1)} collective-permute-done((bf16[528,1024]{1,0:T(8,128)(2,1)}, bf16[528,1024]{1,0:T(8,128)(2,1)}, u32[]{:S(2)}, u32[]{:S(2)}) %collective-permute-start.7) | collective-permute-done | bytes 1081376 | tf_op jit(solution)/shard_map/ppermute | solution.py:21
  92.2 2.3 reduce-window.6
  99.3 3.0 %copy.38.dec_ref = f32[2,512,512]{2,1,0:T(8,128)} copy(f32[2,512,512]{1,2,0:T(8,128)} %bitcast.238) | data formatting | bytes 4194304 | tf_op jit(solution)/shard_map/reshape | solution.py:383
  104.0 3.2 %copy.49.e_ref = f32[2,512,512]{2,1,0:T(8,128)} copy(f32[2,512,512]{1,2,0:T(8,128)} %bitcast.239) | data formatting | bytes 4194304 | tf_op jit(solution)/shard_map/reshape | solution.py:386
  120.2 14.3 %collective-permute-done.11 = bf16[512,512]{1,0:T(8,128)(2,1)} collective-permute-done((bf16[512,512]{1,0:T(8,128)(2,1)S(1)}, bf16[512,512]{1,0:T(8,128)(2,1)}, u32[]{:S(2)}, u32[]{:S(2)}) %collective-permute-start.11) | collective-permute-done | bytes 524320 | tf_op jit(solution)/shard_map/ppermute | solution.py:21
  134.5 2.6 collective-permute-done.15
  138.8 3.2 %pad_maximum_fusion.1 = bf16[2,528,1024]{2,1,0:T(8,128)(2,1)} fusion(bf16[1,528,1024]{2,1,0:T(8,128)(2,1)S(1)} %collective-permute-done.13, bf16[1,528,1024]{2,1,0:T(8,128)(2,1)} %bitcast.47), kind=kLoop, calls=%fused_computation.2 | loop fusion | flops 1081344 | bytes 4325376 | tf_op jit(solution)/shard_map/concatenate | solution.py:82
  147.3 2.6 collective-permute-done.16
  150.0 3.8 %pad_maximum_fusion.refs_2_.refs_1_ = bf16[4,528,1024]{2,1,0:T(8,128)(2,1)} fusion(bf16[2,528,1024]{2,1,0:T(8,128)(2,1)} %collective-permute-done.16, bf16[1,528,1024]{2,1,0:T(8,128)(2,1)} %copy-done.26, bf16[1,528,1024]{2,1,0:T(8,128)(2,1)} %bitcast.47), kind=kLoop, calls=%fused_computation | loop fusion | flops 4325376 | bytes 8650752 | tf_op jit(solution)/shard_map/concatenate | solution.py:353
  154.8 9.3 %project.3.x_ref = bf16[2,528,512]{2,1,0:T(8,128)(2,1)S(1)} custom-call(s32[3,8]{1,0:T(4,128)S(1)} %copy-done.18, bf16[32,4096]{1,0:T(8,128)(2,1)S(1)} %fusion.42.refs_0_, bf16[512,4096]{1,0:T(8,128)(2,1)} %refs_0_.1, bf16[4,528,1024]{2,1,0:T(8,128)(2,1)} %pad_maximum_fusion.refs_2_.refs_1_, bf16[544,512]{1,0:T(8,128)(2,1)S(1)} %get-tuple-element.98.refs_3_, ...), custom_call_target="tpu_custom_call" | custom-call | flops 1 | bytes 1 | tf_op jit(solution)/shard_map/project/pallas_call | solution.py:230
  165.7 6.2 %project.4.bc_ref = bf16[2,528,256]{2,1,0:T(8,128)(2,1)S(1)} custom-call(s32[3,8]{1,0:T(4,128)S(1)} %copy-done.18, bf16[32,4096]{1,0:T(8,128)(2,1)S(1)} %fusion.42.refs_0_, bf16[512,4096]{1,0:T(8,128)(2,1)} %refs_0_.1, bf16[4,528,1024]{2,1,0:T(8,128)(2,1)} %pad_maximum_fusion.refs_2_.refs_1_, bf16[4096,256]{1,0:T(8,128)(2,1)S(1)} %copy-done.5), custom_call_target="tpu_custom_call" | custom-call | flops 1 | bytes 1 | tf_op jit(solution)/shard_map/project/pallas_call | solution.py:230
  172.0 4.8 %front.1 = (bf16[2,512,512]{2,1,0:T(8,128)(2,1)S(1)}, bf16[2,512,256]{2,1,0:T(8,128)(2,1)S(1)}, f32[2,2,128,512]{3,2,1,0:T(8,128)S(1)}) custom-call(s32[2]{0:T(128)S(1)} %copy-done.22, bf16[2,528,512]{2,1,0:T(8,128)(2,1)S(1)} %project.3.x_ref, bf16[2,528,256]{2,1,0:T(8,128)(2,1)S(1)} %project.4.bc_ref, bf16[16,512]{1,0:T(8,128)(2,1)S(1)} %pad.27.tx_ref, ...), custom_call_target="tpu_custom_call" | custom-call | flops 1 | bytes 1 | tf_op jit(solution)/shard_map/front/pallas_call | solution.py:187
  187.2 3.7 %collective-permute-start.18 = (bf16[128,512]{1,0:T(8,128)(2,1)S(1)}, bf16[128,512]{1,0:T(8,128)(2,1)S(1)}, u32[]{:S(2)}, u32[]{:S(2)}) collective-permute-start(bf16[128,512]{1,0:T(8,128)(2,1)S(1)} %add_convert_fusion), channel_id=1, source_target_pairs={{0,16},{4,20},{8,24},{12,28},{1,17},{5,21},{9,25},{13,29},{2,18},{... | collective-permute-start | bytes 393224 | tf_op jit(solution)/shard_map/ppermute | solution.py:26
  192.3 3.1 %intra.1.y_ref = f32[2,512,512]{2,1,0:T(8,128)S(1)} custom-call(bf16[2,512,512]{2,1,0:T(8,128)(2,1)S(1)} %get-tuple-element.40.x_ref, bf16[2,512,256]{2,1,0:T(8,128)(2,1)S(1)} %copy-done.7, f32[2,512,8]{2,1,0:T(8,128)S(1)} %copy-done.8, f32[2,2,8,256]{3,2,1,0:T(8,128)S(1)} %copy-done.15), custom_call_target="tpu_custom_call" | custom-call | flops 1 | bytes 1 | tf_op jit(solution)/shard_map/intra/pallas_call | solution.py:250
  195.6 13.0 %collective-permute-done.22.refs_9_ = bf16[512,512]{1,0:T(8,128)(2,1)S(1)} collective-permute-done((bf16[512,512]{1,0:T(8,128)(2,1)}, bf16[512,512]{1,0:T(8,128)(2,1)S(1)}, u32[]{:S(2)}, u32[]{:S(2)}) %collective-permute-start.22) | collective-permute-done | bytes 524320 | tf_op jit(solution)/shard_map/ppermute | solution.py:21
  211.8 8.5 %project.5.z_ref = bf16[2,512,512]{2,1,0:T(8,128)(2,1)S(1)} custom-call(s32[3,8]{1,0:T(4,128)S(1)} %copy-done.18, bf16[512,4096]{1,0:T(8,128)(2,1)} %refs_0_.1, bf16[4,528,1024]{2,1,0:T(8,128)(2,1)} %pad_maximum_fusion.refs_2_.refs_1_, bf16[512,512]{1,0:T(8,128)(2,1)S(1)} %copy-done.4, bf16[512,512]{1,0:T(8,128)(2,1)S(1)} %copy-done.12, ...), custom_call_target="tpu_custom_call" | custom-call | flops 1 | bytes 1 | tf_op jit(solution)/shard_map/project/pallas_call | solution.py:230
  222.0 4.0 %gate.1 = (bf16[2,512,512]{2,1,0:T(8,128)(2,1)S(1)}, f32[2,512,128]{2,1,0:T(8,128)S(1)}) custom-call(f32[2,512,512]{2,1,0:T(8,128)} %copy-done.2, bf16[2,512,512]{2,1,0:T(8,128)(2,1)S(1)} %get-tuple-element.40.x_ref, bf16[2,512,256]{2,1,0:T(8,128)(2,1)S(1)} %copy-done.7, f32[2,2,128,512]{3,2,1,0:T(8,128)S(1)} %pad_maximum_fusion.2.st_ref, ...), custom_call_target="tpu_custom_call" | custom-call | flops 1 | bytes 1 | tf_op jit(solution)/shard_map/gate/pallas_call | solution.py:269
  241.7 20.1 %collective-permute-done.32 = bf16[1024,512]{0,1:T(8,128)(2,1)S(1)} collective-permute-done((bf16[1024,512]{0,1:T(8,128)(2,1)S(1)}, bf16[1024,512]{0,1:T(8,128)(2,1)S(1)}, u32[]{:S(2)}, u32[]{:S(2)}) %collective-permute-start.32) | collective-permute-done | bytes 1048608 | tf_op jit(solution)/shard_map/ppermute | solution.py:21
  270.3 7.1 %collective-permute-done.33 = bf16[512,512]{0,1:T(8,128)(2,1)} collective-permute-done((bf16[512,512]{0,1:T(8,128)(2,1)}, bf16[512,512]{0,1:T(8,128)(2,1)}, u32[]{:S(2)}, u32[]{:S(2)}) %collective-permute-start.33) | collective-permute-done | bytes 524320 | tf_op jit(solution)/shard_map/ppermute | solution.py:21
  279.5 2.7 multiply_convert_fusion.1
  (336 shorter events, 108.0 us)
Async XLA Ops:
  6.5 157.6 %all-gather.2.cloned.1.call-start = ((), (), s32[]{:S(2)}) async-start(), calls=%async_computation | async-start | bytes 2162688 | tf_op jit(solution)/shard_map/all_gather | solution.py:370
  12.2 33.2 %collective-permute-start.1 = (bf16[544,512]{1,0:T(8,128)(2,1)S(1)}, bf16[544,512]{1,0:T(8,128)(2,1)S(1)}, u32[]{:S(2)}, u32[]{:S(2)}) collective-permute-start(bf16[544,512]{1,0:T(8,128)(2,1)S(1)} %get-tuple-element.98.refs_3_), channel_id=1, source_target_pairs={{0,4},{4,0},{8,12},{12,8},{16,20},{20,16},{24,28},{28,24},{1,5},{5... | collective-permute-start | bytes 1671176 | tf_op jit(solution)/shard_map/ppermute | solution.py:21
  15.1 30.2 %collective-permute-start.2 = (bf16[544,512]{1,0:T(8,128)(2,1)S(1)}, bf16[544,512]{1,0:T(8,128)(2,1)S(1)}, u32[]{:S(2)}, u32[]{:S(2)}) collective-permute-start(bf16[544,512]{1,0:T(8,128)(2,1)S(1)} %get-tuple-element.98.refs_3_), channel_id=1, source_target_pairs={{0,16},{4,20},{8,24},{12,28},{16,0},{20,4},{24,8},{28,12},{1,17},{... | collective-permute-start | bytes 1671176 | tf_op jit(solution)/shard_map/ppermute | solution.py:21
  17.7 27.6 %collective-permute-start = (bf16[544,512]{1,0:T(8,128)(2,1)}, bf16[544,512]{1,0:T(8,128)(2,1)}, u32[]{:S(2)}, u32[]{:S(2)}) collective-permute-start(bf16[544,512]{1,0:T(8,128)(2,1)} %get-tuple-element.99), channel_id=1, source_target_pairs={{0,8},{4,12},{8,0},{12,4},{16,24},{20,28},{24,16},{28,20},{1,9},{5... | collective-permute-start | bytes 1671176 | tf_op jit(solution)/shard_map/ppermute | solution.py:21
  20.2 20.7 %collective-permute-start.3 = (bf16[512,512]{1,0:T(8,128)(2,1)S(1)}, bf16[512,512]{1,0:T(8,128)(2,1)S(1)}, u32[]{:S(2)}, u32[]{:S(2)}) collective-permute-start(bf16[512,512]{1,0:T(8,128)(2,1)S(1)} %get-tuple-element.33.refs_2_), channel_id=1, source_target_pairs={{0,4},{4,0},{8,12},{12,8},{16,20},{20,16},{24,28},{28,24},{1,5},{5... | collective-permute-start | bytes 1572872 | tf_op jit(solution)/shard_map/ppermute | solution.py:21
  23.8 66.9 %collective-permute-start.7 = (bf16[528,1024]{1,0:T(8,128)(2,1)}, bf16[528,1024]{1,0:T(8,128)(2,1)}, u32[]{:S(2)}, u32[]{:S(2)}) collective-permute-start(bf16[528,1024]{1,0:T(8,128)(2,1)} %fusion.7), channel_id=1, source_target_pairs={{0,8},{4,12},{8,0},{12,4},{16,24},{20,28},{24,16},{28,20},{1,9},{5... | collective-permute-start | bytes 3244040 | tf_op jit(solution)/shard_map/ppermute | solution.py:21
  45.3 50.6 %collective-permute-start.4 = (bf16[544,512]{1,0:T(8,128)(2,1)}, bf16[544,512]{1,0:T(8,128)(2,1)}, u32[]{:S(2)}, u32[]{:S(2)}) collective-permute-start(bf16[544,512]{1,0:T(8,128)(2,1)} %collective-permute-done.refs_5_), channel_id=1, source_target_pairs={{0,4},{4,0},{8,12},{12,8},{16,20},{20,16},{24,28},{28,24},{1,5},{5... | collective-permute-start | bytes 1671176 | tf_op jit(solution)/shard_map/ppermute | solution.py:21
  45.8 50.1 %collective-permute-start.6 = (bf16[544,512]{1,0:T(8,128)(2,1)}, bf16[544,512]{1,0:T(8,128)(2,1)}, u32[]{:S(2)}, u32[]{:S(2)}) collective-permute-start(bf16[544,512]{1,0:T(8,128)(2,1)} %collective-permute-done.refs_5_), channel_id=1, source_target_pairs={{0,16},{4,20},{8,24},{12,28},{16,0},{20,4},{24,8},{28,12},{1,17},{... | collective-permute-start | bytes 1671176 | tf_op jit(solution)/shard_map/ppermute | solution.py:21
  46.3 65.2 %collective-permute-start.10 = (bf16[512,512]{1,0:T(8,128)(2,1)S(1)}, bf16[512,512]{1,0:T(8,128)(2,1)}, u32[]{:S(2)}, u32[]{:S(2)}) collective-permute-start(bf16[512,512]{1,0:T(8,128)(2,1)S(1)} %get-tuple-element.33.refs_2_), channel_id=1, source_target_pairs={{0,16},{4,20},{8,24},{12,28},{16,0},{20,4},{24,8},{28,12},{1,17},{... | collective-permute-start | bytes 1572872 | tf_op jit(solution)/shard_map/ppermute | solution.py:21
  48.7 47.2 %collective-permute-start.5 = (bf16[544,512]{1,0:T(8,128)(2,1)S(1)}, bf16[544,512]{1,0:T(8,128)(2,1)}, u32[]{:S(2)}, u32[]{:S(2)}) collective-permute-start(bf16[544,512]{1,0:T(8,128)(2,1)S(1)} %collective-permute-done.2.refs_7_), channel_id=1, source_target_pairs={{0,4},{4,0},{8,12},{12,8},{16,20},{20,16},{24,28},{28,24},{1,5},{5... | collective-permute-start | bytes 1671176 | tf_op jit(solution)/shard_map/ppermute | solution.py:21
  96.0 16.6 %collective-permute-start.8 = (bf16[512,512]{1,0:T(8,128)(2,1)}, bf16[512,512]{1,0:T(8,128)(2,1)}, u32[]{:S(2)}, u32[]{:S(2)}) collective-permute-start(bf16[512,512]{1,0:T(8,128)(2,1)} %get-tuple-element.31), channel_id=1, source_target_pairs={{0,8},{4,12},{8,0},{12,4},{16,24},{20,28},{24,16},{28,20},{1,9},{5... | collective-permute-start | bytes 1572872 | tf_op jit(solution)/shard_map/ppermute | solution.py:21
  107.2 31.7 %collective-permute-start.13 = (bf16[1,528,1024]{2,1,0:T(8,128)(2,1)}, bf16[1,528,1024]{2,1,0:T(8,128)(2,1)S(1)}, u32[]{:S(2)}, u32[]{:S(2)}) collective-permute-start(bf16[1,528,1024]{2,1,0:T(8,128)(2,1)} %bitcast.47), channel_id=1, source_target_pairs={{0,2},{1,3},{2,0},{3,1},{4,6},{5,7},{6,4},{7,5},{8,10},{9,11},{10,... | collective-permute-start | bytes 3244040 | tf_op jit(solution)/shard_map/ppermute | solution.py:21
  109.2 27.9 %collective-permute-start.15 = (bf16[512,512]{1,0:T(8,128)(2,1)}, bf16[512,512]{1,0:T(8,128)(2,1)}, u32[]{:S(2)}, u32[]{:S(2)}) collective-permute-start(bf16[512,512]{1,0:T(8,128)(2,1)} %get-tuple-element.32), channel_id=1, source_target_pairs={{0,16},{4,20},{8,24},{12,28},{16,0},{20,4},{24,8},{28,12},{1,17},{... | collective-permute-start | bytes 1572872 | tf_op jit(solution)/shard_map/ppermute | solution.py:21
  112.6 21.9 %collective-permute-start.11 = (bf16[512,512]{1,0:T(8,128)(2,1)S(1)}, bf16[512,512]{1,0:T(8,128)(2,1)}, u32[]{:S(2)}, u32[]{:S(2)}) collective-permute-start(bf16[512,512]{1,0:T(8,128)(2,1)S(1)} %copy-done.31), channel_id=1, source_target_pairs={{0,8},{4,12},{8,0},{12,4},{16,24},{20,28},{24,16},{28,20},{1,9},{5... | collective-permute-start | bytes 1572872 | tf_op jit(solution)/shard_map/ppermute | solution.py:21
  115.4 26.7 %collective-permute-start.14 = (bf16[512,512]{1,0:T(8,128)(2,1)}, bf16[512,512]{1,0:T(8,128)(2,1)S(1)}, u32[]{:S(2)}, u32[]{:S(2)}) collective-permute-start(bf16[512,512]{1,0:T(8,128)(2,1)} %collective-permute-done.10.refs_6_), channel_id=1, source_target_pairs={{0,4},{4,0},{8,12},{12,8},{16,20},{20,16},{24,28},{28,24},{1,5},{5... | collective-permute-start | bytes 1572872 | tf_op jit(solution)/shard_map/ppermute | solution.py:21
  117.1 24.9 %collective-permute-start.12 = (bf16[544,512]{1,0:T(8,128)(2,1)}, bf16[544,512]{1,0:T(8,128)(2,1)S(1)}, u32[]{:S(2)}, u32[]{:S(2)}) collective-permute-start(bf16[544,512]{1,0:T(8,128)(2,1)} %collective-permute-done.6.refs_9_), channel_id=1, source_target_pairs={{0,4},{4,0},{8,12},{12,8},{16,20},{20,16},{24,28},{28,24},{1,5},{5... | collective-permute-start | bytes 1671176 | tf_op jit(solution)/shard_map/ppermute | solution.py:21
  137.1 44.5 %collective-permute-start.24 = (bf16[512,512]{1,0:T(8,128)(2,1)}, bf16[512,512]{1,0:T(8,128)(2,1)}, u32[]{:S(2)}, u32[]{:S(2)}) collective-permute-start(bf16[512,512]{1,0:T(8,128)(2,1)} %collective-permute-done.11), channel_id=1, source_target_pairs={{0,16},{4,20},{8,24},{12,28},{16,0},{20,4},{24,8},{28,12},{1,17},{... | collective-permute-start | bytes 1572872 | tf_op jit(solution)/shard_map/ppermute | solution.py:21
  142.0 40.0 %collective-permute-start.19 = (bf16[512,512]{1,0:T(8,128)(2,1)}, bf16[512,512]{1,0:T(8,128)(2,1)}, u32[]{:S(2)}, u32[]{:S(2)}) collective-permute-start(bf16[512,512]{1,0:T(8,128)(2,1)} %collective-permute-done.8.refs_4_), channel_id=1, source_target_pairs={{0,4},{4,0},{8,12},{12,8},{16,20},{20,16},{24,28},{28,24},{1,5},{5... | collective-permute-start | bytes 1572872 | tf_op jit(solution)/shard_map/ppermute | solution.py:21
  143.8 40.5 %collective-permute-start.20 = (bf16[512,512]{1,0:T(8,128)(2,1)}, bf16[512,512]{1,0:T(8,128)(2,1)}, u32[]{:S(2)}, u32[]{:S(2)}) collective-permute-start(bf16[512,512]{1,0:T(8,128)(2,1)} %collective-permute-done.8.refs_4_), channel_id=1, source_target_pairs={{0,16},{4,20},{8,24},{12,28},{16,0},{20,4},{24,8},{28,12},{1,17},{... | collective-permute-start | bytes 1572872 | tf_op jit(solution)/shard_map/ppermute | solution.py:21
  145.0 37.1 %collective-permute-start.21 = (bf16[512,512]{1,0:T(8,128)(2,1)}, bf16[512,512]{1,0:T(8,128)(2,1)}, u32[]{:S(2)}, u32[]{:S(2)}) collective-permute-start(bf16[512,512]{1,0:T(8,128)(2,1)} %collective-permute-done.15), channel_id=1, source_target_pairs={{0,4},{4,0},{8,12},{12,8},{16,20},{20,16},{24,28},{28,24},{1,5},{5... | collective-permute-start | bytes 1572872 | tf_op jit(solution)/shard_map/ppermute | solution.py:21
  181.6 46.5 %collective-permute-start.25 = (bf16[512,512]{1,0:T(8,128)(2,1)}, bf16[512,512]{1,0:T(8,128)(2,1)S(1)}, u32[]{:S(2)}, u32[]{:S(2)}) collective-permute-start(bf16[512,512]{1,0:T(8,128)(2,1)} %collective-permute-done.24), channel_id=1, source_target_pairs={{0,4},{4,0},{8,12},{12,8},{16,20},{20,16},{24,28},{28,24},{1,5},{5... | collective-permute-start | bytes 1572872 | tf_op jit(solution)/shard_map/ppermute | solution.py:21
  184.3 24.3 %collective-permute-start.22 = (bf16[512,512]{1,0:T(8,128)(2,1)}, bf16[512,512]{1,0:T(8,128)(2,1)S(1)}, u32[]{:S(2)}, u32[]{:S(2)}) collective-permute-start(bf16[512,512]{1,0:T(8,128)(2,1)} %collective-permute-done.20.refs_8_), channel_id=1, source_target_pairs={{0,4},{4,0},{8,12},{12,8},{16,20},{20,16},{24,28},{28,24},{1,5},{5... | collective-permute-start | bytes 1572872 | tf_op jit(solution)/shard_map/ppermute | solution.py:21
  237.4 24.4 %collective-permute-start.32 = (bf16[1024,512]{0,1:T(8,128)(2,1)S(1)}, bf16[1024,512]{0,1:T(8,128)(2,1)S(1)}, u32[]{:S(2)}, u32[]{:S(2)}) collective-permute-start(bf16[1024,512]{0,1:T(8,128)(2,1)S(1)} %slice_add_fusion), channel_id=1, source_target_pairs={{0,2},{1,3},{2,0},{3,1},{4,6},{5,7},{6,4},{7,5},{8,10},{9,11},{10,... | collective-permute-start | bytes 3145736 | tf_op jit(solution)/shard_map/ppermute | solution.py:21
  240.2 25.8 %collective-permute-start.28 = (bf16[512,1024]{0,1:T(8,128)(2,1)S(1)}, bf16[512,1024]{0,1:T(8,128)(2,1)S(1)}, u32[]{:S(2)}, u32[]{:S(2)}) collective-permute-start(bf16[512,1024]{0,1:T(8,128)(2,1)S(1)} %fusion.2), channel_id=1, source_target_pairs={{0,8},{4,12},{8,0},{12,4},{16,24},{20,28},{24,16},{28,20},{1,9},{5... | collective-permute-start | bytes 3145736 | tf_op jit(solution)/shard_map/ppermute | solution.py:21
  (71 other events, 882.5 us)
Sparse Core Ops, SparseCore 0:
  25.8 103.8 all-gather.1

commit v8 on v7

--- a/solution.py
+++ b/solution.py
@@ -171,6 +171,35 @@
     g_ref[0] = (gated * gain_ref[...]).astype(BF16)
     total = jnp.sum(gated * gated, axis=1, keepdims=True)
     ss_ref[0] = jnp.broadcast_to(total, ss_ref.shape[1:])
+
+
+def finish_kernel(place_ref, scale_ref, *refs):
+    out_ref = refs[-1]
+    count = (len(refs) - 1) // 2
+    width = refs[0].shape[1]
+    for i in range(count):
+        value = (refs[i][...] + refs[count + i][...].astype(F32)) * scale_ref[:, :1]
+        start = pl.multiple_of(place_ref[i] * width, width)
+        out_ref[:, pl.ds(start, width)] = value.astype(BF16)
+
+
+def finish(places, scale, kept, received):
+    rows, width = received[0].shape
+    tile = min(rows, 256)
+
+    def part(value):
+        return pl.BlockSpec((tile, value.shape[1]), lambda i: (i, 0))
+
+    return pl.pallas_call(
+        finish_kernel,
+        grid=(rows // tile,),
+        in_specs=[pl.BlockSpec(memory_space=pltpu.SMEM)] + [part(v) for v in (scale, *kept, *received)],
+        out_specs=pl.BlockSpec((tile, width * len(kept)), lambda i: (i, 0)),
+        out_shape=jax.ShapeDtypeStruct((rows, width * len(kept)), BF16),
+        compiler_params=params(1),
+        cost_estimate=LIGHT,
+        name="finish",
+    )(places, scale, *kept, *received)
 
 
 def params(grid):
@@ -470,17 +499,18 @@
         bit = 2
         while len(parts) > 1:
             sent = jnp.concatenate(parts[1::2], axis=1) if len(parts) > 2 else parts[1]
-            got = swapped(sent.astype(BF16), "head", bit).astype(F32)
-            parts = columns_added(parts[::2], got)
+            got = swapped(sent.astype(BF16), "head", bit)
+            if len(parts) == 2:
+                return parts[0], got
+            parts = columns_added(parts[::2], got.astype(F32))
             bit *= 2
-        return parts[0]
 
     def columns_added(parts, got):
         width = parts[0].shape[1]
         return [part + got[:, i * width : (i + 1) * width] for i, part in enumerate(parts)]
 
     def swap_pair(value):
-        return swapped(value.astype(BF16), "seq", PAIR).astype(F32)
+        return swapped(value.astype(BF16), "seq", PAIR)
 
     squares = squares[0, :, 0] + swapped(squares[1, :, 0], "seq", PAIR)
     paired = squares
@@ -497,8 +527,8 @@
         got_far = send_far(weights)
         parts = columns_added([dot(flat, w) for w in weights[::2]], got_far)
         parts = [after(part, upper) if i else part for i, part in enumerate(parts)]
-        whole = fold_head(parts)
-        done[low] = whole[:rows] + swap_pair(whole[rows:])
+        whole, got = fold_head(parts)
+        done[low] = whole, swap_pair(whole[rows:] + got[rows:].astype(F32)), got
     flat = after(flat, paired)
     for low in range(1, per, 2):
         weights = by_destination(low)
@@ -506,10 +536,12 @@
         near = weights[::2]
         away = swap_pair(dot(gated[1], jnp.concatenate(near, axis=1)) + got_far[rows:])
         here = columns_added([dot(gated[0], w) for w in near], got_far[:rows])
-        done[low] = fold_head(columns_added(here, away))
-
-    result = by_xor([done[low] for low in range(per)], me % per)
-    return jnp.concatenate([(piece * scale).astype(BF16) for piece in result], axis=1)
+        done[low] = fold_head(columns_added(here, away.astype(F32)))
+
+    kept = [done[low][0][:rows] + done[low][2][:rows].astype(F32) if len(done[low]) == 3 else done[low][0] for low in range(per)]
+    places = jnp.stack([jnp.int32(low ^ (me % per)) for low in range(per)])
+    scale = jnp.broadcast_to(scale, (rows, 128))
+    return finish(places, scale, kept, [done[low][1] for low in range(per)])
 
 
 def solution(mesh):

time: 292 us -> 291 us (level)
  transfers between devices with their start and end apart: 36 -> 36, of which waited for: 16 -> 16; matrix products, arithmetic and copies ran while one was open for 24% -> 26% of each run, Pallas kernels for 12% -> 12%
where the time goes in v8:
time: 291 us; the launch traced here: 289 us
  waiting for transfers between devices  113 us (39%)
  local copies, waits for them, and re-layouts  47.7 us (16%)
  starting transfers between devices  37.9 us (13%)
  Pallas kernels  37.6 us (13%)
  other arithmetic  26.7 us (9%)
  between operations  14.5 us (5%)
  matrix products  11.9 us (4%)
    ppermute x34, waiting for transfers between devices, swapped(): return lax.ppermute(value, axis, [(i, i ^ bit) for i in range(size)])  113 us
    ppermute x34, starting transfers between devices, swapped(): return lax.ppermute(value, axis, [(i, i ^ bit) for i in range(size)])  34.2 us
    pallas_call x3, Pallas kernels, project(): pl.pallas_call(functools.partial(project_kernel, depth, halo is not None,...  23.9 us
    unnamed x125, local copies, waits for them, and re-layouts  13.4 us
    dot_general x7, matrix products, dot(): return jnp.dot(a, b, preferred_element_type=F32)  11.9 us
    dynamic_slice x10, local copies, waits for them, and re-layouts, cut(): return lax.dynamic_slice_in_dim(value, index * size, size, axis)  9.33 us
  transfers between devices with their start and end apart: 36, of which 16 were waited for; matrix products, arithmetic and copies ran while one was open for 26% of the time, Pallas kernels for 12%

profile of v8, /device:TPU:0, one launch (start us, length us, event | category | flops | bytes accessed | tf_op | source)
XLA Modules:
  0.0 289.0 jit_solution(14377358523128405955)
XLA Ops:
  12.2 2.9 %collective-permute-start.1 = (bf16[544,512]{1,0:T(8,128)(2,1)S(1)}, bf16[544,512]{1,0:T(8,128)(2,1)S(1)}, u32[]{:S(2)}, u32[]{:S(2)}) collective-permute-start(bf16[544,512]{1,0:T(8,128)(2,1)S(1)} %get-tuple-element.98.refs_3_), channel_id=1, source_target_pairs={{0,4},{4,0},{8,12},{12,8},{16,20},{20,16},{24,28},{28,24},{1,5},{5... | collective-permute-start | bytes 1671176 | tf_op jit(solution)/shard_map/ppermute | solution.py:21
  15.1 2.6 collective-permute-start.2
  40.9 4.4 %collective-permute-done.refs_5_ = bf16[544,512]{1,0:T(8,128)(2,1)} collective-permute-done((bf16[544,512]{1,0:T(8,128)(2,1)}, bf16[544,512]{1,0:T(8,128)(2,1)}, u32[]{:S(2)}, u32[]{:S(2)}) %collective-permute-start) | collective-permute-done | bytes 557088 | tf_op jit(solution)/shard_map/ppermute | solution.py:21
  46.3 2.4 collective-permute-start.10
  52.5 38.2 %collective-permute-done.7 = bf16[528,1024]{1,0:T(8,128)(2,1)} collective-permute-done((bf16[528,1024]{1,0:T(8,128)(2,1)}, bf16[528,1024]{1,0:T(8,128)(2,1)}, u32[]{:S(2)}, u32[]{:S(2)}) %collective-permute-start.7) | collective-permute-done | bytes 1081376 | tf_op jit(solution)/shard_map/ppermute | solution.py:21
  99.3 3.0 %copy.32.dec_ref = f32[2,512,512]{2,1,0:T(8,128)} copy(f32[2,512,512]{1,2,0:T(8,128)} %bitcast.238) | data formatting | bytes 4194304 | tf_op jit(solution)/shard_map/reshape | solution.py:412
  104.0 3.2 %copy.43.e_ref = f32[2,512,512]{2,1,0:T(8,128)} copy(f32[2,512,512]{1,2,0:T(8,128)} %bitcast.239) | data formatting | bytes 4194304 | tf_op jit(solution)/shard_map/reshape | solution.py:415
  120.2 14.3 %collective-permute-done.11 = bf16[512,512]{1,0:T(8,128)(2,1)} collective-permute-done((bf16[512,512]{1,0:T(8,128)(2,1)S(1)}, bf16[512,512]{1,0:T(8,128)(2,1)}, u32[]{:S(2)}, u32[]{:S(2)}) %collective-permute-start.11) | collective-permute-done | bytes 524320 | tf_op jit(solution)/shard_map/ppermute | solution.py:21
  134.5 2.6 collective-permute-done.15
  138.8 3.2 %pad_maximum_fusion.1 = bf16[2,528,1024]{2,1,0:T(8,128)(2,1)} fusion(bf16[1,528,1024]{2,1,0:T(8,128)(2,1)S(1)} %collective-permute-done.13, bf16[1,528,1024]{2,1,0:T(8,128)(2,1)} %bitcast.49), kind=kLoop, calls=%fused_computation.2 | loop fusion | flops 1081344 | bytes 4325376 | tf_op jit(solution)/shard_map/concatenate | solution.py:82
  147.4 2.6 collective-permute-done.16
  150.0 3.8 %pad_maximum_fusion.refs_2_.refs_1_ = bf16[4,528,1024]{2,1,0:T(8,128)(2,1)} fusion(bf16[2,528,1024]{2,1,0:T(8,128)(2,1)} %collective-permute-done.16, bf16[1,528,1024]{2,1,0:T(8,128)(2,1)} %copy-done.26, bf16[1,528,1024]{2,1,0:T(8,128)(2,1)} %bitcast.49), kind=kLoop, calls=%fused_computation | loop fusion | flops 4325376 | bytes 8650752 | tf_op jit(solution)/shard_map/concatenate | solution.py:382
  154.8 9.3 %project.3.x_ref = bf16[2,528,512]{2,1,0:T(8,128)(2,1)S(1)} custom-call(s32[3,8]{1,0:T(4,128)S(1)} %copy-done.18, bf16[32,4096]{1,0:T(8,128)(2,1)S(1)} %fusion.41.refs_0_, bf16[512,4096]{1,0:T(8,128)(2,1)} %refs_0_.1, bf16[4,528,1024]{2,1,0:T(8,128)(2,1)} %pad_maximum_fusion.refs_2_.refs_1_, bf16[544,512]{1,0:T(8,128)(2,1)S(1)} %get-tuple-element.98.refs_3_, ...), custom_call_target="tpu_custom_call" | custom-call | flops 1 | bytes 1 | tf_op jit(solution)/shard_map/project/pallas_call | solution.py:259
  165.7 6.2 %project.4.bc_ref = bf16[2,528,256]{2,1,0:T(8,128)(2,1)S(1)} custom-call(s32[3,8]{1,0:T(4,128)S(1)} %copy-done.18, bf16[32,4096]{1,0:T(8,128)(2,1)S(1)} %fusion.41.refs_0_, bf16[512,4096]{1,0:T(8,128)(2,1)} %refs_0_.1, bf16[4,528,1024]{2,1,0:T(8,128)(2,1)} %pad_maximum_fusion.refs_2_.refs_1_, bf16[4096,256]{1,0:T(8,128)(2,1)S(1)} %copy-done.5), custom_call_target="tpu_custom_call" | custom-call | flops 1 | bytes 1 | tf_op jit(solution)/shard_map/project/pallas_call | solution.py:259
  172.0 4.8 %front.1 = (bf16[2,512,512]{2,1,0:T(8,128)(2,1)S(1)}, bf16[2,512,256]{2,1,0:T(8,128)(2,1)S(1)}, f32[2,2,128,512]{3,2,1,0:T(8,128)S(1)}) custom-call(s32[2]{0:T(128)S(1)} %copy-done.22, bf16[2,528,512]{2,1,0:T(8,128)(2,1)S(1)} %project.3.x_ref, bf16[2,528,256]{2,1,0:T(8,128)(2,1)S(1)} %project.4.bc_ref, bf16[16,512]{1,0:T(8,128)(2,1)S(1)} %pad.27.tx_ref, ...), custom_call_target="tpu_custom_call" | custom-call | flops 1 | bytes 1 | tf_op jit(solution)/shard_map/front/pallas_call | solution.py:216
  187.2 3.7 %collective-permute-start.18 = (bf16[128,512]{1,0:T(8,128)(2,1)S(1)}, bf16[128,512]{1,0:T(8,128)(2,1)S(1)}, u32[]{:S(2)}, u32[]{:S(2)}) collective-permute-start(bf16[128,512]{1,0:T(8,128)(2,1)S(1)} %add_convert_fusion), channel_id=1, source_target_pairs={{0,16},{4,20},{8,24},{12,28},{1,17},{5,21},{9,25},{13,29},{2,18},{... | collective-permute-start | bytes 393224 | tf_op jit(solution)/shard_map/ppermute | solution.py:26
  192.3 3.1 %intra.1.y_ref = f32[2,512,512]{2,1,0:T(8,128)S(1)} custom-call(bf16[2,512,512]{2,1,0:T(8,128)(2,1)S(1)} %get-tuple-element.40.x_ref, bf16[2,512,256]{2,1,0:T(8,128)(2,1)S(1)} %copy-done.7, f32[2,512,8]{2,1,0:T(8,128)S(1)} %copy-done.8, f32[2,2,8,256]{3,2,1,0:T(8,128)S(1)} %copy-done.15), custom_call_target="tpu_custom_call" | custom-call | flops 1 | bytes 1 | tf_op jit(solution)/shard_map/intra/pallas_call | solution.py:279
  195.6 13.0 %collective-permute-done.22.refs_9_ = bf16[512,512]{1,0:T(8,128)(2,1)S(1)} collective-permute-done((bf16[512,512]{1,0:T(8,128)(2,1)}, bf16[512,512]{1,0:T(8,128)(2,1)S(1)}, u32[]{:S(2)}, u32[]{:S(2)}) %collective-permute-start.22) | collective-permute-done | bytes 524320 | tf_op jit(solution)/shard_map/ppermute | solution.py:21
  211.8 8.5 %project.5.z_ref = bf16[2,512,512]{2,1,0:T(8,128)(2,1)S(1)} custom-call(s32[3,8]{1,0:T(4,128)S(1)} %copy-done.18, bf16[512,4096]{1,0:T(8,128)(2,1)} %refs_0_.1, bf16[4,528,1024]{2,1,0:T(8,128)(2,1)} %pad_maximum_fusion.refs_2_.refs_1_, bf16[512,512]{1,0:T(8,128)(2,1)S(1)} %copy-done.4, bf16[512,512]{1,0:T(8,128)(2,1)S(1)} %copy-done.12, ...), custom_call_target="tpu_custom_call" | custom-call | flops 1 | bytes 1 | tf_op jit(solution)/shard_map/project/pallas_call | solution.py:259
  222.0 4.0 %gate.1 = (bf16[2,512,512]{2,1,0:T(8,128)(2,1)S(1)}, f32[2,512,128]{2,1,0:T(8,128)S(1)}) custom-call(f32[2,512,512]{2,1,0:T(8,128)} %copy-done.2, bf16[2,512,512]{2,1,0:T(8,128)(2,1)S(1)} %get-tuple-element.40.x_ref, bf16[2,512,256]{2,1,0:T(8,128)(2,1)S(1)} %copy-done.7, f32[2,2,128,512]{3,2,1,0:T(8,128)S(1)} %pad_maximum_fusion.2.st_ref, ...), custom_call_target="tpu_custom_call" | custom-call | flops 1 | bytes 1 | tf_op jit(solution)/shard_map/gate/pallas_call | solution.py:298
  235.4 3.7 %slice_add_fusion.1 = bf16[1024,512]{1,0:T(8,128)(2,1)} fusion(f32[1024,1024]{1,0:T(8,128)S(1)} %convert_element_type.94, bf16[1024,512]{1,0:T(8,128)(2,1)S(1)} %bitcast.234, pred[]{:T(512)S(6)} %ne.116, bf16[512,512]{1,0:T(8,128)(2,1)} %collective-permute-done.27, bf16[512,512]{1,0:T(8,128)(2,1)} %collective-permute-done.15, pred[]{:T(512)S(6)} %ne.117, ...), kind=kOutput, calls=%fused_computation.6 | convolution fusion | flops 538705920 | bytes 6291458 | tf_op jit(solution)/shard_map/dot_general | solution.py:106
  244.9 2.7 slice_add_fusion.2
  247.6 16.2 %collective-permute-done.29 = bf16[1024,512]{1,0:T(8,128)(2,1)} collective-permute-done((bf16[1024,512]{1,0:T(8,128)(2,1)}, bf16[1024,512]{1,0:T(8,128)(2,1)}, u32[]{:S(2)}, u32[]{:S(2)}) %collective-permute-start.29) | collective-permute-done | bytes 1048608 | tf_op jit(solution)/shard_map/ppermute | solution.py:21
  270.0 8.9 %collective-permute-done.33.refs_2_ = bf16[512,512]{1,0:T(8,128)(2,1)S(1)} collective-permute-done((bf16[512,512]{1,0:T(8,128)(2,1)S(1)}, bf16[512,512]{1,0:T(8,128)(2,1)S(1)}, u32[]{:S(2)}, u32[]{:S(2)}) %collective-permute-start.33) | collective-permute-done | bytes 524320 | tf_op jit(solution)/shard_map/ppermute | solution.py:21
  (337 shorter events, 107.2 us)
Async XLA Ops:
  6.5 157.6 %all-gather.2.cloned.1.call-start = ((), (), s32[]{:S(2)}) async-start(), calls=%async_computation | async-start | bytes 2162688 | tf_op jit(solution)/shard_map/all_gather | solution.py:399
  12.2 33.2 %collective-permute-start.1 = (bf16[544,512]{1,0:T(8,128)(2,1)S(1)}, bf16[544,512]{1,0:T(8,128)(2,1)S(1)}, u32[]{:S(2)}, u32[]{:S(2)}) collective-permute-start(bf16[544,512]{1,0:T(8,128)(2,1)S(1)} %get-tuple-element.98.refs_3_), channel_id=1, source_target_pairs={{0,4},{4,0},{8,12},{12,8},{16,20},{20,16},{24,28},{28,24},{1,5},{5... | collective-permute-start | bytes 1671176 | tf_op jit(solution)/shard_map/ppermute | solution.py:21
  15.1 30.2 %collective-permute-start.2 = (bf16[544,512]{1,0:T(8,128)(2,1)S(1)}, bf16[544,512]{1,0:T(8,128)(2,1)S(1)}, u32[]{:S(2)}, u32[]{:S(2)}) collective-permute-start(bf16[544,512]{1,0:T(8,128)(2,1)S(1)} %get-tuple-element.98.refs_3_), channel_id=1, source_target_pairs={{0,16},{4,20},{8,24},{12,28},{16,0},{20,4},{24,8},{28,12},{1,17},{... | collective-permute-start | bytes 1671176 | tf_op jit(solution)/shard_map/ppermute | solution.py:21
  17.7 27.6 %collective-permute-start = (bf16[544,512]{1,0:T(8,128)(2,1)}, bf16[544,512]{1,0:T(8,128)(2,1)}, u32[]{:S(2)}, u32[]{:S(2)}) collective-permute-start(bf16[544,512]{1,0:T(8,128)(2,1)} %get-tuple-element.99), channel_id=1, source_target_pairs={{0,8},{4,12},{8,0},{12,4},{16,24},{20,28},{24,16},{28,20},{1,9},{5... | collective-permute-start | bytes 1671176 | tf_op jit(solution)/shard_map/ppermute | solution.py:21
  20.2 20.7 %collective-permute-start.3 = (bf16[512,512]{1,0:T(8,128)(2,1)S(1)}, bf16[512,512]{1,0:T(8,128)(2,1)S(1)}, u32[]{:S(2)}, u32[]{:S(2)}) collective-permute-start(bf16[512,512]{1,0:T(8,128)(2,1)S(1)} %get-tuple-element.33.refs_2_), channel_id=1, source_target_pairs={{0,4},{4,0},{8,12},{12,8},{16,20},{20,16},{24,28},{28,24},{1,5},{5... | collective-permute-start | bytes 1572872 | tf_op jit(solution)/shard_map/ppermute | solution.py:21
  23.8 66.9 %collective-permute-start.7 = (bf16[528,1024]{1,0:T(8,128)(2,1)}, bf16[528,1024]{1,0:T(8,128)(2,1)}, u32[]{:S(2)}, u32[]{:S(2)}) collective-permute-start(bf16[528,1024]{1,0:T(8,128)(2,1)} %fusion.5), channel_id=1, source_target_pairs={{0,8},{4,12},{8,0},{12,4},{16,24},{20,28},{24,16},{28,20},{1,9},{5... | collective-permute-start | bytes 3244040 | tf_op jit(solution)/shard_map/ppermute | solution.py:21
  45.3 50.6 %collective-permute-start.4 = (bf16[544,512]{1,0:T(8,128)(2,1)}, bf16[544,512]{1,0:T(8,128)(2,1)}, u32[]{:S(2)}, u32[]{:S(2)}) collective-permute-start(bf16[544,512]{1,0:T(8,128)(2,1)} %collective-permute-done.refs_5_), channel_id=1, source_target_pairs={{0,4},{4,0},{8,12},{12,8},{16,20},{20,16},{24,28},{28,24},{1,5},{5... | collective-permute-start | bytes 1671176 | tf_op jit(solution)/shard_map/ppermute | solution.py:21
  45.8 50.1 %collective-permute-start.6 = (bf16[544,512]{1,0:T(8,128)(2,1)}, bf16[544,512]{1,0:T(8,128)(2,1)}, u32[]{:S(2)}, u32[]{:S(2)}) collective-permute-start(bf16[544,512]{1,0:T(8,128)(2,1)} %collective-permute-done.refs_5_), channel_id=1, source_target_pairs={{0,16},{4,20},{8,24},{12,28},{16,0},{20,4},{24,8},{28,12},{1,17},{... | collective-permute-start | bytes 1671176 | tf_op jit(solution)/shard_map/ppermute | solution.py:21
  46.3 65.2 %collective-permute-start.10 = (bf16[512,512]{1,0:T(8,128)(2,1)S(1)}, bf16[512,512]{1,0:T(8,128)(2,1)}, u32[]{:S(2)}, u32[]{:S(2)}) collective-permute-start(bf16[512,512]{1,0:T(8,128)(2,1)S(1)} %get-tuple-element.33.refs_2_), channel_id=1, source_target_pairs={{0,16},{4,20},{8,24},{12,28},{16,0},{20,4},{24,8},{28,12},{1,17},{... | collective-permute-start | bytes 1572872 | tf_op jit(solution)/shard_map/ppermute | solution.py:21
  48.7 47.2 %collective-permute-start.5 = (bf16[544,512]{1,0:T(8,128)(2,1)S(1)}, bf16[544,512]{1,0:T(8,128)(2,1)}, u32[]{:S(2)}, u32[]{:S(2)}) collective-permute-start(bf16[544,512]{1,0:T(8,128)(2,1)S(1)} %collective-permute-done.2.refs_7_), channel_id=1, source_target_pairs={{0,4},{4,0},{8,12},{12,8},{16,20},{20,16},{24,28},{28,24},{1,5},{5... | collective-permute-start | bytes 1671176 | tf_op jit(solution)/shard_map/ppermute | solution.py:21
  107.2 31.7 %collective-permute-start.13 = (bf16[1,528,1024]{2,1,0:T(8,128)(2,1)}, bf16[1,528,1024]{2,1,0:T(8,128)(2,1)S(1)}, u32[]{:S(2)}, u32[]{:S(2)}) collective-permute-start(bf16[1,528,1024]{2,1,0:T(8,128)(2,1)} %bitcast.49), channel_id=1, source_target_pairs={{0,2},{1,3},{2,0},{3,1},{4,6},{5,7},{6,4},{7,5},{8,10},{9,11},{10,... | collective-permute-start | bytes 3244040 | tf_op jit(solution)/shard_map/ppermute | solution.py:21
  109.2 27.9 %collective-permute-start.15 = (bf16[512,512]{1,0:T(8,128)(2,1)}, bf16[512,512]{1,0:T(8,128)(2,1)}, u32[]{:S(2)}, u32[]{:S(2)}) collective-permute-start(bf16[512,512]{1,0:T(8,128)(2,1)} %get-tuple-element.32), channel_id=1, source_target_pairs={{0,16},{4,20},{8,24},{12,28},{16,0},{20,4},{24,8},{28,12},{1,17},{... | collective-permute-start | bytes 1572872 | tf_op jit(solution)/shard_map/ppermute | solution.py:21
  112.6 21.9 %collective-permute-start.11 = (bf16[512,512]{1,0:T(8,128)(2,1)S(1)}, bf16[512,512]{1,0:T(8,128)(2,1)}, u32[]{:S(2)}, u32[]{:S(2)}) collective-permute-start(bf16[512,512]{1,0:T(8,128)(2,1)S(1)} %copy-done.31), channel_id=1, source_target_pairs={{0,8},{4,12},{8,0},{12,4},{16,24},{20,28},{24,16},{28,20},{1,9},{5... | collective-permute-start | bytes 1572872 | tf_op jit(solution)/shard_map/ppermute | solution.py:21
  115.4 26.7 %collective-permute-start.14 = (bf16[512,512]{1,0:T(8,128)(2,1)}, bf16[512,512]{1,0:T(8,128)(2,1)S(1)}, u32[]{:S(2)}, u32[]{:S(2)}) collective-permute-start(bf16[512,512]{1,0:T(8,128)(2,1)} %collective-permute-done.10.refs_6_), channel_id=1, source_target_pairs={{0,4},{4,0},{8,12},{12,8},{16,20},{20,16},{24,28},{28,24},{1,5},{5... | collective-permute-start | bytes 1572872 | tf_op jit(solution)/shard_map/ppermute | solution.py:21
  117.1 24.9 %collective-permute-start.12 = (bf16[544,512]{1,0:T(8,128)(2,1)}, bf16[544,512]{1,0:T(8,128)(2,1)S(1)}, u32[]{:S(2)}, u32[]{:S(2)}) collective-permute-start(bf16[544,512]{1,0:T(8,128)(2,1)} %collective-permute-done.6.refs_9_), channel_id=1, source_target_pairs={{0,4},{4,0},{8,12},{12,8},{16,20},{20,16},{24,28},{28,24},{1,5},{5... | collective-permute-start | bytes 1671176 | tf_op jit(solution)/shard_map/ppermute | solution.py:21
  137.1 44.5 %collective-permute-start.27 = (bf16[512,512]{1,0:T(8,128)(2,1)}, bf16[512,512]{1,0:T(8,128)(2,1)}, u32[]{:S(2)}, u32[]{:S(2)}) collective-permute-start(bf16[512,512]{1,0:T(8,128)(2,1)} %collective-permute-done.11), channel_id=1, source_target_pairs={{0,16},{4,20},{8,24},{12,28},{16,0},{20,4},{24,8},{28,12},{1,17},{... | collective-permute-start | bytes 1572872 | tf_op jit(solution)/shard_map/ppermute | solution.py:21
  142.0 40.0 %collective-permute-start.19 = (bf16[512,512]{1,0:T(8,128)(2,1)}, bf16[512,512]{1,0:T(8,128)(2,1)}, u32[]{:S(2)}, u32[]{:S(2)}) collective-permute-start(bf16[512,512]{1,0:T(8,128)(2,1)} %collective-permute-done.8.refs_4_), channel_id=1, source_target_pairs={{0,4},{4,0},{8,12},{12,8},{16,20},{20,16},{24,28},{28,24},{1,5},{5... | collective-permute-start | bytes 1572872 | tf_op jit(solution)/shard_map/ppermute | solution.py:21
  143.8 40.5 %collective-permute-start.20 = (bf16[512,512]{1,0:T(8,128)(2,1)}, bf16[512,512]{1,0:T(8,128)(2,1)}, u32[]{:S(2)}, u32[]{:S(2)}) collective-permute-start(bf16[512,512]{1,0:T(8,128)(2,1)} %collective-permute-done.8.refs_4_), channel_id=1, source_target_pairs={{0,16},{4,20},{8,24},{12,28},{16,0},{20,4},{24,8},{28,12},{1,17},{... | collective-permute-start | bytes 1572872 | tf_op jit(solution)/shard_map/ppermute | solution.py:21
  145.0 37.1 %collective-permute-start.21 = (bf16[512,512]{1,0:T(8,128)(2,1)}, bf16[512,512]{1,0:T(8,128)(2,1)}, u32[]{:S(2)}, u32[]{:S(2)}) collective-permute-start(bf16[512,512]{1,0:T(8,128)(2,1)} %collective-permute-done.15), channel_id=1, source_target_pairs={{0,4},{4,0},{8,12},{12,8},{16,20},{20,16},{24,28},{28,24},{1,5},{5... | collective-permute-start | bytes 1572872 | tf_op jit(solution)/shard_map/ppermute | solution.py:21
  181.6 46.5 %collective-permute-start.30 = (bf16[512,512]{1,0:T(8,128)(2,1)}, bf16[512,512]{1,0:T(8,128)(2,1)S(1)}, u32[]{:S(2)}, u32[]{:S(2)}) collective-permute-start(bf16[512,512]{1,0:T(8,128)(2,1)} %collective-permute-done.27), channel_id=1, source_target_pairs={{0,4},{4,0},{8,12},{12,8},{16,20},{20,16},{24,28},{28,24},{1,5},{5... | collective-permute-start | bytes 1572872 | tf_op jit(solution)/shard_map/ppermute | solution.py:21
  184.3 24.3 %collective-permute-start.22 = (bf16[512,512]{1,0:T(8,128)(2,1)}, bf16[512,512]{1,0:T(8,128)(2,1)S(1)}, u32[]{:S(2)}, u32[]{:S(2)}) collective-permute-start(bf16[512,512]{1,0:T(8,128)(2,1)} %collective-permute-done.20.refs_8_), channel_id=1, source_target_pairs={{0,4},{4,0},{8,12},{12,8},{16,20},{20,16},{24,28},{28,24},{1,5},{5... | collective-permute-start | bytes 1572872 | tf_op jit(solution)/shard_map/ppermute | solution.py:21
  239.1 24.7 %collective-permute-start.29 = (bf16[1024,512]{1,0:T(8,128)(2,1)}, bf16[1024,512]{1,0:T(8,128)(2,1)}, u32[]{:S(2)}, u32[]{:S(2)}) collective-permute-start(bf16[1024,512]{1,0:T(8,128)(2,1)} %slice_add_fusion.1), channel_id=1, source_target_pairs={{0,2},{1,3},{2,0},{3,1},{4,6},{5,7},{6,4},{7,5},{8,10},{9,11},{10,... | collective-permute-start | bytes 3145736 | tf_op jit(solution)/shard_map/ppermute | solution.py:21
  243.4 25.4 %collective-permute-start.32 = (bf16[512,1024]{1,0:T(8,128)(2,1)}, bf16[512,1024]{1,0:T(8,128)(2,1)S(1)}, u32[]{:S(2)}, u32[]{:S(2)}) collective-permute-start(bf16[512,1024]{1,0:T(8,128)(2,1)} %fusion.1), channel_id=1, source_target_pairs={{0,8},{4,12},{8,0},{12,4},{16,24},{20,28},{24,16},{28,20},{1,9},{5... | collective-permute-start | bytes 3145736 | tf_op jit(solution)/shard_map/ppermute | solution.py:21
  244.9 24.6 %collective-permute-start.26 = (f32[512]{0:T(512)S(1)}, f32[512]{0:T(512)S(1)}, u32[]{:S(2)}, u32[]{:S(2)}) collective-permute-start(f32[512]{0:T(512)S(1)} %add.331), channel_id=1, source_target_pairs={{0,1},{1,0},{2,3},{3,2},{4,5},{5,4},{6,7},{7,6},{8,9},{9,8},{10,11... | collective-permute-start | bytes 6152 | tf_op jit(solution)/shard_map/ppermute | solution.py:21
  (71 other events, 874.0 us)
Sparse Core Ops, SparseCore 0:
  25.8 103.8 all-gather.1
